TPU v7x, 32 devices: a whole 2x2x4 slice. The times are simulated.
32 devices in a mesh: groups: 2 (over y), tensor: 8 (over z, x), section: 2 (over core).
Axes of the slice: x: 2, y: 2, z: 4, core: 2. Of those that a mesh axis runs over, the one named last changes fastest.
Arguments:
- hidden_in: bfloat16 [256, 8192], P('groups', 'tensor'), parts along dimension 0, may hold values from -6 to 6
- cotangent: bfloat16 [256, 8192], P('groups', 'tensor'), parts along dimension 0, may hold values from -0.119628906 to 0.119628906
- norm_gain: float32 [2, 8192], P('section', 'tensor'), may hold values from 0.5 to 1.5
- value_weight: bfloat16 [2, 8192, 1024], P('section', 'tensor'), may hold values from -0.0625 to 0.0625
- output_weight: bfloat16 [2, 8192, 8192], P('section', 'tensor'), may hold values from -0.0625 to 0.0625
- rotation: float32 [2, 128, 128], P('section'), may hold values from -0.5 to 1
- attention: bfloat16 [2, 4, 64, 4096], P('section', 'groups'), parts along dimension 1, may hold values from 0 to 1, as said below
Outputs:
- rotation_grad: float32 [2, 256, 128], P('section', 'groups'), parts along dimension 1
- rotation_new: float32 [2, 256, 128], P('section', 'groups'), parts along dimension 1
There are 2 independent parts, one for each index of `groups`. A program takes and returns all parts, laid end to end along the dimension named above; an argument that names none is the same for every part. Nothing has to cross between parts.
Inputs may be any that keep to these rules, and one draw needn't show every extreme that they name: `attention`: each aligned block of 64 entries is one query's row over keys and is causal: nonnegative at and below the diagonal, zero above it, and sums to one.
All inputs are finite; a program needn't handle non-finite values.
Results may differ from a plain program's by a relative error of at most 0.013.
Values may be sent and summed in bfloat16 or wider, within the bound.
No kernel may reach another device: no remote copies, remote signals or barrier semaphores. Data moves between devices by JAX's collectives and lax.ppermute only.
A program may use at most 320 MiB of HBM per device.

v0:
```python
import jax
import jax.numpy as jnp
from jax import lax
from jax.sharding import PartitionSpec as P

SEQ = 64


quant_levels = 7.0
full_turn = 6.283185307179586
norm_eps = 1e-05
scale_eps = 1e-06
step_size = 0.1
precise = lax.Precision.HIGHEST


def from_behind(shard, axis, by):
    length = lax.axis_size(axis)
    pairs = [(i, i + by) for i in range(length) if 0 <= i + by < length]
    return lax.ppermute(shard, axis, pairs)


def soft_quant(rotated):
    col_scale = (jnp.max(jnp.abs(rotated), axis=0) + scale_eps) / quant_levels
    ratio_vals = rotated / col_scale
    return (col_scale * (ratio_vals - jnp.sin(full_turn * ratio_vals) / full_turn), ratio_vals)


def cayley(rot_grad, rotation_mat):
    skew_part = jnp.dot(rot_grad, rotation_mat.T, precision=precise) - jnp.dot(
        rotation_mat, rot_grad.T, precision=precise
    )
    update = rotation_mat - step_size * jnp.dot(skew_part, rotation_mat, precision=precise)
    for sweep_idx in range(2):
        update = rotation_mat - 0.5 * step_size * jnp.dot(
            skew_part, rotation_mat + update, precision=precise
        )
    return update


def mix_heads(attn_probs, values, kv_count):
    block_count = attn_probs.shape[0]
    head_count = attn_probs.shape[1]
    seq_len = attn_probs.shape[2]
    head_dim = values.shape[1] // kv_count
    grouped = attn_probs.astype(jnp.float32).reshape(
        block_count, kv_count, head_count // kv_count, seq_len, seq_len
    )
    value_blocks = values.astype(jnp.float32).reshape(block_count, seq_len, kv_count, head_dim)
    mixed_heads = jnp.einsum("bgkqs,bsgd->bqgkd", grouped, value_blocks)
    return mixed_heads.reshape(block_count * seq_len, head_count * head_dim).astype(jnp.bfloat16)


def on_device(hidden_in, cotangent, norm_gain, value_weight, output_weight, rotation, attention):
    section_idx = lax.axis_index("section")
    section_count = lax.axis_size("section")
    tensor_idx = lax.axis_index("tensor")
    tensor_count = lax.axis_size("tensor")
    rotation_mat = rotation[0]
    gain_row = norm_gain[0]
    seq_len = SEQ
    block_count = attention.shape[1]
    head_count = attention.shape[2]
    attn_probs = attention[0].reshape(block_count, head_count, seq_len, seq_len)
    head_dim = rotation_mat.shape[0]
    local_width = hidden_in.shape[1]
    model_width = local_width * tensor_count
    value_wide = value_weight[0].astype(jnp.float32)
    kv_width = value_wide.shape[1]
    kv_count = kv_width // head_dim
    per_group = head_count // kv_count
    value_heads = value_wide.reshape(local_width, kv_count, head_dim)
    value_rot = jnp.einsum("dgk,kj->dgj", value_heads, rotation_mat, precision=precise).reshape(
        local_width, kv_width
    )
    value_peak = lax.pmax(jnp.max(jnp.abs(value_rot), axis=0), "tensor")
    value_scale = (value_peak + scale_eps) / quant_levels
    value_ratio = value_rot / value_scale
    value_eff = (value_scale * (value_ratio - jnp.sin(full_turn * value_ratio) / full_turn)).astype(
        jnp.bfloat16
    )
    out_wide = output_weight[0].astype(jnp.float32)
    mixed_width = out_wide.shape[1]
    out_heads = out_wide.reshape(local_width, head_count, head_dim)
    out_rot = jnp.einsum("chk,kj->hjc", out_heads, rotation_mat, precision=precise).reshape(
        mixed_width, local_width
    )
    out_q, out_ratio = soft_quant(out_rot)
    out_eff = out_q.astype(jnp.bfloat16)
    col_count = mixed_width // tensor_count
    first_col = tensor_idx * col_count
    local_heads = max(col_count // head_dim, 1)
    head_part = min(col_count, head_dim)
    head_ids = first_col // head_dim + jnp.arange(local_heads, dtype=jnp.int32)
    probs_local = jnp.take(attn_probs, head_ids, axis=1)
    out_rows = lax.all_to_all(out_eff, "tensor", split_axis=0, concat_axis=1, tiled=True)

    def forward(rows_in, probs_block):
        widened = rows_in.astype(jnp.float32)
        squares = lax.psum(jnp.sum(widened * widened, axis=1), "tensor")
        inverse_rms = lax.rsqrt(squares / model_width + norm_eps)[:, None]
        normed = (widened * inverse_rms * gain_row).astype(jnp.bfloat16)
        partial_values = jnp.dot(normed, value_eff, preferred_element_type=jnp.float32)
        values = lax.psum(partial_values, "tensor").astype(jnp.bfloat16)
        mixed_heads = mix_heads(probs_block, values, kv_count)
        produced = (
            widened + jnp.dot(mixed_heads, out_eff, preferred_element_type=jnp.float32)
        ).astype(jnp.bfloat16)
        return (produced, (widened, inverse_rms, normed, mixed_heads))

    def add_rows(shard_rows):
        return jnp.dot(shard_rows, out_rows.T, preferred_element_type=jnp.float32)

    def backward(incoming, saved, probs_block):
        widened, inverse_rms, normed, mixed_heads = saved
        rows_n = incoming.shape[0]
        blocks_here = rows_n // seq_len
        out_grad = jnp.dot(mixed_heads.T, incoming, preferred_element_type=jnp.float32)
        mix_grad = add_rows(lax.all_gather(incoming, "tensor", axis=1, tiled=True)).astype(
            jnp.bfloat16
        )
        grad_blocks = mix_grad.astype(jnp.float32).reshape(
            blocks_here, seq_len, local_heads, head_part
        )
        head_term = jnp.einsum("bhqs,bqhd->bshd", probs_block.astype(jnp.float32), grad_blocks)
        head_term = head_term.reshape(rows_n, col_count).astype(jnp.bfloat16)
        columns = first_col + jnp.arange(col_count, dtype=jnp.int32)
        target = columns // (per_group * head_dim) * head_dim + columns % head_dim
        placing = (target[:, None] == jnp.arange(kv_width, dtype=jnp.int32)[None, :]).astype(
            jnp.bfloat16
        )
        placed = jnp.dot(head_term, placing, preferred_element_type=jnp.float32)
        value_grad = lax.psum(placed, "tensor").astype(jnp.bfloat16)
        value_grad_w = jnp.dot(normed.T, value_grad, preferred_element_type=jnp.float32)
        normed_grad = jnp.dot(value_grad, value_eff.T, preferred_element_type=jnp.float32)
        input_grad = (incoming.astype(jnp.float32) + inverse_rms * gain_row * normed_grad).astype(
            jnp.bfloat16
        )
        return (input_grad, out_grad, value_grad_w)

    current = hidden_in
    hop_idx = 0
    produced, unused_saved = forward(current, attn_probs)
    arrived = from_behind(produced, "section", 1)
    current = jnp.where(section_idx == hop_idx + 1, arrived, current)
    produced, saved = forward(current, attn_probs)
    incoming = cotangent
    hop_idx = 0
    input_grad, unused_out, unused_value = backward(incoming, saved, probs_local)
    arrived = from_behind(input_grad, "section", -1)
    incoming = jnp.where(section_idx == section_count - 2 - hop_idx, arrived, incoming)
    input_grad, out_grad_total, value_grad_total = backward(incoming, saved, probs_local)
    out_slope = out_grad_total * (1.0 - jnp.cos(full_turn * out_ratio))
    value_slope = value_grad_total * (1.0 - jnp.cos(full_turn * value_ratio))
    partial_rot = jnp.einsum(
        "chk,hjc->kj",
        out_heads,
        out_slope.reshape(head_count, head_dim, local_width),
        precision=precise,
    )
    partial_rot = partial_rot + jnp.einsum(
        "dgk,dgj->kj",
        value_heads,
        value_slope.reshape(local_width, kv_count, head_dim),
        precision=precise,
    )
    rot_grad = lax.psum(partial_rot, "tensor")
    return (rot_grad[None], cayley(rot_grad, rotation_mat)[None])


def solution(mesh):
    in_specs = (
        P("groups", "tensor"),
        P("groups", "tensor"),
        P("section", "tensor"),
        P("section", "tensor", None),
        P("section", "tensor", None),
        P("section", None, None),
        P("section", "groups", None, None),
    )
    out_specs = (P("section", "groups", None), P("section", "groups", None))
    return jax.shard_map(
        on_device, mesh=mesh, in_specs=in_specs, out_specs=out_specs, check_vma=False
    )
```

profile of v0, /device:TPU:0, one launch (start us, length us, event | category | flops | bytes accessed | tf_op | source)
XLA Modules:
  0.0 1301.1 jit_solution(4640352599582029376)
XLA Ops:
  7.2 9.7 copy.59
  16.9 52.7 %fusion.4 = (f32[1024]{0:T(1024)S(1)}, f32[128,1024,64]{1,0,2:T(8,128)}) fusion(bf16[1024,64,128]{2,1,0:T(8,128)(2,1)S(1)} %bitcast.154, f32[1,128,128]{2,1,0:T(8,128)S(1)} %copy-done.9), kind=kOutput, calls=%fused_computation.8 | convolution fusion | flops 12901678080 | bytes 50401280 | tf_op jit(solution)/shard_map/chk,kj->hjc/dot_general | solution.py:85
  69.6 31.9 %copy.29 = f32[8,1024,1024]{1,2,0:T(8,128)} copy(f32[8,1024,1024]{2,1,0:T(8,128)} %bitcast.153) | data formatting | bytes 67108864 | tf_op jit(solution)/shard_map/reshape | solution.py:85
  101.5 123.2 %multiply_convert_fusion = bf16[8,1024,1024]{1,2,0:T(8,128)(2,1)} fusion(f32[8,1024,1024]{1,2,0:T(8,128)} %copy.29, f32[1024]{0:T(1024)S(1)} %add_multiply_fusion), kind=kLoop, calls=%fused_computation.9 | loop fusion | flops 50331648 | bytes 50335744 | tf_op jit(solution)/shard_map/convert_element_type | solution.py:89
  224.7 7.2 all-to-all-start
  232.7 2.2 copy.57
  235.1 306.8 %psum.49 = f32[128]{0:T(128)S(1)} all-reduce(f32[128]{0:T(128)S(1)} %fusion.45), channel_id=1, replica_groups=mesh['groups'=2,'tensor'=8,'section'=2] {'tensor'}, use_global_device_ids=true, to_apply=%region_1.0 | all-reduce | flops 128 | bytes 1024 | tf_op jit(solution)/shard_map/psum | solution.py:100
  541.9 3.9 abs_reduce_fusion
  545.8 106.0 %pmax.7 = f32[1024]{0:T(1024)S(1)} all-reduce(f32[1024]{0:T(1024)S(1)} %bitcast.175), channel_id=1, replica_groups=mesh['groups'=2,'tensor'=8,'section'=2] {'tensor'}, use_global_device_ids=true, to_apply=%region_3.4 | all-reduce | flops 1024 | bytes 8192 | tf_op jit(solution)/shard_map/pmax | solution.py:76
  651.9 117.3 %multiply_convert_fusion.1 = bf16[64,128,1024]{2,1,0:T(8,128)(2,1)} fusion(f32[128,1024,64]{1,0,2:T(8,128)} %get-tuple-element.15, f32[1024]{0:T(1024)S(1)} %add_multiply_fusion), kind=kLoop, calls=%fused_computation.10 | loop fusion | flops 50331648 | bytes 50335744 | tf_op jit(solution)/shard_map/convert_element_type | solution.py:89
  769.2 17.0 %multiply_convert_fusion.2 = (bf16[1024,1024]{0,1:T(8,128)(2,1)S(1)}, f32[1024,1024]{0,1:T(8,128)}) fusion(f32[1024]{0:T(1024)S(1)} %add_multiply_fusion.1, f32[1024,8,128]{0,2,1:T(8,128)S(1)} %copy-done.5), kind=kLoop, calls=%fused_computation.20 | loop fusion | flops 6291456 | bytes 10489856 | tf_op jit(solution)/shard_map/convert_element_type | solution.py:79
  787.9 41.6 %all-reduce.8 = bf16[128,1024]{1,0:T(8,128)(2,1)} all-reduce(f32[128,1024]{1,0:T(8,128)} %fusion.49), channel_id=1, replica_groups=mesh['groups'=2,'tensor'=8,'section'=2] {'tensor'}, use_global_device_ids=true, to_apply=%region_4.5 | all-reduce | flops 131072 | bytes 786432 | tf_op jit(solution)/shard_map/psum | solution.py:104
  831.2 3.3 reshape.140
  835.4 2.3 convert_bitcast_fusion.1
  837.7 2.7 copy.24
  840.4 4.2 convert_element_type.108
  844.6 9.5 fusion.19
  854.0 2.0 collective-permute-start
  856.0 3.4 reshape_squeeze.3
  859.5 2.9 gather_fusion
  862.6 10.9 fusion.23
  876.4 41.6 %all-reduce.9 = (bf16[128,1024]{1,0:T(8,128)(2,1)S(1)}, f32[128]{0:T(128)S(1)}) all-reduce(f32[128,1024]{1,0:T(8,128)S(1)} %fusion.10, f32[128]{0:T(128)S(1)} %fusion.42), channel_id=1, replica_groups=mesh['groups'=2,'tensor'=8,'section'=2] {'tensor'}, use_global_device_ids=true, to_apply=%region_9.10 | all-reduce | flops 131200 | bytes 787456 | tf_op jit(solution)/shard_map/psum | solution.py:133
  919.8 2.1 collective-permute-done.1
  923.9 45.8 %all-gather.5.cloned.1.call-done = bf16[128,8192]{1,0:T(8,128)(2,1)} async-done(((bf16[128,1024]{1,0:T(8,128)(2,1)}), bf16[128,8192]{1,0:T(8,128)(2,1)}) %all-gather.5.cloned.1.call-update) | async-done | bytes 2097168 | tf_op jit(solution)/shard_map/all_gather | solution.py:119
  969.7 8.7 fusion.22
  980.0 70.2 %all-reduce.10 = (bf16[128,1024]{1,0:T(8,128)(2,1)}, bf16[128,1024]{1,0:T(8,128)(2,1)}) all-reduce(f32[128,1024]{1,0:T(8,128)S(1)} %fusion.9, f32[128,1024]{1,0:T(8,128)S(1)} %fusion.79), channel_id=1, replica_groups=mesh['groups'=2,'tensor'=8,'section'=2] {'tensor'}, use_global_device_ids=true, to_apply=%region_10.11 | all-reduce | flops 262144 | bytes 1572864 | tf_op jit(solution)/shard_map/psum | solution.py:133
  1053.4 2.3 convert_element_type.117
  1055.7 116.5 %fusion.3 = f32[8192,1024]{1,0:T(8,128)} fusion(f32[128,1024,64]{1,0,2:T(8,128)} %get-tuple-element.15, f32[1024]{0:T(1024)S(1)} %add_multiply_fusion, bf16[128,8192]{1,0:T(8,128)(2,1)} %convert_element_type.117, bf16[128,1024]{1,0:T(8,128)(2,1)S(1)} %copy-done.10), kind=kOutput, calls=%fused_computation.5 | convolution fusion | flops 2181038080 | bytes 69472256 | tf_op jit(solution)/shard_map/dot_general | solution.py:118
  1172.2 14.0 %subtract_multiply_fusion = f32[1024,1024]{0,1:T(8,128)S(1)} fusion(f32[1024,1024]{0,1:T(8,128)S(1)} %copy-done.1, bf16[128,1024]{1,0:T(8,128)(2,1)S(1)} %copy-done.11, f32[128]{0:T(128)S(1)} %add_rsqrt_fusion, f32[1024]{0:T(1024)S(1)} %bitcast.174, bf16[128,1024]{1,0:T(8,128)(2,1)} %collective-permute-done, bf16[128,1024]{1,0:T(8,128)(2,1)S(1)} %copy-done.6, ...), kind=kOutput, calls=%fused_computation.16 | convolution fusion | flops 272236544 | bytes 9179649 | tf_op jit(solution)/shard_map/dot_general | solution.py:134
  1186.2 2.4 fusion.33
  1188.6 33.5 %fusion.39 = f32[128,128]{0,1:T(8,128)} fusion(f32[128,128]{1,0:T(8,128)S(1)} %fusion.33, f32[64,128,1024]{2,1,0:T(8,128)} %bitcast.157, bf16[1024,64,128]{2,1,0:T(8,128)(2,1)} %bitcast.155), kind=kOutput, calls=%fused_computation.55 | convolution fusion | flops 12884918272 | bytes 50462720 | tf_op jit(solution)/shard_map/chk,hjc->kj/dot_general | solution.py:155
  1222.1 68.2 %all-reduce.7.cloned.1.call-done = f32[128,128]{0,1:T(8,128)} async-done(((f32[128,128]{0,1:T(8,128)}), f32[128,128]{0,1:T(8,128)}) %all-reduce.7.cloned.1.call-update) | async-done | bytes 65552 | tf_op jit(solution)/shard_map/psum | solution.py:167
  (72 shorter events, 20.7 us)
Async XLA Ops:
  7.2 9.7 copy-start.9
  16.9 52.7 %copy-start = (bf16[128,8,64,128]{3,2,1,0:T(8,128)(2,1)}, bf16[128,8,64,128]{3,2,1,0:T(8,128)(2,1)S(1)}, u32[]{:S(2)}) copy-start(bf16[128,8,64,128]{3,2,1,0:T(8,128)(2,1)S(1)} %copy.59) | copy-start | bytes 50331652
  224.7 637.9 %all-to-all-start = ((bf16[8,1024,1024]{1,2,0:T(8,128)(2,1)}), bf16[8,1024,1024]{1,2,0:T(8,128)(2,1)}, u32[]{:S(2)}, u32[]{:S(2)}) async-start(bf16[8,1024,1024]{1,2,0:T(8,128)(2,1)} %multiply_convert_fusion), calls=%async_computation | async-start | bytes 33554432 | tf_op jit(solution)/shard_map/all_to_all | solution.py:96
  232.0 3.0 copy-start.6
  232.0 630.6 %all-gather.3.cloned.1.call-start = ((), (), s32[]{:S(2)}) async-start(), calls=%async_computation.1 | async-start | bytes 2359296 | tf_op jit(solution)/shard_map/all_gather | solution.py:119
  232.7 737.0 %all-gather.5.cloned.1.call-start = ((), (), s32[]{:S(2)}) async-start(), calls=%async_computation.2 | async-start | bytes 2359296 | tf_op jit(solution)/shard_map/all_gather | solution.py:119
  235.0 534.2 %copy-start.2 = (bf16[128,8,8,128]{3,2,1,0:T(8,128)(2,1)}, bf16[128,8,8,128]{3,2,1,0:T(8,128)(2,1)S(1)}, u32[]{:S(2)}) copy-start(bf16[128,8,8,128]{3,2,1,0:T(8,128)(2,1)S(1)} %copy.57) | copy-start | bytes 6291460
  651.9 117.3 %copy-start.5 = (f32[1024,8,128]{0,2,1:T(8,128)S(1)}, f32[1024,8,128]{0,2,1:T(8,128)}, u32[]{:S(2)}) copy-start(f32[1024,8,128]{0,2,1:T(8,128)} %get-tuple-element.13) | copy-start | bytes 12582916
  769.2 17.1 %copy-start.13 = (f32[1,1024]{1,0:T(1,128)S(1)}, f32[1,1024]{1,0:T(1,128)}, u32[]{:S(2)}) copy-start(f32[1,1024]{1,0:T(1,128)} %param.9) | copy-start | bytes 12292
  786.2 44.9 %copy-start.7 = (bf16[1,2,64,4096]{3,2,1,0:T(8,128)(2,1)S(1)}, bf16[1,2,64,4096]{3,2,1,0:T(8,128)(2,1)}, u32[]{:S(2)}) copy-start(bf16[1,2,64,4096]{3,2,1,0:T(8,128)(2,1)} %param.13) | copy-start | bytes 3145732
  854.0 8.3 collective-permute-start
  873.5 44.6 %copy-start.8 = (bf16[128,1024]{1,0:T(8,128)(2,1)S(1)}, bf16[128,1024]{1,0:T(8,128)(2,1)}, u32[]{:S(2)}) copy-start(bf16[128,1024]{1,0:T(8,128)(2,1)} %param.8) | copy-start | bytes 786436
  918.5 3.4 collective-permute-start.1
  922.7 367.6 %all-reduce.7.cloned.1.call-start = ((), (), s32[]{:S(2)}) async-start(), calls=%async_computation.3 | async-start | bytes 131072 | tf_op jit(solution)/shard_map/psum | solution.py:167
  923.8 54.7 %copy-start.12 = (bf16[8,2,64,64]{3,2,1,0:T(8,128)(2,1)S(1)}, bf16[8,2,64,64]{3,2,1,0:T(8,128)(2,1)}, u32[]{:S(2)}) copy-start(bf16[8,2,64,64]{3,2,1,0:T(8,128)(2,1)} %gather_fusion) | copy-start | bytes 393220
  978.4 72.8 %copy-start.4 = (bf16[2,8,8,64,64]{4,3,2,1,0:T(8,128)(2,1)S(1)}, bf16[2,8,8,64,64]{4,3,2,1,0:T(8,128)(2,1)}, u32[]{:S(2)}) copy-start(bf16[2,8,8,64,64]{4,3,2,1,0:T(8,128)(2,1)} %reshape.140) | copy-start | bytes 3145732
  1052.0 3.7 copy-start.10
  1055.7 116.5 %copy-start.1 = (f32[1024,1024]{0,1:T(8,128)S(1)}, f32[1024,1024]{0,1:T(8,128)}, u32[]{:S(2)}) copy-start(f32[1024,1024]{0,1:T(8,128)} %get-tuple-element.11) | copy-start | bytes 12582916
  1055.7 116.5 %copy-start.11 = (bf16[128,1024]{1,0:T(8,128)(2,1)S(1)}, bf16[128,1024]{1,0:T(8,128)(2,1)}, u32[]{:S(2)}) copy-start(bf16[128,1024]{1,0:T(8,128)(2,1)} %get-tuple-element.6) | copy-start | bytes 786436
  1172.2 14.0 %copy-start.3 = (bf16[128,8,8,128]{3,2,1,0:T(8,128)(2,1)S(1)}, bf16[128,8,8,128]{3,2,1,0:T(8,128)(2,1)}, u32[]{:S(2)}) copy-start(bf16[128,8,8,128]{3,2,1,0:T(8,128)(2,1)} %copy-done.2) | copy-start | bytes 6291460
Sparse Core Ops, SparseCore 0:
  235.0 305.4 all-gather.2
  922.9 46.7 all-gather.4
  1222.2 68.0 all-reduce.6
where the time goes:
time: 1320 us; the launch traced here: 1300 us
  blocking collectives  566 us (43%)
  matrix products  264 us (20%)
  other arithmetic  259 us (20%)
  waiting for transfers between devices  117 us (9%)
  local copies, waits for them, and re-layouts  70 us (5%)
  between operations  14.4 us (1%)
    psum x1, blocking collectives, forward(): squares = lax.psum(jnp.sum(widened * widened, axis=1), 'tensor')  307 us
    convert_element_type x2, other arithmetic, on_device(): out_eff = out_q.astype(jnp.bfloat16)  240 us
    dot_general x1, matrix products, backward(): jnp.dot(mixed_heads.T, incoming, preferred_element_type=jnp.float32)  116 us
    psum x2, blocking collectives, backward(): value_grad = lax.psum(placed, 'tensor').astype(jnp.bfloat16)  112 us
    pmax x1, blocking collectives, on_device(): value_peak = lax.pmax(jnp.max(jnp.abs(value_rot), axis=0), 'tensor')  106 us
    psum x1, waiting for transfers between devices, on_device(): rot_grad = lax.psum(partial_rot, 'tensor')  68.2 us
    dot_general x1, matrix products, on_device(): jnp.einsum('chk,kj->hjc', out_heads, rotation_mat, precision=precise)  52.7 us
    all_gather x2, waiting for transfers between devices, backward(): lax.all_gather(incoming, 'tensor', axis=1, tiled=True)  45.9 us
  transfers between devices with their start and end apart: 6, of which 3 were waited for; matrix products, arithmetic and copies ran while one was open for 13% of the time, Pallas kernels for 0%

commit v1 on v0

v1 whole, which is shorter than its diff:
```python
import functools

import jax
import jax.numpy as jnp
from jax import lax
from jax.experimental import pallas as pl
from jax.experimental.pallas import tpu as pltpu
from jax.sharding import PartitionSpec as P

quant_levels = 7.0
norm_eps = 1e-05
scale_eps = 1e-06
step_size = 0.1
precise = lax.Precision.HIGHEST
F32 = jnp.float32
BF16 = jnp.bfloat16
LANES = 128
VMEM_BYTES = 56 * 1024 * 1024

sin_coefs = (3.141582078119497, -5.16714420271071, 2.541908924984016, -0.5546570710297597)
cos_coefs = (0.31830775207531137, -1.570521249499652, 1.2863806003857212, -0.38901512525748255)


def dot_nn(a, b):
    return lax.dot_general(a, b, (((1,), (0,)), ((), ())), preferred_element_type=F32)


def dot_nt(a, b):
    return lax.dot_general(a, b, (((1,), (1,)), ((), ())), preferred_element_type=F32)


def dot_tn(a, b):
    return lax.dot_general(a, b, (((0,), (0,)), ((), ())), preferred_element_type=F32)


def horner(coefs, z):
    total = coefs[-1] * z + coefs[-2]
    for coef in coefs[-3::-1]:
        total = total * z + coef
    return total


def soft_parts(ratio):
    whole = jnp.round(ratio)
    rest = ratio - whole
    square = rest * rest
    sine = rest * horner(sin_coefs, square)
    cosine = horner(cos_coefs, square)
    return whole + (rest - sine * cosine), sine * sine


def rotation_pair(rot):
    high = rot.astype(BF16)
    low = (rot - high.astype(F32)).astype(BF16)
    zero = jnp.zeros_like(high)

    def blocks(part):
        return jnp.concatenate(
            [jnp.concatenate([part, zero], 1), jnp.concatenate([zero, part], 1)], 0
        )

    return blocks(high), blocks(low)


def column_of(row):
    count = row.shape[1]
    return jnp.transpose(jnp.broadcast_to(row, (count, count)))


def call(kernel, out_shape, cost, **kw):
    flops, moved = cost
    return pl.pallas_call(
        kernel,
        out_shape=out_shape,
        compiler_params=pltpu.CompilerParams(vmem_limit_bytes=VMEM_BYTES),
        cost_estimate=pl.CostEstimate(flops=flops, bytes_accessed=moved, transcendentals=0),
        **kw,
    )


def shaped(shape, dtype):
    return jax.ShapeDtypeStruct(shape, dtype)


def value_rot_kernel(hidden_ref, ct_ref, value_ref, rot_ref, x_ref, ct_t_ref, vrot_ref, stat_ref):
    kv_width = value_ref.shape[1]
    high, low = rotation_pair(rot_ref[...])
    for at in range(0, kv_width, 2 * LANES):
        cols = slice(at, at + 2 * LANES)
        block = value_ref[:, cols]
        turned = dot_nn(block, high) + dot_nn(block, low)
        vrot_ref[:, cols] = turned
        stat_ref[:, cols] = jnp.max(jnp.abs(turned), axis=0, keepdims=True)
    x = jnp.transpose(hidden_ref[...].astype(F32))
    x_ref[...] = x.astype(BF16)
    stat_ref[:, kv_width:] = jnp.sum(x * x, axis=0, keepdims=True)
    ct_t_ref[...] = jnp.transpose(ct_ref[...].astype(F32)).astype(BF16)


def mix_back(probs_ref, grad_of, out_ref, seq, per_group, kv_count):
    blocks = probs_ref.shape[0]
    for b in range(blocks):
        rows = slice(b * seq, (b + 1) * seq)
        for k in range(kv_count):
            stacked = jnp.concatenate(
                [
                    grad_of(rows, slice(h * LANES, (h + 1) * LANES))
                    for h in range(k * per_group, (k + 1) * per_group)
                ],
                0,
            )
            probs = probs_ref[b, k * per_group * seq : (k + 1) * per_group * seq, :]
            out_ref[rows, k * LANES : (k + 1) * LANES] = dot_tn(probs, stacked).astype(
                out_ref.dtype
            )


def mix_forward(probs_ref, values_of, mixed_ref, seq, per_group, kv_count):
    blocks = probs_ref.shape[0]
    for b in range(blocks):
        rows = slice(b * seq, (b + 1) * seq)
        for k in range(kv_count):
            probs = probs_ref[b, k * per_group * seq : (k + 1) * per_group * seq, :]
            heads = dot_nn(probs, values_of(rows, slice(k * LANES, (k + 1) * LANES))).astype(BF16)
            for j in range(per_group):
                h = k * per_group + j
                mixed_ref[rows, h * LANES : (h + 1) * LANES] = heads[j * seq : (j + 1) * seq]


def prep_kernel(
    kv_count, w_ref, rot_ref, ct_ref, probs_ref,
    q_ref, slope_ref, scale_ref, back_ref, vg_ref,
    turned_ref, inv_ref, total_ref,
):
    rows, width = w_ref.shape
    high, low = rotation_pair(rot_ref[...])
    peak = jnp.zeros((rows, 2 * LANES), F32)
    for at in range(0, width, 2 * LANES):
        cols = slice(at, at + 2 * LANES)
        block = w_ref[:, cols]
        turned = dot_nn(block, high) + dot_nn(block, low)
        turned_ref[:, cols] = turned
        peak = jnp.maximum(peak, jnp.abs(turned))
    peak = jnp.max(peak, axis=1, keepdims=True)
    scale = (peak + scale_eps) / quant_levels
    scale_ref[...] = scale
    inv_ref[...] = jnp.broadcast_to(1.0 / scale, inv_ref.shape)
    step, span = 16, min(512, width)

    @pl.loop(0, rows // step)
    def _(i):
        here = pl.ds(pl.multiple_of(i * step, step), step)
        inv = inv_ref[here, :1]
        for at in range(0, width, span):
            cols = slice(at, at + span)
            effective, slope = soft_parts(turned_ref[here, cols] * inv)
            q_ref[here, cols] = effective.astype(BF16)
            slope_ref[here, cols] = slope.astype(BF16)

    scaled = (ct_ref[...].astype(F32) * scale).astype(BF16)

    @pl.when(pl.program_id(0) == 0)
    def _():
        total_ref[...] = jnp.zeros_like(total_ref)

    wide = min(1024, width)
    for at in range(0, width, wide):
        cols = slice(at, at + wide)
        total_ref[:, cols] += dot_tn(scaled, q_ref[:, cols])

    @pl.when(pl.program_id(0) == pl.num_programs(0) - 1)
    def _():
        back_ref[...] = total_ref[...].astype(BF16)
        seq = probs_ref.shape[2]
        per_group = width // LANES // kv_count
        mix_back(
            probs_ref, lambda r, c: back_ref[r, c], vg_ref, seq, per_group, kv_count
        )


def value_quant_kernel(
    turned_ref, stats_ref, x_ref, gain_ref, q_ref, slope_ref, part_ref, scale_ref, mean_ref, *, model_width
):
    kv_width = turned_ref.shape[1]
    stats = stats_ref[...]
    scale = (jnp.max(stats[:, :kv_width], axis=0, keepdims=True) + scale_eps) / quant_levels
    scale_ref[...] = scale
    squares = jnp.sum(stats[:, kv_width:], axis=0, keepdims=True)
    mean_ref[...] = lax.rsqrt(squares / model_width + norm_eps)
    inv = 1.0 / scale
    step = 16

    @pl.loop(0, turned_ref.shape[0] // step)
    def _(i):
        here = pl.ds(pl.multiple_of(i * step, step), step)
        effective, slope = soft_parts(turned_ref[here, :] * inv)
        q_ref[here, :] = effective.astype(BF16)
        slope_ref[here, :] = slope.astype(BF16)

    gained = (x_ref[...].astype(F32) * gain_ref[...]).astype(BF16)
    part_ref[...] = dot_tn(gained, q_ref[...]).astype(BF16)


def input_grad_kernel(vg_ref, scale_ref, q_ref, gain_ref, out_ref):
    scaled = (vg_ref[...].astype(F32) * scale_ref[...]).astype(BF16)
    out_ref[...] = (dot_nt(q_ref[...], scaled) * gain_ref[...]).astype(BF16)


def forward_kernel(
    kv_count, values_ref, mean_ref, vscale_ref, probs_ref, q_ref, scale_ref, x_ref, grad_ref,
    mixed_ref, out_ref, back_ref, total_ref, v_ref,
):
    first = pl.program_id(0) == 0
    width = q_ref.shape[1]
    seq = probs_ref.shape[2]
    per_group = width // LANES // kv_count

    @pl.when(first)
    def _():
        total_ref[...] = jnp.zeros_like(total_ref)
        inverse = column_of(mean_ref[...])
        for k in range(kv_count):
            cols = slice(k * LANES, (k + 1) * LANES)
            v_ref[:, cols] = (
                values_ref[:, cols].astype(F32) * inverse[:, :1] * vscale_ref[:, cols]
            ).astype(BF16)
        mix_forward(probs_ref, lambda r, c: v_ref[r, c], mixed_ref, seq, per_group, kv_count)

    scale = scale_ref[...]
    out_ref[...] = (x_ref[...].astype(F32) + dot_nt(q_ref[...], mixed_ref[...]) * scale).astype(BF16)
    scaled = (grad_ref[...].astype(F32) * scale).astype(BF16)
    wide = min(1024, width)
    for at in range(0, width, wide):
        cols = slice(at, at + wide)
        total_ref[:, cols] += dot_tn(scaled, q_ref[:, cols])

    @pl.when(pl.program_id(0) == pl.num_programs(0) - 1)
    def _():
        back_ref[...] = total_ref[...].astype(BF16)


def project_kernel(x_ref, gain_ref, q_ref, out_ref):
    kv_width = q_ref.shape[1]
    x = x_ref[...].astype(F32)
    gained = (x * gain_ref[...]).astype(BF16)
    out_ref[:, :kv_width] = dot_tn(gained, q_ref[...]).astype(BF16)
    squares = jnp.sum(x * x, axis=0, keepdims=True)
    tokens = squares.shape[1]
    out_ref[:, kv_width:] = jnp.broadcast_to(squares, (tokens, tokens)).astype(BF16)


def value_grad_kernel(kv_count, mean_ref, ct_back_ref, back_ref, probs_ref, out_ref):
    inverse = column_of(mean_ref[...])[:, :1]
    seq = probs_ref.shape[2]
    per_group = back_ref.shape[1] // LANES // kv_count

    def grad_of(rows, cols):
        return (
            ct_back_ref[rows, cols].astype(F32) + inverse[rows] * back_ref[rows, cols].astype(F32)
        ).astype(BF16)

    mix_back(probs_ref, grad_of, out_ref, seq, per_group, kv_count)


def out_grad_kernel(
    kv_count, section_ref, values_ref, mean_ref, vscale_ref, probs_ref, mixed_in_ref,
    ct_ref, grad_ref, w_ref, slope_ref, out_ref, mixed_ref, total_ref,
):
    width = w_ref.shape[1]
    seq = probs_ref.shape[2]
    per_group = width // LANES // kv_count
    last_section = section_ref[0] != 0

    @pl.when(pl.program_id(0) == 0)
    def _():
        total_ref[...] = jnp.zeros_like(total_ref)

        @pl.when(last_section)
        def _():
            inverse = column_of(mean_ref[...])[:, :1]

            def values_of(rows, cols):
                return (
                    values_ref[rows, cols].astype(F32) * inverse[rows] * vscale_ref[:, cols]
                ).astype(BF16)

            mix_forward(probs_ref, values_of, mixed_ref, seq, per_group, kv_count)

        @pl.when(jnp.logical_not(last_section))
        def _():
            mixed_ref[...] = mixed_in_ref[...]

    keep = jnp.where(last_section, 0.0, 1.0)
    grad = (
        ct_ref[...].astype(F32) + (keep * mean_ref[...]) * grad_ref[...].astype(F32)
    ).astype(BF16)
    for at in range(0, width, 2 * LANES):
        cols = slice(at, at + 2 * LANES)
        out_grad = dot_nn(grad, mixed_ref[:, cols])
        sloped = (out_grad * slope_ref[:, cols].astype(F32)).astype(BF16)
        total_ref[...] += dot_tn(w_ref[:, cols], sloped)

    @pl.when(pl.program_id(0) == pl.num_programs(0) - 1)
    def _():
        out_ref[...] = total_ref[:LANES, :LANES] + total_ref[LANES:, LANES:]


def value_part_kernel(x_ref, mean_ref, gain_ref, vg_ref, v_ref, slope_ref, other_ref, out_ref):
    normed = (x_ref[...].astype(F32) * mean_ref[...] * gain_ref[...]).astype(BF16)
    total = other_ref[...]
    for at in range(0, v_ref.shape[1], 2 * LANES):
        cols = slice(at, at + 2 * LANES)
        grad = dot_nn(normed, vg_ref[:, cols])
        sloped = (grad * slope_ref[:, cols].astype(F32)).astype(BF16)
        both = dot_tn(v_ref[:, cols], sloped)
        total = total + both[:LANES, :LANES] + both[LANES:, LANES:]
    out_ref[...] = (2.0 * total).astype(out_ref.dtype)


def cayley_kernel(parts_ref, rot_ref, grad_ref, new_ref):
    count = parts_ref.shape[0] // LANES
    grad = parts_ref[:LANES].astype(F32)
    for i in range(1, count):
        grad = grad + parts_ref[i * LANES : (i + 1) * LANES].astype(F32)
    grad_ref[...] = grad
    rot = rot_ref[...]

    def product(a, b, dims=(1, 0)):
        return lax.dot_general(
            a, b, (((dims[0],), (dims[1],)), ((), ())), precision=precise, preferred_element_type=F32
        )

    turn = product(grad, rot, (1, 1))
    skew = turn - jnp.transpose(turn)
    update = rot - step_size * product(skew, rot)
    for _ in range(2):
        update = rot - 0.5 * step_size * product(skew, rot + update)
    new_ref[...] = update


def exchange(rows):
    return lax.all_to_all(rows, "tensor", split_axis=0, concat_axis=0, tiled=True)


def on_device(hidden, cotangent, norm_gain, value_weight, output_weight, rotation, attention):
    section = lax.axis_index("section")
    count = lax.axis_size("tensor")
    is_first = section == 0
    flag = section.astype(jnp.int32).reshape(1)
    rot = rotation[0]
    value_w = value_weight[0]
    out_w = output_weight[0]
    local, width = out_w.shape
    kv_width = value_w.shape[1]
    kv_count = kv_width // LANES
    tokens = hidden.shape[0]
    _, blocks, heads, flat = attention.shape
    seq = tokens // blocks
    probs = attention[0].reshape(blocks, heads * seq, seq)
    gain = norm_gain[0].reshape(local, 1)
    model_width = local * count
    big = 2 * tokens * local * width

    x0, ct, value_rot, stat = call(
        value_rot_kernel,
        (
            shaped((local, tokens), BF16),
            shaped((local, tokens), BF16),
            shaped((local, kv_width), F32),
            shaped((1, kv_width + tokens), F32),
        ),
        (4 * local * kv_width * LANES, 6 * local * kv_width),
    )(hidden, cotangent, value_w, rot)
    stats = lax.all_gather(stat, "tensor", axis=0, tiled=True)

    rows = min(local, 256)
    steps = local // rows

    def split(*tail):
        return pl.BlockSpec((rows,) + tail, lambda i: (i, 0))

    def whole(*shape):
        return pl.BlockSpec(shape, lambda i: (0,) * len(shape))

    quant, slope, scale, ct_back, ct_vg = call(
        functools.partial(prep_kernel, kv_count),
        (
            shaped((local, width), BF16),
            shaped((local, width), BF16),
            shaped((local, 1), F32),
            shaped((tokens, width), BF16),
            shaped((tokens, kv_width), BF16),
        ),
        (3 * big, 6 * local * width),
        grid=(steps,),
        in_specs=[split(width), whole(LANES, LANES), split(tokens), whole(*probs.shape)],
        out_specs=(
            split(width),
            split(width),
            split(1),
            whole(tokens, width),
            whole(tokens, kv_width),
        ),
        scratch_shapes=[
            pltpu.VMEM((rows, width), F32),
            pltpu.VMEM((rows, LANES), F32),
            pltpu.VMEM((tokens, width), F32),
        ],
    )(out_w, rot, ct, probs)

    value_q, value_slope, value_part, value_scale, mean0 = call(
        functools.partial(value_quant_kernel, model_width=model_width),
        (
            shaped((local, kv_width), BF16),
            shaped((local, kv_width), BF16),
            shaped((tokens, kv_width), BF16),
            shaped((1, kv_width), F32),
            shaped((1, tokens), F32),
        ),
        (2 * local * kv_width * tokens, 8 * local * kv_width),
    )(value_rot, stats, x0, gain)

    def add_parts(received):
        return received.reshape(count, tokens // count, -1).astype(F32).sum(0)

    def spread(part):
        return jnp.tile(part.astype(BF16), (count, 1))

    summed = exchange(spread(add_parts(exchange(jnp.where(is_first, value_part, ct_vg)))))

    grad1 = call(
        input_grad_kernel,
        shaped((local, tokens), BF16),
        (2 * local * kv_width * tokens, 2 * local * kv_width),
    )(summed, value_scale, value_q, gain)
    grad1 = lax.ppermute(grad1, "section", [(1, 0)])

    mixed, x1, grad_back = call(
        functools.partial(forward_kernel, kv_count),
        (
            shaped((tokens, width), BF16),
            shaped((local, tokens), BF16),
            shaped((tokens, width), BF16),
        ),
        (2 * big, 2 * local * width),
        grid=(steps,),
        in_specs=[
            whole(tokens, kv_width),
            whole(1, tokens),
            whole(1, kv_width),
            whole(*probs.shape),
            split(width),
            split(1),
            split(tokens),
            split(tokens),
        ],
        out_specs=(whole(tokens, width), split(tokens), whole(tokens, width)),
        scratch_shapes=[pltpu.VMEM((tokens, width), F32), pltpu.VMEM((tokens, kv_width), BF16)],
    )(summed, mean0, value_scale, probs, quant, scale, x0, grad1)
    arrived = lax.ppermute(x1, "section", [(0, 1)])
    x1 = jnp.where(is_first, x1, arrived)

    projected = call(
        project_kernel,
        shaped((tokens, kv_width + tokens), BF16),
        (2 * local * kv_width * tokens, 2 * local * kv_width),
    )(x1, gain, value_q)
    received = add_parts(exchange(projected))
    mean1 = lax.rsqrt(received[:1, kv_width:] / model_width + norm_eps)

    vg0 = call(
        functools.partial(value_grad_kernel, kv_count),
        shaped((tokens, kv_width), BF16),
        (2 * tokens * width * seq, 6 * tokens * width),
    )(mean1, ct_back, grad_back, probs)
    values1 = exchange(jnp.where(is_first, vg0, spread(received[:, :kv_width])))
    vg_full = exchange(spread(add_parts(values1)))

    out_part = call(
        functools.partial(out_grad_kernel, kv_count),
        shaped((LANES, LANES), F32),
        (2 * big, 4 * local * width),
        grid=(steps,),
        in_specs=[
            pl.BlockSpec(memory_space=pltpu.SMEM),
            whole(tokens, kv_width),
            whole(1, tokens),
            whole(1, kv_width),
            whole(*probs.shape),
            whole(tokens, width),
            split(tokens),
            split(tokens),
            split(width),
            split(width),
        ],
        out_specs=whole(LANES, LANES),
        scratch_shapes=[
            pltpu.VMEM((tokens, width), BF16),
            pltpu.VMEM((2 * LANES, 2 * LANES), F32),
        ],
    )(flag, values1, mean1, value_scale, probs, mixed, ct, grad1, out_w, slope)

    rot_part = call(
        value_part_kernel,
        shaped((LANES, LANES), BF16),
        (4 * local * kv_width * tokens, 4 * local * kv_width),
    )(
        jnp.where(is_first, x0, x1),
        jnp.where(is_first, mean0, mean1),
        gain,
        jnp.where(is_first, vg_full, summed),
        value_w,
        value_slope,
        out_part,
    )
    rot_grad, rot_new = call(
        cayley_kernel,
        (shaped((LANES, LANES), F32), shaped((LANES, LANES), F32)),
        (12 * 5 * LANES**3, 8 * LANES**2),
    )(exchange(jnp.tile(rot_part, (count, 1))), rot)
    return rot_grad[None], rot_new[None]


def solution(mesh):
    in_specs = (
        P("groups", "tensor"),
        P("groups", "tensor"),
        P("section", "tensor"),
        P("section", "tensor", None),
        P("section", "tensor", None),
        P("section", None, None),
        P("section", "groups", None, None),
    )
    out_specs = (P("section", "groups", None), P("section", "groups", None))
    return jax.shard_map(
        on_device, mesh=mesh, in_specs=in_specs, out_specs=out_specs, check_vma=False
    )
```

time: 1320 us -> 237 us (0.18); the launches traced: 1300 us -> 236 us
  blocking collectives: 566 us -> 97.6 us
  matrix products: 264 us -> 0 us
  other arithmetic: 259 us -> 5.28 us
  Pallas kernels: 0 us -> 114 us
  waiting for transfers between devices: 117 us -> 3.5 us
  local copies, waits for them, and re-layouts: 70 us -> 8.83 us
  between operations: 14.4 us -> 0.74 us
    psum x4 -> x0, blocking collectives: 460 us -> none  [the longest x1 307 us: forward(): squares = lax.psum(jnp.sum(widened * widened, axis=1), 'tensor')]
    dot_general x22 -> x0, matrix products: 264 us -> none  [the longest x1 116 us: backward(): jnp.dot(mixed_heads.T, incoming, preferred_element_type=jnp.float32)]
    convert_element_type x3 -> x0, other arithmetic: 258 us -> none  [the longest x2 240 us: on_device(): out_eff = out_q.astype(jnp.bfloat16)]
    pallas_call x0 -> x10, Pallas kernels: none -> 114 us  [the longest x1 50.6 us: on_device(): call(functools.partial(prep_kernel, kv_count), (shaped((local, width), BF...]
    pmax x1 -> x0, blocking collectives: 106 us -> none  [on_device(): value_peak = lax.pmax(jnp.max(jnp.abs(value_rot), axis=0), 'tensor')]
    psum x1 -> x0, waiting for transfers between devices: 68.2 us -> none  [on_device(): rot_grad = lax.psum(partial_rot, 'tensor')]
    all_to_all x0 -> x5, blocking collectives: none -> 65 us  [exchange(): lax.all_to_all(rows, 'tensor', split_axis=0, concat_axis=0, tiled=True)]
    all_gather x2 -> x0, waiting for transfers between devices: 45.9 us -> none  [backward(): lax.all_gather(incoming, 'tensor', axis=1, tiled=True)]
  transfers between devices with their start and end apart: 6 -> 3, of which waited for: 3 -> 2; matrix products, arithmetic and copies ran while one was open for 13% -> 0% of each run, Pallas kernels for 0% -> 7%
where the time goes in v1:
time: 237 us; the launch traced here: 236 us
  Pallas kernels  114 us (48%)
  blocking collectives  97.6 us (41%)
  local copies, waits for them, and re-layouts  8.83 us (4%)
  starting transfers between devices  6.93 us (3%)
  other arithmetic  5.28 us (2%)
  waiting for transfers between devices  3.5 us (1%)
    all_to_all x5, blocking collectives, exchange(): lax.all_to_all(rows, 'tensor', split_axis=0, concat_axis=0, tiled=True)  65 us
    pallas_call x1, Pallas kernels, on_device(): call(functools.partial(prep_kernel, kv_count), (shaped((local, width), BF...  50.6 us
    all_gather x1, blocking collectives, on_device(): stats = lax.all_gather(stat, 'tensor', axis=0, tiled=True)  32.6 us
    pallas_call x1, Pallas kernels, on_device(): call(functools.partial(out_grad_kernel, kv_count), shaped((LANES, LANES),...  16.9 us
    pallas_call x1, Pallas kernels, on_device(): call(functools.partial(forward_kernel, kv_count), (shaped((tokens, width)...  14.3 us
    pallas_call x1, Pallas kernels, on_device(): call(functools.partial(value_quant_kernel, model_width=model_width), (sha...  7.91 us
    pallas_call x1, Pallas kernels, on_device(): call(value_rot_kernel, (shaped((local, tokens), BF16), shaped((local, tok...  5.22 us
    pallas_call x1, Pallas kernels, on_device(): call(functools.partial(value_grad_kernel, kv_count), shaped((tokens, kv_w...  4.85 us
  transfers between devices with their start and end apart: 3, of which 2 were waited for; matrix products, arithmetic and copies ran while one was open for 0% of the time, Pallas kernels for 7%

profile of v1, /device:TPU:0, one launch (start us, length us, event | category | flops | bytes accessed | tf_op | source)
XLA Modules:
  0.0 236.4 jit_solution(15384535876856027350)
XLA Ops:
  0.6 1.7 copy.13.gain_ref
  2.4 4.2 %reshape_squeeze.7.probs_ref = bf16[2,4096,64]{2,1,0:T(8,128)(2,1)} reshape(bf16[1,2,64,4096]{3,2,1,0:T(8,128)(2,1)} %param.13) | data formatting | bytes 2097152 | tf_op jit(solution)/shard_map/reshape;squeeze | solution.py:359
  6.6 5.2 %shard_map.86 = (bf16[1024,128]{1,0:T(8,128)(2,1)}, bf16[1024,128]{1,0:T(8,128)(2,1)}, f32[1024,1024]{1,0:T(8,128)}, f32[1,1152]{1,0:T(1,128)}) custom-call(bf16[128,1024]{1,0:T(8,128)(2,1)} %hidden_ref.1, bf16[128,1024]{1,0:T(8,128)(2,1)} %ct_ref.1, bf16[1024,1024]{1,0:T(8,128)(2,1)} %bitcast.26, f32[128,128]{1,0:T(8,128)} %bitcast.36), custom_call_target="tpu_custom_call" | custom-call | flops 536870912 | bytes 6291456 | tf_op jit(solution)/shard_map/pallas_call | solution.py:364
  11.8 32.6 %all-gather = f32[8,1,1152]{2,1,0:T(1,128)S(1)} all-gather(f32[1,1,1152]{2,1,0:T(1,128)} %bitcast.39), channel_id=1, replica_groups=mesh['groups'=2,'tensor'=8,'section'=2] {'tensor'}, dimensions={0}, use_global_device_ids=true | all-gather | bytes 41472 | tf_op jit(solution)/shard_map/all_gather | solution.py:374
  44.4 0.6 copy.19
  45.0 50.6 %shard_map.88 = (bf16[1024,8192]{1,0:T(8,128)(2,1)}, bf16[1024,8192]{1,0:T(8,128)(2,1)}, f32[1024,1]{1,0:T(8,128)}, bf16[128,8192]{1,0:T(8,128)(2,1)}, bf16[128,1024]{1,0:T(8,128)(2,1)}) custom-call(bf16[1024,8192]{1,0:T(8,128)(2,1)} %bitcast.24, f32[128,128]{1,0:T(8,128)} %bitcast.37, bf16[1024,128]{1,0:T(8,128)(2,1)} %get-tuple-element.25.ct_ref, ...), custom_call_target="tpu_custom_call" | custom-call | flops 6442450944 | bytes 50331648 | tf_op jit(solution)/shard_map/pallas_call | solution.py:385
  95.6 7.9 %shard_map.87 = (bf16[1024,1024]{1,0:T(8,128)(2,1)}, bf16[1024,1024]{1,0:T(8,128)(2,1)}, bf16[128,1024]{1,0:T(8,128)(2,1)}, f32[1,1024]{1,0:T(1,128)}, f32[1,128]{1,0:T(1,128)}) custom-call(f32[1024,1024]{1,0:T(8,128)} %get-tuple-element.22.turned_ref, f32[8,1152]{1,0:T(8,128)} %bitcast.35, bf16[1024,128]{1,0:T(8,128)(2,1)} %get-tuple-element.21.x_ref, ...), custom_call_target="tpu_custom_call" | custom-call | flops 268435456 | bytes 8388608 | tf_op jit(solution)/shard_map/pallas_call | solution.py:411
  103.5 1.0 broadcast_select_fusion
  104.5 13.4 %all_to_all.54 = bf16[8,16,1024]{2,1,0:T(8,128)(2,1)S(1)} all-to-all(bf16[8,16,1024]{2,1,0:T(8,128)(2,1)S(1)} %bitcast.33), channel_id=1, replica_groups=mesh['groups'=2,'tensor'=8,'section'=2] {'tensor'}, dimensions={0} | all-to-all | bytes 524288 | tf_op jit(solution)/shard_map/all_to_all | solution.py:342
  118.0 13.1 %all_to_all.55 = bf16[8,16,1024]{2,1,0:T(8,128)(2,1)} all-to-all(bf16[8,16,1024]{2,1,0:T(8,128)(2,1)S(1)} %tile.10), channel_id=1, replica_groups=mesh['groups'=2,'tensor'=8,'section'=2] {'tensor'}, dimensions={0} | all-to-all | bytes 524288 | tf_op jit(solution)/shard_map/all_to_all | solution.py:342
  131.1 3.2 %shard_map.89 = bf16[1024,128]{1,0:T(8,128)(2,1)} custom-call(bf16[128,1024]{1,0:T(8,128)(2,1)} %bitcast.28, f32[1,1024]{1,0:T(1,128)} %get-tuple-element.28.scale_ref.vscale_ref, bf16[1024,1024]{1,0:T(8,128)(2,1)} %get-tuple-element.31.q_ref, f32[1024,1]{1,0:T(8,128)} %copy.13.gain_ref), custom_call_target="tpu_custom_call" | custom-call | flops 268435456 | bytes 2097152 | tf_op jit(solution)/shard_map/pallas_call | solution.py:431
  134.3 1.3 collective-permute-start
  135.6 2.3 collective-permute-done.grad_ref
  137.9 0.7 copy-done.3
  138.6 14.3 %shard_map.90 = (bf16[128,8192]{1,0:T(8,128)(2,1)}, bf16[1024,128]{1,0:T(8,128)(2,1)}, bf16[128,8192]{1,0:T(8,128)(2,1)}) custom-call(bf16[128,1024]{1,0:T(8,128)(2,1)} %bitcast.29, f32[1,128]{1,0:T(1,128)} %get-tuple-element.27.mean_ref, f32[1,1024]{1,0:T(1,128)} %get-tuple-element.28.scale_ref.vscale_ref, bf16[2,4096,64]{2,1,0:T(8,128)(2,1)} %reshape_squeeze.7.probs_ref, ...), custom_call_target="tpu_custom_call" | custom-call | flops 4294967296 | bytes 16777216 | tf_op jit(solution)/shard_map/pallas_call | solution.py:438
  152.9 2.2 collective-permute-start.1
  155.1 1.2 collective-permute-done.1
  156.3 1.8 broadcast_select_fusion.1
  158.1 3.3 %shard_map.91 = bf16[128,1152]{1,0:T(8,128)(2,1)} custom-call(bf16[1024,128]{1,0:T(8,128)(2,1)} %get-tuple-element.41.x_ref, f32[1024,1]{1,0:T(8,128)} %copy.13.gain_ref, bf16[1024,1024]{1,0:T(8,128)(2,1)} %get-tuple-element.31.q_ref), custom_call_target="tpu_custom_call" | custom-call | flops 268435456 | bytes 2097152 | tf_op jit(solution)/shard_map/pallas_call | solution.py:463
  161.4 13.5 %all_to_all.56 = bf16[8,16,1152]{2,1,0:T(8,128)(2,1)S(1)} all-to-all(bf16[8,16,1152]{2,1,0:T(8,128)(2,1)} %bitcast.31), channel_id=1, replica_groups=mesh['groups'=2,'tensor'=8,'section'=2] {'tensor'}, dimensions={0} | all-to-all | bytes 589824 | tf_op jit(solution)/shard_map/all_to_all | solution.py:342
  175.0 0.6 fusion.1
  175.6 4.9 %shard_map.92 = bf16[128,1024]{1,0:T(8,128)(2,1)} custom-call(f32[1,128]{1,0:T(1,128)} %get-tuple-element.42.mean_ref, bf16[128,8192]{1,0:T(8,128)(2,1)} %get-tuple-element.33.ct_back_ref, bf16[128,8192]{1,0:T(8,128)(2,1)} %get-tuple-element.34.back_ref, bf16[2,4096,64]{2,1,0:T(8,128)(2,1)} %reshape_squeeze.7.probs_ref), custom_call_target="tpu_custom_call" | custom-call | flops 134217728 | bytes 6291456 | tf_op jit(solution)/shard_map/pallas_call | solution.py:471
  180.5 1.0 bitcast_select_fusion.1
  181.5 10.9 %all_to_all.57 = bf16[8,16,1024]{2,1,0:T(8,128)(2,1)S(1)} all-to-all(bf16[8,16,1024]{2,1,0:T(8,128)(2,1)S(1)} %bitcast.32), channel_id=1, replica_groups=mesh['groups'=2,'tensor'=8,'section'=2] {'tensor'}, dimensions={0} | all-to-all | bytes 524288 | tf_op jit(solution)/shard_map/all_to_all | solution.py:342
  192.4 0.7 tile.13
  193.1 3.4 %all-to-all-start.4 = ((bf16[8,16,1024]{2,1,0:T(8,128)(2,1)}), bf16[8,16,1024]{2,1,0:T(8,128)(2,1)S(1)}, u32[]{:S(2)}, u32[]{:S(2)}) async-start(bf16[8,16,1024]{2,1,0:T(8,128)(2,1)} %tile.13), calls=%async_computation.4 | async-start | bytes 524288 | tf_op jit(solution)/shard_map/all_to_all | solution.py:342
  196.6 16.9 %shard_map.93.other_ref = f32[128,128]{1,0:T(8,128)} custom-call(s32[1]{0:T(128)} %bitcast.11.section_ref, bf16[128,1024]{1,0:T(8,128)(2,1)} %bitcast.30, f32[1,128]{1,0:T(1,128)} %get-tuple-element.42.mean_ref, f32[1,1024]{1,0:T(1,128)} %get-tuple-element.28.scale_ref.vscale_ref, bf16[2,4096,64]{2,1,0:T(8,128)(2,1)} %reshape_squeeze.7.probs_ref, ...), custom_call_target="tpu_custom_call" | custom-call | flops 4294967296 | bytes 33554432 | tf_op jit(solution)/shard_map/pallas_call | solution.py:479
  213.5 0.8 bitcast_select_fusion.vg_ref
  214.3 4.6 %shard_map.94 = bf16[128,128]{1,0:T(8,128)(2,1)} custom-call(bf16[1024,128]{1,0:T(8,128)(2,1)} %get-tuple-element.40.x_ref, f32[1,128]{1,0:T(1,128)} %get-tuple-element.43.mean_ref, f32[1024,1]{1,0:T(8,128)} %copy.13.gain_ref, bf16[128,1024]{1,0:T(8,128)(2,1)} %bitcast_select_fusion.vg_ref, bf16[1024,1024]{1,0:T(8,128)(2,1)} %bitcast.27, ...), custom_call_target="tpu_custom_call" | custom-call | flops 536870912 | bytes 4194304 | tf_op jit(solution)/shard_map/pallas_call | solution.py:503
  218.9 0.8 tile.14
  219.7 14.0 %all_to_all.58 = bf16[8,128,128]{2,1,0:T(8,128)(2,1)} all-to-all(bf16[8,128,128]{2,1,0:T(8,128)(2,1)S(1)} %tile.14), channel_id=1, replica_groups=mesh['groups'=2,'tensor'=8,'section'=2] {'tensor'}, dimensions={0} | all-to-all | bytes 524288 | tf_op jit(solution)/shard_map/all_to_all | solution.py:342
  233.7 2.6 %shard_map.95 = (f32[128,128]{1,0:T(8,128)}, f32[128,128]{1,0:T(8,128)}) custom-call(bf16[1024,128]{1,0:T(8,128)(2,1)} %bitcast.34, f32[128,128]{1,0:T(8,128)} %bitcast.38), custom_call_target="tpu_custom_call" | custom-call | flops 125829120 | bytes 131072 | tf_op jit(solution)/shard_map/pallas_call | solution.py:516
  (17 shorter events, 0.2 us)
Async XLA Ops:
  95.6 7.9 %copy-start.4 = (bf16[128,1024]{1,0:T(8,128)(2,1)S(1)}, bf16[128,1024]{1,0:T(8,128)(2,1)}, u32[]{:S(2)}) copy-start(bf16[128,1024]{1,0:T(8,128)(2,1)} %get-tuple-element.26) | copy-start | bytes 786436
  134.3 3.6 %collective-permute-start = (bf16[1024,128]{1,0:T(8,128)(2,1)}, bf16[1024,128]{1,0:T(8,128)(2,1)S(1)}, u32[]{:S(2)}, u32[]{:S(2)}) collective-permute-start(bf16[1024,128]{1,0:T(8,128)(2,1)} %shard_map.89), channel_id=1, source_target_pairs={{1,0},{3,2},{5,4},{7,6},{9,8},{11,10},{13,12},{15,14},{17,16},{19,... | collective-permute-start | bytes 786440 | tf_op jit(solution)/shard_map/ppermute | solution.py:436
  137.9 0.7 copy-start.3
  138.6 17.7 %copy-start.1 = (bf16[1024,128]{1,0:T(8,128)(2,1)S(1)}, bf16[1024,128]{1,0:T(8,128)(2,1)}, u32[]{:S(2)}) copy-start(bf16[1024,128]{1,0:T(8,128)(2,1)} %get-tuple-element.21.x_ref) | copy-start | bytes 786436
  152.9 3.4 %collective-permute-start.1 = (bf16[1024,128]{1,0:T(8,128)(2,1)}, bf16[1024,128]{1,0:T(8,128)(2,1)S(1)}, u32[]{:S(2)}, u32[]{:S(2)}) collective-permute-start(bf16[1024,128]{1,0:T(8,128)(2,1)} %get-tuple-element.32), channel_id=1, source_target_pairs={{0,1},{2,3},{4,5},{6,7},{8,9},{10,11},{12,13},{14,15},{16,17},{18,... | collective-permute-start | bytes 786440 | tf_op jit(solution)/shard_map/ppermute | solution.py:460
  158.1 16.9 %copy-start.5 = (f32[1,128]{1,0:T(1,128)S(1)}, f32[1,128]{1,0:T(1,128)}, u32[]{:S(2)}) copy-start(f32[1,128]{1,0:T(1,128)} %get-tuple-element.27.mean_ref) | copy-start | bytes 1540
  192.3 4.2 %copy-start.2 = (bf16[8,16,1024]{2,1,0:T(8,128)(2,1)}, bf16[8,16,1024]{2,1,0:T(8,128)(2,1)S(1)}, u32[]{:S(2)}) copy-start(bf16[8,16,1024]{2,1,0:T(8,128)(2,1)S(1)} %all_to_all.57) | copy-start | bytes 786436
  193.1 20.3 %all-to-all-start.4 = ((bf16[8,16,1024]{2,1,0:T(8,128)(2,1)}), bf16[8,16,1024]{2,1,0:T(8,128)(2,1)S(1)}, u32[]{:S(2)}, u32[]{:S(2)}) async-start(bf16[8,16,1024]{2,1,0:T(8,128)(2,1)} %tile.13), calls=%async_computation.4 | async-start | bytes 524288 | tf_op jit(solution)/shard_map/all_to_all | solution.py:342
  196.6 16.9 %copy-start = (bf16[8,16,1024]{2,1,0:T(8,128)(2,1)S(1)}, bf16[8,16,1024]{2,1,0:T(8,128)(2,1)}, u32[]{:S(2)}) copy-start(bf16[8,16,1024]{2,1,0:T(8,128)(2,1)} %all_to_all.55) | copy-start | bytes 786436

commit v2 on v1

v2 whole, which is shorter than its diff:
```python
import functools

import jax
import jax.numpy as jnp
from jax import lax
from jax.experimental import pallas as pl
from jax.experimental.pallas import tpu as pltpu
from jax.sharding import PartitionSpec as P

quant_levels = 7.0
norm_eps = 1e-05
scale_eps = 1e-06
step_size = 0.1
precise = lax.Precision.HIGHEST
F32 = jnp.float32
BF16 = jnp.bfloat16
LANES = 128
VMEM_BYTES = 56 * 1024 * 1024

sin_coefs = (3.141582078119497, -5.16714420271071, 2.541908924984016, -0.5546570710297597)
sin_top = sin_coefs[3]
slope_factor = 2.0 * sin_top * sin_top
unit = 1.000002 / (sin_top * sin_top)


def dot_nn(a, b):
    return lax.dot_general(a, b, (((1,), (0,)), ((), ())), preferred_element_type=F32)


def dot_nt(a, b):
    return lax.dot_general(a, b, (((1,), (1,)), ((), ())), preferred_element_type=F32)


def dot_tn(a, b):
    return lax.dot_general(a, b, (((0,), (0,)), ((), ())), preferred_element_type=F32)


def sine_scale(scale):
    return scale * (-sin_top * sin_top / 3.141592653589793)


def soft_parts(turned, inverse, factor):
    ratio = turned * inverse
    rest = ratio - jnp.round(ratio)
    square = rest * rest
    sine = rest * (
        ((square + sin_coefs[2] / sin_top) * square + sin_coefs[1] / sin_top) * square
        + sin_coefs[0] / sin_top
    )
    slope = sine * sine
    below = unit - slope
    return turned - (sine * (below * lax.rsqrt(below))) * factor, slope


def rotation_pair(rot):
    high = rot.astype(BF16)
    low = (rot - high.astype(F32)).astype(BF16)
    zero = jnp.zeros_like(high)

    def blocks(part):
        return jnp.concatenate(
            [jnp.concatenate([part, zero], 1), jnp.concatenate([zero, part], 1)], 0
        )

    return blocks(high), blocks(low)


def column_of(row):
    count = row.shape[1]
    return jnp.transpose(jnp.broadcast_to(row, (count, count)))


def call(kernel, out_shape, cost, **kw):
    flops, moved = cost
    return pl.pallas_call(
        kernel,
        out_shape=out_shape,
        compiler_params=pltpu.CompilerParams(vmem_limit_bytes=VMEM_BYTES),
        cost_estimate=pl.CostEstimate(flops=flops, bytes_accessed=moved, transcendentals=0),
        **kw,
    )


def shaped(shape, dtype):
    return jax.ShapeDtypeStruct(shape, dtype)


def value_rot_kernel(
    hidden_ref, ct_ref, gain_row_ref, value_ref, rot_ref, x_ref, ct_t_ref, gain_ref, vrot_ref, stat_ref
):
    kv_width = value_ref.shape[1]
    high, low = rotation_pair(rot_ref[...])

    @pl.when(pl.program_id(0) == 0)
    def _():
        stat_ref[...] = jnp.zeros_like(stat_ref)

    for at in range(0, kv_width, 2 * LANES):
        cols = slice(at, at + 2 * LANES)
        block = value_ref[:, cols]
        turned = dot_nn(block, high) + dot_nn(block, low)
        vrot_ref[:, cols] = turned
        peak = jnp.max(jnp.abs(turned), axis=0, keepdims=True)
        stat_ref[:, cols] = jnp.maximum(stat_ref[:, cols], peak)
    x = jnp.transpose(hidden_ref[...].astype(F32))
    x_ref[...] = x.astype(BF16)
    stat_ref[:, kv_width:] += jnp.sum(x * x, axis=0, keepdims=True)
    ct_t_ref[...] = jnp.transpose(ct_ref[...].astype(F32)).astype(BF16)
    gain_ref[...] = jnp.transpose(jnp.broadcast_to(gain_row_ref[...], hidden_ref.shape))


def mix_back(probs_ref, grad_of, out_ref, seq, per_group, kv_count):
    blocks = probs_ref.shape[0]
    for b in range(blocks):
        rows = slice(b * seq, (b + 1) * seq)
        for k in range(kv_count):
            stacked = jnp.concatenate(
                [
                    grad_of(rows, slice(h * LANES, (h + 1) * LANES))
                    for h in range(k * per_group, (k + 1) * per_group)
                ],
                0,
            )
            probs = probs_ref[b, k * per_group * seq : (k + 1) * per_group * seq, :]
            out_ref[rows, k * LANES : (k + 1) * LANES] = dot_tn(probs, stacked).astype(
                out_ref.dtype
            )


def mix_forward(probs_ref, values_of, mixed_ref, seq, per_group, kv_count):
    blocks = probs_ref.shape[0]
    for b in range(blocks):
        rows = slice(b * seq, (b + 1) * seq)
        for k in range(kv_count):
            probs = probs_ref[b, k * per_group * seq : (k + 1) * per_group * seq, :]
            heads = dot_nn(probs, values_of(rows, slice(k * LANES, (k + 1) * LANES))).astype(BF16)
            for j in range(per_group):
                h = k * per_group + j
                mixed_ref[rows, h * LANES : (h + 1) * LANES] = heads[j * seq : (j + 1) * seq]


def prep_kernel(kv_count, starts, ends, number, *refs):
    refs = list(refs)
    w_ref, rot_ref, ct_ref = refs[:3]
    del refs[:3]
    if ends:
        probs_ref = refs.pop(0)
    if not starts:
        held_ref = refs[1]
        del refs[:4]
    q_ref, slope_ref = refs[:2]
    del refs[:2]
    if ends:
        back_ref, vg_ref = refs[:2]
        del refs[:2]
    total_ref, turned_ref, inv_ref, factor_ref = refs
    rows, width = w_ref.shape
    step, last = pl.program_id(0), number - 1
    lines = 16
    wide = min(1024, width)

    @pl.when(step == 0)
    def _():
        total_ref[...] = jnp.zeros_like(total_ref) if starts else held_ref[...]

    high, low = rotation_pair(rot_ref[...])
    peak = jnp.zeros((rows, LANES), F32)
    for at in range(0, width, 2 * LANES):
        cols = slice(at, at + 2 * LANES)
        block = w_ref[:, cols]
        turned = dot_nn(block, high) + dot_nn(block, low)
        turned_ref[:, cols] = turned
        size = jnp.abs(turned)
        peak = jnp.maximum(peak, jnp.maximum(size[:, :LANES], size[:, LANES:]))
    scale = (jnp.max(peak, axis=1, keepdims=True) + scale_eps) / quant_levels
    inv_ref[...] = jnp.broadcast_to(1.0 / scale, inv_ref.shape)
    factor_ref[...] = jnp.broadcast_to(sine_scale(scale), inv_ref.shape)

    @pl.loop(0, rows // lines, unroll=2)
    def _(i):
        here = pl.ds(pl.multiple_of(i * lines, lines), lines)
        inverse, factor = inv_ref[here, :], factor_ref[here, :]
        for at in range(0, width, LANES):
            cols = slice(at, at + LANES)
            effective, slope = soft_parts(turned_ref[here, cols], inverse, factor)
            q_ref[here, cols] = effective.astype(BF16)
            slope_ref[here, cols] = slope.astype(BF16)

    for at in range(0, width, wide):
        cols = slice(at, at + wide)
        total_ref[:, cols] += dot_tn(ct_ref[...], q_ref[:, cols])

    if ends:

        @pl.when(step == last)
        def _():
            back_ref[...] = total_ref[...].astype(BF16)
            seq = probs_ref.shape[2]
            per_group = width // LANES // kv_count
            mix_back(probs_ref, lambda r, c: back_ref[r, c], vg_ref, seq, per_group, kv_count)


def value_quant_kernel(
    model_width, turned_ref, stats_ref, x_ref, gain_ref, q_ref, slope_ref, part_ref, mean_ref, total_ref
):
    kv_width = turned_ref.shape[1]
    stats = stats_ref[...]
    scale = (jnp.max(stats[:, :kv_width], axis=0, keepdims=True) + scale_eps) / quant_levels
    squares = jnp.sum(stats[:, kv_width:], axis=0, keepdims=True)
    mean = lax.rsqrt(squares / model_width + norm_eps)
    inverse = 1.0 / scale
    factor = sine_scale(scale)
    lines = 16
    inverses = [
        jnp.broadcast_to(inverse[:, at : at + LANES], (lines, LANES))
        for at in range(0, kv_width, LANES)
    ]

    @pl.loop(0, turned_ref.shape[0] // lines)
    def _(i):
        here = pl.ds(pl.multiple_of(i * lines, lines), lines)
        for j, wide in enumerate(inverses):
            cols = slice(j * LANES, (j + 1) * LANES)
            effective, slope = soft_parts(turned_ref[here, cols], wide, factor[:, cols])
            q_ref[here, cols] = effective.astype(BF16)
            slope_ref[here, cols] = slope.astype(BF16)

    @pl.when(pl.program_id(0) == 0)
    def _():
        mean_ref[...] = mean
        total_ref[...] = jnp.zeros_like(total_ref)

    normed = (x_ref[...].astype(F32) * mean * gain_ref[...]).astype(BF16)
    total_ref[...] += dot_tn(normed, q_ref[...])

    @pl.when(pl.program_id(0) == pl.num_programs(0) - 1)
    def _():
        part_ref[...] = total_ref[...].astype(BF16)


def input_grad_kernel(vg_ref, q_ref, gain_ref, out_ref):
    out_ref[...] = (dot_nt(q_ref[...], vg_ref[...]) * gain_ref[...]).astype(BF16)


def forward_kernel(kv_count, values_ref, probs_ref, q_ref, x_ref, mixed_ref, out_ref):
    @pl.when(pl.program_id(0) == 0)
    def _():
        seq = probs_ref.shape[2]
        per_group = q_ref.shape[1] // LANES // kv_count
        mix_forward(probs_ref, lambda r, c: values_ref[r, c], mixed_ref, seq, per_group, kv_count)

    out_ref[...] = (x_ref[...].astype(F32) + dot_nt(q_ref[...], mixed_ref[...])).astype(BF16)


def back_kernel(q_ref, grad_ref, back_ref, total_ref):
    width = q_ref.shape[1]

    @pl.when(pl.program_id(0) == 0)
    def _():
        total_ref[...] = jnp.zeros_like(total_ref)

    wide = min(1024, width)
    for at in range(0, width, wide):
        cols = slice(at, at + wide)
        total_ref[:, cols] += dot_tn(grad_ref[...], q_ref[:, cols])

    @pl.when(pl.program_id(0) == pl.num_programs(0) - 1)
    def _():
        back_ref[...] = total_ref[...].astype(BF16)


def project_kernel(x_ref, gain_ref, q_ref, out_ref):
    kv_width = q_ref.shape[1]
    x = x_ref[...].astype(F32)
    gained = (x * gain_ref[...]).astype(BF16)
    out_ref[:, :kv_width] = dot_tn(gained, q_ref[...]).astype(BF16)
    squares = jnp.sum(x * x, axis=0, keepdims=True)
    tokens = squares.shape[1]
    out_ref[:, kv_width:] = jnp.broadcast_to(squares, (tokens, tokens)).astype(BF16)


def value_grad_kernel(kv_count, mean_ref, ct_back_ref, back_ref, probs_ref, out_ref):
    inverse = column_of(mean_ref[...])[:, :1]
    seq = probs_ref.shape[2]
    per_group = back_ref.shape[1] // LANES // kv_count

    def grad_of(rows, cols):
        return (
            ct_back_ref[rows, cols].astype(F32) + inverse[rows] * back_ref[rows, cols].astype(F32)
        ).astype(BF16)

    mix_back(probs_ref, grad_of, out_ref, seq, per_group, kv_count)


def out_grad_kernel(
    kv_count, section_ref, values_ref, mean_ref, probs_ref, mixed_in_ref,
    ct_ref, grad_ref, w_ref, slope_ref, out_ref, mixed_ref, total_ref,
):
    width = w_ref.shape[1]
    seq = probs_ref.shape[2]
    per_group = width // LANES // kv_count
    last_section = section_ref[0] != 0

    @pl.when(pl.program_id(0) == 0)
    def _():
        total_ref[...] = jnp.zeros_like(total_ref)

        @pl.when(last_section)
        def _():
            mix_forward(
                probs_ref, lambda r, c: values_ref[r, c], mixed_ref, seq, per_group, kv_count
            )

        @pl.when(jnp.logical_not(last_section))
        def _():
            mixed_ref[...] = mixed_in_ref[...]

    keep = jnp.where(last_section, 0.0, 1.0)
    grad = (
        ct_ref[...].astype(F32) + (keep * mean_ref[...]) * grad_ref[...].astype(F32)
    ).astype(BF16)
    for at in range(0, width, 2 * LANES):
        cols = slice(at, at + 2 * LANES)
        out_grad = dot_nn(grad, mixed_ref[:, cols])
        sloped = (out_grad * slope_ref[:, cols].astype(F32)).astype(BF16)
        total_ref[...] += dot_tn(w_ref[:, cols], sloped)

    @pl.when(pl.program_id(0) == pl.num_programs(0) - 1)
    def _():
        out_ref[...] = total_ref[:LANES, :LANES] + total_ref[LANES:, LANES:]


def value_part_kernel(x_ref, mean_ref, gain_ref, vg_ref, v_ref, slope_ref, other_ref, out_ref):
    normed = (x_ref[...].astype(F32) * mean_ref[...] * gain_ref[...]).astype(BF16)
    total = other_ref[...]
    for at in range(0, v_ref.shape[1], 2 * LANES):
        cols = slice(at, at + 2 * LANES)
        grad = dot_nn(normed, vg_ref[:, cols])
        sloped = (grad * slope_ref[:, cols].astype(F32)).astype(BF16)
        both = dot_tn(v_ref[:, cols], sloped)
        total = total + both[:LANES, :LANES] + both[LANES:, LANES:]
    out_ref[...] = (slope_factor * total).astype(out_ref.dtype)


def cayley_kernel(parts_ref, rot_ref, grad_ref, new_ref):
    count = parts_ref.shape[0] // LANES
    grad = parts_ref[:LANES].astype(F32)
    for i in range(1, count):
        grad = grad + parts_ref[i * LANES : (i + 1) * LANES].astype(F32)
    grad_ref[...] = grad
    rot = rot_ref[...]

    def product(a, b, dims=(1, 0)):
        return lax.dot_general(
            a, b, (((dims[0],), (dims[1],)), ((), ())), precision=precise, preferred_element_type=F32
        )

    turn = product(grad, rot, (1, 1))
    skew = turn - jnp.transpose(turn)
    update = rot - step_size * product(skew, rot)
    for _ in range(2):
        update = rot - 0.5 * step_size * product(skew, rot + update)
    new_ref[...] = update


def exchange(rows):
    return lax.all_to_all(rows, "tensor", split_axis=0, concat_axis=0, tiled=True)


def on_device(hidden, cotangent, norm_gain, value_weight, output_weight, rotation, attention):
    section = lax.axis_index("section")
    count = lax.axis_size("tensor")
    is_first = section == 0
    flag = section.astype(jnp.int32).reshape(1)
    rot = rotation[0]
    value_w = value_weight[0]
    out_w = output_weight[0]
    local, width = out_w.shape
    kv_width = value_w.shape[1]
    kv_count = kv_width // LANES
    tokens = hidden.shape[0]
    _, blocks, heads, flat = attention.shape
    seq = tokens // blocks
    probs = attention[0].reshape(blocks, heads * seq, seq)
    model_width = local * count
    big = 2 * tokens * local * width

    def split(rows, *tail):
        return pl.BlockSpec((rows,) + tail, lambda i: (i, 0))

    def across(lines, rows):
        return pl.BlockSpec((lines, rows), lambda i: (0, i))

    def whole(*shape):
        return pl.BlockSpec(shape, lambda i: (0,) * len(shape))

    rows = min(local, 256)
    x0, ct, gain, value_rot, stat = call(
        value_rot_kernel,
        (
            shaped((local, tokens), BF16),
            shaped((local, tokens), BF16),
            shaped((local, tokens), F32),
            shaped((local, kv_width), F32),
            shaped((1, kv_width + tokens), F32),
        ),
        (4 * local * kv_width * LANES, 6 * local * kv_width),
        grid=(local // rows,),
        in_specs=[
            across(tokens, rows),
            across(tokens, rows),
            across(1, rows),
            split(rows, kv_width),
            whole(LANES, LANES),
        ],
        out_specs=(
            split(rows, tokens),
            split(rows, tokens),
            split(rows, tokens),
            split(rows, kv_width),
            whole(1, kv_width + tokens),
        ),
    )(hidden, cotangent, norm_gain, value_w, rot)
    stats = exchange(jnp.tile(stat, (count, 1)))

    part_rows = min(local, 128)
    part_count = local // part_rows

    def prepare(first, number, before):
        starts, ends = first == 0, first + number == part_count

        def ahead(lines, *tail):
            return pl.BlockSpec((lines,) + tail, lambda i: (first + i, 0))

        def behind(lines, *tail):
            return pl.BlockSpec((lines,) + tail, lambda i: (first + i, 0))

        anywhere = pl.BlockSpec(memory_space=pl.ANY)
        operands = [out_w, rot, ct]
        in_specs = [ahead(part_rows, width), whole(LANES, LANES), behind(part_rows, tokens)]
        if ends:
            operands.append(probs)
            in_specs.append(whole(*probs.shape))
        aliases = {}
        if not starts:
            quant, slope, held, after = before
            at = len(operands)
            operands += [after, held, quant, slope]
            in_specs += [anywhere, whole(tokens, width), anywhere, anywhere]
            aliases = {at + 2: 0, at + 3: 1}
        outs = [shaped((local, width), BF16), shaped((local, width), BF16)]
        out_specs = [behind(part_rows, width), behind(part_rows, width)]
        scratch = []
        if ends:
            outs += [shaped((tokens, width), BF16), shaped((tokens, kv_width), BF16)]
            out_specs += [whole(tokens, width), whole(tokens, kv_width)]
            scratch.append(pltpu.VMEM((tokens, width), F32))
        else:
            outs.append(shaped((tokens, width), F32))
            out_specs.append(whole(tokens, width))
        scratch += [
            pltpu.VMEM((part_rows, width), F32),
            pltpu.VMEM((part_rows, LANES), F32),
            pltpu.VMEM((part_rows, LANES), F32),
        ]
        return call(
            functools.partial(prep_kernel, kv_count, starts, ends, number),
            tuple(outs),
            (40 * big * number // part_count, 6 * local * width * number // part_count),
            grid=(number,),
            in_specs=in_specs,
            out_specs=tuple(out_specs),
            scratch_shapes=scratch,
            input_output_aliases=aliases,
        )(*operands)

    lead = part_count // 4
    before = prepare(0, lead, None) if lead else None

    value_q, value_slope, value_part, mean0 = call(
        functools.partial(value_quant_kernel, model_width),
        (
            shaped((local, kv_width), BF16),
            shaped((local, kv_width), BF16),
            shaped((tokens, kv_width), BF16),
            shaped((1, tokens), F32),
        ),
        (2 * local * kv_width * tokens, 8 * local * kv_width),
        grid=(local // rows,),
        in_specs=[
            split(rows, kv_width),
            whole(count, kv_width + tokens),
            split(rows, tokens),
            split(rows, tokens),
        ],
        out_specs=(
            split(rows, kv_width),
            split(rows, kv_width),
            whole(tokens, kv_width),
            whole(1, tokens),
        ),
        scratch_shapes=[pltpu.VMEM((tokens, kv_width), F32)],
    )(value_rot, stats, x0, gain)

    def add_parts(received):
        return received.reshape(count, tokens // count, -1).astype(F32).sum(0)

    def spread(part):
        return jnp.tile(part.astype(BF16), (count, 1))

    values0 = spread(add_parts(exchange(value_part)))
    if lead:
        before = tuple(before) + (value_part,)
    quant, slope, ct_back, ct_vg = prepare(lead, part_count - lead, before)

    second = exchange(jnp.where(is_first, values0, ct_vg))
    vg1 = exchange(spread(add_parts(second)))

    mixed, x1 = call(
        functools.partial(forward_kernel, kv_count),
        (shaped((tokens, width), BF16), shaped((local, tokens), BF16)),
        (big, 2 * local * width),
        grid=(local // rows,),
        in_specs=[
            whole(tokens, kv_width),
            whole(*probs.shape),
            split(rows, width),
            split(rows, tokens),
        ],
        out_specs=(whole(tokens, width), split(rows, tokens)),
    )(second, probs, quant, x0)
    arrived = lax.ppermute(x1, "section", [(0, 1)])
    x1 = jnp.where(is_first, x1, arrived)

    projected = call(
        project_kernel,
        shaped((tokens, kv_width + tokens), BF16),
        (2 * local * kv_width * tokens, 2 * local * kv_width),
    )(x1, gain, value_q)
    received = add_parts(exchange(projected))
    mean1 = lax.rsqrt(received[:1, kv_width:] / model_width + norm_eps)

    grad1 = call(
        input_grad_kernel,
        shaped((local, tokens), BF16),
        (2 * local * kv_width * tokens, 2 * local * kv_width),
    )(vg1, value_q, gain)
    grad1 = lax.ppermute(grad1, "section", [(1, 0)])
    grad_back = call(
        back_kernel,
        shaped((tokens, width), BF16),
        (big, 2 * local * width),
        grid=(local // rows,),
        in_specs=[split(rows, width), split(rows, tokens)],
        out_specs=whole(tokens, width),
        scratch_shapes=[pltpu.VMEM((tokens, width), F32)],
    )(quant, grad1)

    vg0 = call(
        functools.partial(value_grad_kernel, kv_count),
        shaped((tokens, kv_width), BF16),
        (2 * tokens * width * seq, 6 * tokens * width),
    )(mean1, ct_back, grad_back, probs)
    mine = lax.axis_index("tensor") * (tokens // count)
    own_mean = lax.dynamic_slice(mean1[0], (mine,), (tokens // count,))[:, None]
    values1 = exchange(jnp.where(is_first, vg0, spread(received[:, :kv_width] * own_mean)))
    vg0 = exchange(spread(add_parts(values1)))

    out_part = call(
        functools.partial(out_grad_kernel, kv_count),
        shaped((LANES, LANES), F32),
        (2 * big, 4 * local * width),
        grid=(local // rows,),
        in_specs=[
            pl.BlockSpec(memory_space=pltpu.SMEM),
            whole(tokens, kv_width),
            whole(1, tokens),
            whole(*probs.shape),
            whole(tokens, width),
            split(rows, tokens),
            split(rows, tokens),
            split(rows, width),
            split(rows, width),
        ],
        out_specs=whole(LANES, LANES),
        scratch_shapes=[
            pltpu.VMEM((tokens, width), BF16),
            pltpu.VMEM((2 * LANES, 2 * LANES), F32),
        ],
    )(flag, values1, mean1, probs, mixed, ct, grad1, out_w, slope)

    rot_part = call(
        value_part_kernel,
        shaped((LANES, LANES), BF16),
        (4 * local * kv_width * tokens, 4 * local * kv_width),
    )(
        jnp.where(is_first, x0, x1),
        jnp.where(is_first, mean0, mean1),
        gain,
        jnp.where(is_first, vg0, vg1),
        value_w,
        value_slope,
        out_part,
    )
    rot_grad, rot_new = call(
        cayley_kernel,
        (shaped((LANES, LANES), F32), shaped((LANES, LANES), F32)),
        (12 * 5 * LANES**3, 8 * LANES**2),
    )(exchange(jnp.tile(rot_part, (count, 1))), rot)
    return rot_grad[None], rot_new[None]


def solution(mesh):
    in_specs = (
        P("groups", "tensor"),
        P("groups", "tensor"),
        P("section", "tensor"),
        P("section", "tensor", None),
        P("section", "tensor", None),
        P("section", None, None),
        P("section", "groups", None, None),
    )
    out_specs = (P("section", "groups", None), P("section", "groups", None))
    return jax.shard_map(
        on_device, mesh=mesh, in_specs=in_specs, out_specs=out_specs, check_vma=False
    )
```

time: 237 us -> 210 us (0.89)
  blocking collectives: 97.6 us -> 43.2 us
  starting transfers between devices: 6.93 us -> 26.5 us
  Pallas kernels: 114 us -> 119 us
  waiting for transfers between devices: 3.5 us -> 5.97 us
    all_gather x1 -> x0, blocking collectives: 32.6 us -> none  [on_device(): stats = lax.all_gather(stat, 'tensor', axis=0, tiled=True)]
    all_to_all x5 -> x3, blocking collectives: 65 us -> 43.2 us  [exchange(): lax.all_to_all(rows, 'tensor', split_axis=0, concat_axis=0, tiled=True)]
    all_to_all x1 -> x5, starting transfers between devices: 3.41 us -> 23.9 us  [exchange(): lax.all_to_all(rows, 'tensor', split_axis=0, concat_axis=0, tiled=True)]
    pallas_call x2 -> x4, Pallas kernels: 58.5 us -> 67.5 us  [the longest x2 50.6 us: prepare(): call(functools.partial(prep_kernel, kv_count, starts, ends, number), tupl...]
    all_to_all x1 -> x5, waiting for transfers between devices: 0.01 us -> 3.64 us  [exchange(): lax.all_to_all(rows, 'tensor', split_axis=0, concat_axis=0, tiled=True)]
    pallas_call x1, Pallas kernels: 14.3 us -> 10.8 us  [on_device(): call(functools.partial(forward_kernel, kv_count), (shaped((tokens, width)...]
  transfers between devices with their start and end apart: 3 -> 7, of which waited for: 2 -> 2; matrix products, arithmetic and copies ran while one was open for 0% -> 3% of each run, Pallas kernels for 7% -> 40%
where the time goes in v2:
time: 210 us; the launch traced here: 208 us
  Pallas kernels  119 us (57%)
  blocking collectives  43.2 us (21%)
  starting transfers between devices  26.5 us (13%)
  local copies, waits for them, and re-layouts  7.99 us (4%)
  waiting for transfers between devices  5.97 us (3%)
  other arithmetic  5.16 us (2%)
    pallas_call x2, Pallas kernels, prepare(): call(functools.partial(prep_kernel, kv_count, starts, ends, number), tupl...  50.6 us
    all_to_all x3, blocking collectives, exchange(): lax.all_to_all(rows, 'tensor', split_axis=0, concat_axis=0, tiled=True)  43.2 us
    all_to_all x5, starting transfers between devices, exchange(): lax.all_to_all(rows, 'tensor', split_axis=0, concat_axis=0, tiled=True)  23.9 us
    pallas_call x1, Pallas kernels, on_device(): call(functools.partial(out_grad_kernel, kv_count), shaped((LANES, LANES),...  16.9 us
    pallas_call x1, Pallas kernels, on_device(): call(functools.partial(forward_kernel, kv_count), (shaped((tokens, width)...  10.8 us
    pallas_call x1, Pallas kernels, on_device(): call(back_kernel, shaped((tokens, width), BF16), (big, 2 * local * width)...  9.12 us
    pallas_call x1, Pallas kernels, on_device(): call(functools.partial(value_quant_kernel, model_width), (shaped((local,...  7.71 us
    pallas_call x1, Pallas kernels, on_device(): call(value_rot_kernel, (shaped((local, tokens), BF16), shaped((local, tok...  5.33 us
  transfers between devices with their start and end apart: 7, of which 2 were waited for; matrix products, arithmetic and copies ran while one was open for 3% of the time, Pallas kernels for 40%

profile of v2, /device:TPU:0, one launch (start us, length us, event | category | flops | bytes accessed | tf_op | source)
XLA Modules:
  0.0 208.4 jit_solution(14480651458702688029)
XLA Ops:
  0.6 5.3 %shard_map.86 = (bf16[1024,128]{1,0:T(8,128)(2,1)}, bf16[1024,128]{1,0:T(8,128)(2,1)}, f32[1024,128]{1,0:T(8,128)}, f32[1024,1024]{1,0:T(8,128)}, f32[1,1152]{1,0:T(1,128)}) custom-call(bf16[128,1024]{1,0:T(8,128)(2,1)} %hidden_ref.1, bf16[128,1024]{1,0:T(8,128)(2,1)} %ct_ref.1, f32[1,1024]{1,0:T(1,128)} %gain_row_ref.1, bf16[1024,1024]{1,0:T(8,128)(2,1)} %bitcast.31, ...), custom_call_target="tpu_custom_call" | custom-call | flops 536870912 | bytes 6291456 | tf_op jit(solution)/shard_map/pallas_call | solution.py:398
  6.0 0.7 reduce.6
  7.3 7.3 %all-to-all-start = ((f32[8,1,1152]{2,1,0:T(1,128)}), f32[8,1,1152]{2,1,0:T(1,128)S(1)}, u32[]{:S(2)}, u32[]{:S(2)}) async-start(f32[8,1,1152]{2,1,0:T(1,128)} %tile.16), calls=%async_computation | async-start | bytes 73728 | tf_op jit(solution)/shard_map/all_to_all | solution.py:367
  14.6 14.6 %shard_map.88 = (bf16[1024,8192]{1,0:T(8,128)(2,1)}, bf16[1024,8192]{1,0:T(8,128)(2,1)}, f32[128,8192]{1,0:T(8,128)}) custom-call(bf16[1024,8192]{1,0:T(8,128)(2,1)} %bitcast.28, f32[128,128]{1,0:T(8,128)} %bitcast.43, bf16[1024,128]{1,0:T(8,128)(2,1)} %get-tuple-element.27.refs_2_.ct_ref), custom_call_target="tpu_custom_call" | custom-call | flops 21474836480 | bytes 12582912 | tf_op jit(solution)/shard_map/pallas_call | solution.py:466
  29.2 3.2 %reshape_squeeze.3.refs_3_.probs_ref = bf16[2,4096,64]{2,1,0:T(8,128)(2,1)} reshape(bf16[1,2,64,4096]{3,2,1,0:T(8,128)(2,1)S(1)} %copy-done.6) | data formatting | bytes 2097152 | tf_op jit(solution)/shard_map/reshape;squeeze | solution.py:384
  33.0 7.7 %shard_map.87 = (bf16[1024,1024]{1,0:T(8,128)(2,1)}, bf16[1024,1024]{1,0:T(8,128)(2,1)}, bf16[128,1024]{1,0:T(8,128)(2,1)}, f32[1,128]{1,0:T(1,128)}) custom-call(f32[1024,1024]{1,0:T(8,128)} %get-tuple-element.23.turned_ref, f32[8,1152]{1,0:T(8,128)} %bitcast.41, bf16[1024,128]{1,0:T(8,128)(2,1)} %get-tuple-element.22.x_ref, ...), custom_call_target="tpu_custom_call" | custom-call | flops 268435456 | bytes 8388608 | tf_op jit(solution)/shard_map/pallas_call | solution.py:480
  40.7 6.0 %all-to-all-start.1 = ((bf16[8,16,1024]{2,1,0:T(8,128)(2,1)}), bf16[8,16,1024]{2,1,0:T(8,128)(2,1)S(1)}, u32[]{:S(2)}, u32[]{:S(2)}) async-start(bf16[8,16,1024]{2,1,0:T(8,128)(2,1)} %bitcast.39), calls=%async_computation.1 | async-start | bytes 524288 | tf_op jit(solution)/shard_map/all_to_all | solution.py:367
  46.7 36.0 %shard_map.89 = (bf16[1024,8192]{1,0:T(8,128)(2,1)}, bf16[1024,8192]{1,0:T(8,128)(2,1)}, bf16[128,8192]{1,0:T(8,128)(2,1)}, bf16[128,1024]{1,0:T(8,128)(2,1)}) custom-call(bf16[1024,8192]{1,0:T(8,128)(2,1)} %bitcast.29, f32[128,128]{1,0:T(8,128)} %bitcast.44, ...), custom_call_target="tpu_custom_call", output_to_operand_aliasing={{0}: (6, {}), {1}: (7, {})} | custom-call | flops 64424509440 | bytes 37748736 | tf_op jit(solution)/shard_map/pallas_call | solution.py:466
  82.9 14.6 %all_to_all.73 = bf16[8,16,1024]{2,1,0:T(8,128)(2,1)} all-to-all(bf16[8,16,1024]{2,1,0:T(8,128)(2,1)S(1)} %bitcast.37), channel_id=1, replica_groups=mesh['groups'=2,'tensor'=8,'section'=2] {'tensor'}, dimensions={0} | all-to-all | bytes 524288 | tf_op jit(solution)/shard_map/all_to_all | solution.py:367
  97.5 10.8 %shard_map.90 = (bf16[128,8192]{1,0:T(8,128)(2,1)}, bf16[1024,128]{1,0:T(8,128)(2,1)}) custom-call(bf16[128,1024]{1,0:T(8,128)(2,1)} %bitcast.34, bf16[2,4096,64]{2,1,0:T(8,128)(2,1)} %reshape_squeeze.3.refs_3_.probs_ref, bf16[1024,8192]{1,0:T(8,128)(2,1)} %get-tuple-element.32.q_ref, bf16[1024,128]{1,0:T(8,128)(2,1)} %get-tuple-element.22.x_ref), custom_call_target="tpu_custom_call" | custom-call | flops 2147483648 | bytes 16777216 | tf_op jit(solution)/shard_map/pallas_call | solution.py:519
  108.3 1.3 collective-permute-start
  109.6 0.7 tile.19
  110.3 3.7 %all-to-all-start.4 = ((bf16[8,16,1024]{2,1,0:T(8,128)(2,1)}), bf16[8,16,1024]{2,1,0:T(8,128)(2,1)S(1)}, u32[]{:S(2)}, u32[]{:S(2)}) async-start(bf16[8,16,1024]{2,1,0:T(8,128)(2,1)} %tile.19), calls=%async_computation.4 | async-start | bytes 524288 | tf_op jit(solution)/shard_map/all_to_all | solution.py:367
  114.0 1.8 broadcast_select_fusion
  115.9 3.1 %shard_map.91 = bf16[128,1152]{1,0:T(8,128)(2,1)} custom-call(bf16[1024,128]{1,0:T(8,128)(2,1)} %get-tuple-element.43.x_ref, f32[1024,128]{1,0:T(8,128)} %get-tuple-element.25.gain_ref, bf16[1024,1024]{1,0:T(8,128)(2,1)} %get-tuple-element.35.q_ref), custom_call_target="tpu_custom_call" | custom-call | flops 268435456 | bytes 2097152 | tf_op jit(solution)/shard_map/pallas_call | solution.py:535
  118.9 3.6 %all-to-all-done.4 = bf16[8,16,1024]{2,1,0:T(8,128)(2,1)S(1)} async-done(((bf16[8,16,1024]{2,1,0:T(8,128)(2,1)}), bf16[8,16,1024]{2,1,0:T(8,128)(2,1)S(1)}, u32[]{:S(2)}, u32[]{:S(2)}) %all-to-all-start.4) | async-done | bytes 262176 | tf_op jit(solution)/shard_map/all_to_all | solution.py:367
  122.5 3.6 %all-to-all-start.3 = ((bf16[8,16,1152]{2,1,0:T(8,128)(2,1)}), bf16[8,16,1152]{2,1,0:T(8,128)(2,1)S(1)}, u32[]{:S(2)}, u32[]{:S(2)}) async-start(bf16[8,16,1152]{2,1,0:T(8,128)(2,1)} %bitcast.36), calls=%async_computation.3 | async-start | bytes 589824 | tf_op jit(solution)/shard_map/all_to_all | solution.py:367
  126.2 3.1 %shard_map.92 = bf16[1024,128]{1,0:T(8,128)(2,1)} custom-call(bf16[128,1024]{1,0:T(8,128)(2,1)} %bitcast.35, bf16[1024,1024]{1,0:T(8,128)(2,1)} %get-tuple-element.35.q_ref, f32[1024,128]{1,0:T(8,128)} %get-tuple-element.25.gain_ref), custom_call_target="tpu_custom_call" | custom-call | flops 268435456 | bytes 2097152 | tf_op jit(solution)/shard_map/pallas_call | solution.py:543
  129.3 1.3 collective-permute-start.1
  130.6 2.3 %collective-permute-done.1.grad_ref = bf16[1024,128]{1,0:T(8,128)(2,1)S(1)} collective-permute-done((bf16[1024,128]{1,0:T(8,128)(2,1)}, bf16[1024,128]{1,0:T(8,128)(2,1)S(1)}, u32[]{:S(2)}, u32[]{:S(2)}) %collective-permute-start.1) | collective-permute-done | bytes 262176 | tf_op jit(solution)/shard_map/ppermute | solution.py:548
  133.6 9.1 %shard_map.93.back_ref = bf16[128,8192]{1,0:T(8,128)(2,1)} custom-call(bf16[1024,8192]{1,0:T(8,128)(2,1)} %get-tuple-element.32.q_ref, bf16[1024,128]{1,0:T(8,128)(2,1)} %copy-done.5), custom_call_target="tpu_custom_call" | custom-call | flops 2147483648 | bytes 16777216 | tf_op jit(solution)/shard_map/pallas_call | solution.py:549
  144.0 4.9 %shard_map.94 = bf16[128,1024]{1,0:T(8,128)(2,1)} custom-call(f32[1,128]{1,0:T(1,128)} %copy-done.7, bf16[128,8192]{1,0:T(8,128)(2,1)} %get-tuple-element.36.ct_back_ref, bf16[128,8192]{1,0:T(8,128)(2,1)} %shard_map.93.back_ref, bf16[2,4096,64]{2,1,0:T(8,128)(2,1)} %reshape_squeeze.3.refs_3_.probs_ref), custom_call_target="tpu_custom_call" | custom-call | flops 134217728 | bytes 6291456 | tf_op jit(solution)/shard_map/pallas_call | solution.py:559
  148.9 1.0 bitcast_select_fusion.1
  149.8 14.1 %all_to_all.74 = bf16[8,16,1024]{2,1,0:T(8,128)(2,1)S(1)} all-to-all(bf16[8,16,1024]{2,1,0:T(8,128)(2,1)S(1)} %bitcast.38), channel_id=1, replica_groups=mesh['groups'=2,'tensor'=8,'section'=2] {'tensor'}, dimensions={0} | all-to-all | bytes 524288 | tf_op jit(solution)/shard_map/all_to_all | solution.py:367
  164.0 0.8 tile.22
  164.8 3.4 %all-to-all-start.6 = ((bf16[8,16,1024]{2,1,0:T(8,128)(2,1)}), bf16[8,16,1024]{2,1,0:T(8,128)(2,1)S(1)}, u32[]{:S(2)}, u32[]{:S(2)}) async-start(bf16[8,16,1024]{2,1,0:T(8,128)(2,1)} %tile.22), calls=%async_computation.6 | async-start | bytes 524288 | tf_op jit(solution)/shard_map/all_to_all | solution.py:367
  168.2 16.9 %shard_map.95.other_ref = f32[128,128]{1,0:T(8,128)} custom-call(s32[1]{0:T(128)} %bitcast.13.section_ref, bf16[128,1024]{1,0:T(8,128)(2,1)} %bitcast.33, f32[1,128]{1,0:T(1,128)} %copy-done.7, bf16[2,4096,64]{2,1,0:T(8,128)(2,1)} %reshape_squeeze.3.refs_3_.probs_ref, bf16[128,8192]{1,0:T(8,128)(2,1)} %get-tuple-element.38.mixed_in_ref, ...), custom_call_target="tpu_custom_call" | custom-call | flops 4294967296 | bytes 33554432 | tf_op jit(solution)/shard_map/pallas_call | solution.py:569
  185.1 0.8 bitcast_select_fusion.vg_ref
  185.9 4.6 %shard_map.96 = bf16[128,128]{1,0:T(8,128)(2,1)} custom-call(bf16[1024,128]{1,0:T(8,128)(2,1)} %get-tuple-element.42.x_ref, f32[1,128]{1,0:T(1,128)} %get-tuple-element.45.mean_ref, f32[1024,128]{1,0:T(8,128)} %get-tuple-element.25.gain_ref, bf16[128,1024]{1,0:T(8,128)(2,1)} %bitcast_select_fusion.vg_ref, bf16[1024,1024]{1,0:T(8,128)(2,1)} %bitcast.32, ...), custom_call_target="tpu_custom_call" | custom-call | flops 536870912 | bytes 4194304 | tf_op jit(solution)/shard_map/pallas_call | solution.py:592
  190.5 0.8 tile.23
  191.3 14.4 %all_to_all.75 = bf16[8,128,128]{2,1,0:T(8,128)(2,1)} all-to-all(bf16[8,128,128]{2,1,0:T(8,128)(2,1)S(1)} %tile.23), channel_id=1, replica_groups=mesh['groups'=2,'tensor'=8,'section'=2] {'tensor'}, dimensions={0} | all-to-all | bytes 524288 | tf_op jit(solution)/shard_map/all_to_all | solution.py:367
  205.7 2.6 %shard_map.97 = (f32[128,128]{1,0:T(8,128)}, f32[128,128]{1,0:T(8,128)}) custom-call(bf16[1024,128]{1,0:T(8,128)(2,1)} %bitcast.40, f32[128,128]{1,0:T(8,128)} %bitcast.45), custom_call_target="tpu_custom_call" | custom-call | flops 125829120 | bytes 131072 | tf_op jit(solution)/shard_map/pallas_call | solution.py:605
  (33 shorter events, 3.4 us)
Async XLA Ops:
  7.3 25.1 %all-to-all-start = ((f32[8,1,1152]{2,1,0:T(1,128)}), f32[8,1,1152]{2,1,0:T(1,128)S(1)}, u32[]{:S(2)}, u32[]{:S(2)}) async-start(f32[8,1,1152]{2,1,0:T(1,128)} %tile.16), calls=%async_computation | async-start | bytes 73728 | tf_op jit(solution)/shard_map/all_to_all | solution.py:367
  14.6 14.6 %copy-start.6 = (bf16[1,2,64,4096]{3,2,1,0:T(8,128)(2,1)S(1)}, bf16[1,2,64,4096]{3,2,1,0:T(8,128)(2,1)}, u32[]{:S(2)}) copy-start(bf16[1,2,64,4096]{3,2,1,0:T(8,128)(2,1)} %param.13) | copy-start | bytes 3145732
  40.7 42.0 %all-to-all-start.1 = ((bf16[8,16,1024]{2,1,0:T(8,128)(2,1)}), bf16[8,16,1024]{2,1,0:T(8,128)(2,1)S(1)}, u32[]{:S(2)}, u32[]{:S(2)}) async-start(bf16[8,16,1024]{2,1,0:T(8,128)(2,1)} %bitcast.39), calls=%async_computation.1 | async-start | bytes 524288 | tf_op jit(solution)/shard_map/all_to_all | solution.py:367
  97.5 12.1 %copy-start.2 = (bf16[8,16,1024]{2,1,0:T(8,128)(2,1)S(1)}, bf16[8,16,1024]{2,1,0:T(8,128)(2,1)}, u32[]{:S(2)}) copy-start(bf16[8,16,1024]{2,1,0:T(8,128)(2,1)} %all_to_all.73) | copy-start | bytes 786436
  97.5 16.5 %copy-start = (bf16[1024,128]{1,0:T(8,128)(2,1)S(1)}, bf16[1024,128]{1,0:T(8,128)(2,1)}, u32[]{:S(2)}) copy-start(bf16[1024,128]{1,0:T(8,128)(2,1)} %get-tuple-element.22.x_ref) | copy-start | bytes 786436
  108.3 5.8 %collective-permute-start = (bf16[1024,128]{1,0:T(8,128)(2,1)}, bf16[1024,128]{1,0:T(8,128)(2,1)S(1)}, u32[]{:S(2)}, u32[]{:S(2)}) collective-permute-start(bf16[1024,128]{1,0:T(8,128)(2,1)} %get-tuple-element.33), channel_id=1, source_target_pairs={{0,1},{2,3},{4,5},{6,7},{8,9},{10,11},{12,13},{14,15},{16,17},{18,... | collective-permute-start | bytes 786440 | tf_op jit(solution)/shard_map/ppermute | solution.py:532
  110.3 12.2 %all-to-all-start.4 = ((bf16[8,16,1024]{2,1,0:T(8,128)(2,1)}), bf16[8,16,1024]{2,1,0:T(8,128)(2,1)S(1)}, u32[]{:S(2)}, u32[]{:S(2)}) async-start(bf16[8,16,1024]{2,1,0:T(8,128)(2,1)} %tile.19), calls=%async_computation.4 | async-start | bytes 524288 | tf_op jit(solution)/shard_map/all_to_all | solution.py:367
  122.5 3.6 %copy-start.3 = (bf16[8,16,1024]{2,1,0:T(8,128)(2,1)}, bf16[8,16,1024]{2,1,0:T(8,128)(2,1)S(1)}, u32[]{:S(2)}) copy-start(bf16[8,16,1024]{2,1,0:T(8,128)(2,1)S(1)} %all-to-all-done.4) | copy-start | bytes 786436
  122.5 20.2 %all-to-all-start.3 = ((bf16[8,16,1152]{2,1,0:T(8,128)(2,1)}), bf16[8,16,1152]{2,1,0:T(8,128)(2,1)S(1)}, u32[]{:S(2)}, u32[]{:S(2)}) async-start(bf16[8,16,1152]{2,1,0:T(8,128)(2,1)} %bitcast.36), calls=%async_computation.3 | async-start | bytes 589824 | tf_op jit(solution)/shard_map/all_to_all | solution.py:367
  129.3 3.6 %collective-permute-start.1 = (bf16[1024,128]{1,0:T(8,128)(2,1)}, bf16[1024,128]{1,0:T(8,128)(2,1)S(1)}, u32[]{:S(2)}, u32[]{:S(2)}) collective-permute-start(bf16[1024,128]{1,0:T(8,128)(2,1)} %shard_map.92), channel_id=1, source_target_pairs={{1,0},{3,2},{5,4},{7,6},{9,8},{11,10},{13,12},{15,14},{17,16},{19,... | collective-permute-start | bytes 786440 | tf_op jit(solution)/shard_map/ppermute | solution.py:548
  130.6 12.2 %copy-start.8 = (f32[1,128]{1,0:T(1,128)S(1)}, f32[1,128]{1,0:T(1,128)}, u32[]{:S(2)}) copy-start(f32[1,128]{1,0:T(1,128)} %get-tuple-element.34) | copy-start | bytes 1540
  132.9 0.7 copy-start.5
  143.4 0.6 copy-start.7
  164.0 4.2 %copy-start.1 = (bf16[8,16,1024]{2,1,0:T(8,128)(2,1)}, bf16[8,16,1024]{2,1,0:T(8,128)(2,1)S(1)}, u32[]{:S(2)}) copy-start(bf16[8,16,1024]{2,1,0:T(8,128)(2,1)S(1)} %all_to_all.74) | copy-start | bytes 786436
  164.8 20.4 %all-to-all-start.6 = ((bf16[8,16,1024]{2,1,0:T(8,128)(2,1)}), bf16[8,16,1024]{2,1,0:T(8,128)(2,1)S(1)}, u32[]{:S(2)}, u32[]{:S(2)}) async-start(bf16[8,16,1024]{2,1,0:T(8,128)(2,1)} %tile.22), calls=%async_computation.6 | async-start | bytes 524288 | tf_op jit(solution)/shard_map/all_to_all | solution.py:367
  168.2 16.9 %copy-start.4 = (bf16[8,16,1024]{2,1,0:T(8,128)(2,1)S(1)}, bf16[8,16,1024]{2,1,0:T(8,128)(2,1)}, u32[]{:S(2)}) copy-start(bf16[8,16,1024]{2,1,0:T(8,128)(2,1)} %copy-done.3) | copy-start | bytes 786436

commit v3 on v2

--- a/solution.py
+++ b/solution.py
@@ -72,6 +72,11 @@
 
 def call(kernel, out_shape, cost, **kw):
     flops, moved = cost
+    prefetch = kw.pop("prefetch", 0)
+    if prefetch:
+        names = ("grid", "in_specs", "out_specs", "scratch_shapes")
+        fields = {name: kw.pop(name) for name in names if name in kw}
+        kw["grid_spec"] = pltpu.PrefetchScalarGridSpec(num_scalar_prefetch=prefetch, **fields)
     return pl.pallas_call(
         kernel,
         out_shape=out_shape,
@@ -86,7 +91,8 @@
 
 
 def value_rot_kernel(
-    hidden_ref, ct_ref, gain_row_ref, value_ref, rot_ref, x_ref, ct_t_ref, gain_ref, vrot_ref, stat_ref
+    hidden_ref, ct_ref, gain_row_ref, value_ref, rot_ref,
+    x_ref, ct_t_ref, gain_ref, vrot_ref, stats_ref, stat_ref,
 ):
     kv_width = value_ref.shape[1]
     high, low = rotation_pair(rot_ref[...])
@@ -107,6 +113,10 @@
     stat_ref[:, kv_width:] += jnp.sum(x * x, axis=0, keepdims=True)
     ct_t_ref[...] = jnp.transpose(ct_ref[...].astype(F32)).astype(BF16)
     gain_ref[...] = jnp.transpose(jnp.broadcast_to(gain_row_ref[...], hidden_ref.shape))
+
+    @pl.when(pl.program_id(0) == pl.num_programs(0) - 1)
+    def _():
+        stats_ref[...] = jnp.broadcast_to(stat_ref[...], stats_ref.shape)
 
 
 def mix_back(probs_ref, grad_of, out_ref, seq, per_group, kv_count):
@@ -150,9 +160,9 @@
         del refs[:4]
     q_ref, slope_ref = refs[:2]
     del refs[:2]
+    back_ref = refs.pop(0)
     if ends:
-        back_ref, vg_ref = refs[:2]
-        del refs[:2]
+        vg_ref = refs.pop(0)
     total_ref, turned_ref, inv_ref, factor_ref = refs
     rows, width = w_ref.shape
     step, last = pl.program_id(0), number - 1
@@ -161,7 +171,7 @@
 
     @pl.when(step == 0)
     def _():
-        total_ref[...] = jnp.zeros_like(total_ref) if starts else held_ref[...]
+        total_ref[...] = jnp.zeros_like(total_ref)
 
     high, low = rotation_pair(rot_ref[...])
     peak = jnp.zeros((rows, LANES), F32)
@@ -194,10 +204,17 @@
 
         @pl.when(step == last)
         def _():
+            if not starts:
+                total_ref[...] += held_ref[...].astype(F32)
             back_ref[...] = total_ref[...].astype(BF16)
             seq = probs_ref.shape[2]
             per_group = width // LANES // kv_count
             mix_back(probs_ref, lambda r, c: back_ref[r, c], vg_ref, seq, per_group, kv_count)
+    else:
+
+        @pl.when(step == last)
+        def _():
+            back_ref[...] = total_ref[...].astype(BF16)
 
 
 def value_quant_kernel(
@@ -238,67 +255,122 @@
         part_ref[...] = total_ref[...].astype(BF16)
 
 
-def input_grad_kernel(vg_ref, q_ref, gain_ref, out_ref):
-    out_ref[...] = (dot_nt(q_ref[...], vg_ref[...]) * gain_ref[...]).astype(BF16)
-
-
-def forward_kernel(kv_count, values_ref, probs_ref, q_ref, x_ref, mixed_ref, out_ref):
-    @pl.when(pl.program_id(0) == 0)
-    def _():
-        seq = probs_ref.shape[2]
-        per_group = q_ref.shape[1] // LANES // kv_count
-        mix_forward(probs_ref, lambda r, c: values_ref[r, c], mixed_ref, seq, per_group, kv_count)
-
-    out_ref[...] = (x_ref[...].astype(F32) + dot_nt(q_ref[...], mixed_ref[...])).astype(BF16)
-
-
-def back_kernel(q_ref, grad_ref, back_ref, total_ref):
+def forward_kernel(kv_count, active_ref, values_ref, probs_ref, q_ref, x_ref, mixed_ref, out_ref):
+    @pl.when(active_ref[0] == 1)
+    def _():
+        @pl.when(pl.program_id(0) == 0)
+        def _():
+            seq = probs_ref.shape[2]
+            per_group = q_ref.shape[1] // LANES // kv_count
+            mix_forward(
+                probs_ref, lambda r, c: values_ref[r, c], mixed_ref, seq, per_group, kv_count
+            )
+
+        out_ref[...] = (x_ref[...].astype(F32) + dot_nt(q_ref[...], mixed_ref[...])).astype(BF16)
+
+
+def back_kernel(active_ref, q_ref, grad_ref, after_ref, back_ref, total_ref):
     width = q_ref.shape[1]
 
-    @pl.when(pl.program_id(0) == 0)
+    @pl.when(active_ref[0] == 1)
+    def _():
+        @pl.when(pl.program_id(0) == 0)
+        def _():
+            total_ref[...] = jnp.zeros_like(total_ref)
+
+        wide = min(1024, width)
+        for at in range(0, width, wide):
+            cols = slice(at, at + wide)
+            total_ref[:, cols] += dot_tn(grad_ref[...], q_ref[:, cols])
+
+        @pl.when(pl.program_id(0) == pl.num_programs(0) - 1)
+        def _():
+            back_ref[...] = total_ref[...].astype(BF16)
+
+
+def project_kernel(
+    active_ref, own_ref, arrived_ref, vg_ref, gain_ref, q_ref, out_ref, grad_ref, total_ref, sum_ref
+):
+    kv_width = q_ref.shape[1]
+    last_section = active_ref[0] == 1
+    first, last = pl.program_id(0) == 0, pl.program_id(0) == pl.num_programs(0) - 1
+
+    @pl.when(first)
     def _():
         total_ref[...] = jnp.zeros_like(total_ref)
-
-    wide = min(1024, width)
-    for at in range(0, width, wide):
-        cols = slice(at, at + wide)
-        total_ref[:, cols] += dot_tn(grad_ref[...], q_ref[:, cols])
-
-    @pl.when(pl.program_id(0) == pl.num_programs(0) - 1)
-    def _():
-        back_ref[...] = total_ref[...].astype(BF16)
-
-
-def project_kernel(x_ref, gain_ref, q_ref, out_ref):
-    kv_width = q_ref.shape[1]
-    x = x_ref[...].astype(F32)
-    gained = (x * gain_ref[...]).astype(BF16)
-    out_ref[:, :kv_width] = dot_tn(gained, q_ref[...]).astype(BF16)
-    squares = jnp.sum(x * x, axis=0, keepdims=True)
-    tokens = squares.shape[1]
-    out_ref[:, kv_width:] = jnp.broadcast_to(squares, (tokens, tokens)).astype(BF16)
-
-
-def value_grad_kernel(kv_count, mean_ref, ct_back_ref, back_ref, probs_ref, out_ref):
-    inverse = column_of(mean_ref[...])[:, :1]
+        sum_ref[...] = jnp.zeros_like(sum_ref)
+
+    x = jnp.where(last_section, arrived_ref[...], own_ref[...]).astype(F32)
+    sum_ref[...] += jnp.sum(x * x, axis=0, keepdims=True)
+
+    @pl.when(last_section)
+    def _():
+        total_ref[...] += dot_tn((x * gain_ref[...]).astype(BF16), q_ref[...])
+        grad_ref[...] = (dot_nt(q_ref[...], vg_ref[...]) * gain_ref[...]).astype(BF16)
+
+    @pl.when(last)
+    def _():
+        out_ref[:, :kv_width] = total_ref[...].astype(BF16)
+        tokens = sum_ref.shape[1]
+        out_ref[:, kv_width:] = jnp.broadcast_to(sum_ref[...], (tokens, tokens)).astype(BF16)
+
+
+def value_grad_kernel(kv_count, active_ref, mean_ref, ct_back_ref, back_ref, probs_ref, out_ref, inv_ref):
     seq = probs_ref.shape[2]
     per_group = back_ref.shape[1] // LANES // kv_count
 
-    def grad_of(rows, cols):
-        return (
-            ct_back_ref[rows, cols].astype(F32) + inverse[rows] * back_ref[rows, cols].astype(F32)
-        ).astype(BF16)
-
-    mix_back(probs_ref, grad_of, out_ref, seq, per_group, kv_count)
+    @pl.when(active_ref[0] == 1)
+    def _():
+        inv_ref[...] = column_of(mean_ref[...])
+        inverse = inv_ref[pl.ds(pl.multiple_of(pl.program_id(0) * seq, seq), seq), :1]
+
+        def grad_of(rows, cols):
+            return (
+                ct_back_ref[rows, cols].astype(F32) + inverse * back_ref[rows, cols].astype(F32)
+            ).astype(BF16)
+
+        mix_back(probs_ref, grad_of, out_ref, seq, per_group, kv_count)
+
+
+def out_grad_block(grad, mixed_ref, w_ref, slope_ref, total_ref):
+    width, together = w_ref.shape[1], 8
+    for first in range(0, width, 2 * LANES * together):
+        pieces = []
+        for at in range(first, min(first + 2 * LANES * together, width), 2 * LANES):
+            cols = slice(at, at + 2 * LANES)
+            out_grad = dot_nn(grad, mixed_ref[:, cols])
+            sloped = (out_grad * slope_ref[:, cols].astype(F32)).astype(BF16)
+            pieces.append((w_ref[:, cols], sloped))
+        total_ref[...] += dot_tn(*(jnp.concatenate(side, 0) for side in zip(*pieces)))
+
+
+def both_heads(total_ref):
+    return total_ref[:LANES, :LANES] + total_ref[LANES:, LANES:]
+
+
+def early_grad_kernel(
+    section_ref, mean_ref, mixed_ref, ct_ref, grad_ref, w_ref, slope_ref, after_ref, out_ref, total_ref
+):
+    @pl.when(pl.program_id(0) == 0)
+    def _():
+        total_ref[...] = jnp.zeros_like(total_ref)
+
+    @pl.when(section_ref[0] == 0)
+    def _():
+        grad = (ct_ref[...].astype(F32) + mean_ref[...] * grad_ref[...].astype(F32)).astype(BF16)
+        out_grad_block(grad, mixed_ref, w_ref, slope_ref, total_ref)
+
+    @pl.when(pl.program_id(0) == pl.num_programs(0) - 1)
+    def _():
+        out_ref[...] = both_heads(total_ref)
 
 
 def out_grad_kernel(
-    kv_count, section_ref, values_ref, mean_ref, probs_ref, mixed_in_ref,
-    ct_ref, grad_ref, w_ref, slope_ref, out_ref, mixed_ref, total_ref,
+    kv_count, half, section_ref, values_ref, mean_ref, probs_ref, mixed_in_ref,
+    ct_ref, grad_ref, w_ref, slope_ref, other_ref, out_ref, mixed_ref, total_ref,
 ):
-    width = w_ref.shape[1]
     seq = probs_ref.shape[2]
-    per_group = width // LANES // kv_count
+    per_group = w_ref.shape[1] // LANES // kv_count
     last_section = section_ref[0] != 0
 
     @pl.when(pl.program_id(0) == 0)
@@ -311,35 +383,49 @@
                 probs_ref, lambda r, c: values_ref[r, c], mixed_ref, seq, per_group, kv_count
             )
 
-        @pl.when(jnp.logical_not(last_section))
-        def _():
-            mixed_ref[...] = mixed_in_ref[...]
-
-    keep = jnp.where(last_section, 0.0, 1.0)
-    grad = (
-        ct_ref[...].astype(F32) + (keep * mean_ref[...]) * grad_ref[...].astype(F32)
-    ).astype(BF16)
-    for at in range(0, width, 2 * LANES):
-        cols = slice(at, at + 2 * LANES)
-        out_grad = dot_nn(grad, mixed_ref[:, cols])
-        sloped = (out_grad * slope_ref[:, cols].astype(F32)).astype(BF16)
-        total_ref[...] += dot_tn(w_ref[:, cols], sloped)
+    @pl.when(last_section)
+    def _():
+        out_grad_block(ct_ref[...], mixed_ref, w_ref, slope_ref, total_ref)
+
+    @pl.when(jnp.logical_and(section_ref[0] == 0, pl.program_id(0) >= half))
+    def _():
+        grad = (ct_ref[...].astype(F32) + mean_ref[...] * grad_ref[...].astype(F32)).astype(BF16)
+        out_grad_block(grad, mixed_in_ref, w_ref, slope_ref, total_ref)
 
     @pl.when(pl.program_id(0) == pl.num_programs(0) - 1)
     def _():
-        out_ref[...] = total_ref[:LANES, :LANES] + total_ref[LANES:, LANES:]
-
-
-def value_part_kernel(x_ref, mean_ref, gain_ref, vg_ref, v_ref, slope_ref, other_ref, out_ref):
-    normed = (x_ref[...].astype(F32) * mean_ref[...] * gain_ref[...]).astype(BF16)
-    total = other_ref[...]
+        out_ref[...] = both_heads(total_ref)
+        if half:
+            out_ref[...] += other_ref[...]
+
+
+def value_part_kernel(
+    section_ref, x0_ref, x1_ref, mean0_ref, mean1_ref, gain_ref, vg0_ref, vg1_ref, v_ref, slope_ref,
+    other_ref, out_ref, total_ref,
+):
+    first = section_ref[0] == 0
+    x = jnp.where(first, x0_ref[...], x1_ref[...]).astype(F32)
+    mean = jnp.where(first, mean0_ref[...], mean1_ref[...])
+    normed = (x * mean * gain_ref[...]).astype(BF16)
+
+    @pl.when(pl.program_id(0) == 0)
+    def _():
+        total_ref[...] = other_ref[...]
+
+    pieces = []
     for at in range(0, v_ref.shape[1], 2 * LANES):
         cols = slice(at, at + 2 * LANES)
-        grad = dot_nn(normed, vg_ref[:, cols])
+        grad = dot_nn(normed, jnp.where(first, vg0_ref[:, cols], vg1_ref[:, cols]))
         sloped = (grad * slope_ref[:, cols].astype(F32)).astype(BF16)
-        both = dot_tn(v_ref[:, cols], sloped)
-        total = total + both[:LANES, :LANES] + both[LANES:, LANES:]
-    out_ref[...] = (slope_factor * total).astype(out_ref.dtype)
+        pieces.append((v_ref[:, cols], sloped))
+    both = dot_tn(*(jnp.concatenate(side, 0) for side in zip(*pieces)))
+    total_ref[...] += both[:LANES, :LANES] + both[LANES:, LANES:]
+
+    @pl.when(pl.program_id(0) == pl.num_programs(0) - 1)
+    def _():
+        total = (slope_factor * total_ref[...]).astype(out_ref.dtype)
+        for i in range(out_ref.shape[0] // LANES):
+            out_ref[i * LANES : (i + 1) * LANES] = total
 
 
 def cayley_kernel(parts_ref, rot_ref, grad_ref, new_ref):
@@ -402,7 +488,7 @@
             shaped((local, tokens), BF16),
             shaped((local, tokens), F32),
             shaped((local, kv_width), F32),
-            shaped((1, kv_width + tokens), F32),
+            shaped((count, kv_width + tokens), F32),
         ),
         (4 * local * kv_width * LANES, 6 * local * kv_width),
         grid=(local // rows,),
@@ -418,10 +504,11 @@
             split(rows, tokens),
             split(rows, tokens),
             split(rows, kv_width),
-            whole(1, kv_width + tokens),
+            whole(count, kv_width + tokens),
         ),
+        scratch_shapes=[pltpu.VMEM((1, kv_width + tokens), F32)],
     )(hidden, cotangent, norm_gain, value_w, rot)
-    stats = exchange(jnp.tile(stat, (count, 1)))
+    stats = exchange(stat)
 
     part_rows = min(local, 128)
     part_count = local // part_rows
@@ -450,13 +537,12 @@
             aliases = {at + 2: 0, at + 3: 1}
         outs = [shaped((local, width), BF16), shaped((local, width), BF16)]
         out_specs = [behind(part_rows, width), behind(part_rows, width)]
-        scratch = []
+        scratch = [pltpu.VMEM((tokens, width), F32)]
         if ends:
             outs += [shaped((tokens, width), BF16), shaped((tokens, kv_width), BF16)]
             out_specs += [whole(tokens, width), whole(tokens, kv_width)]
-            scratch.append(pltpu.VMEM((tokens, width), F32))
         else:
-            outs.append(shaped((tokens, width), F32))
+            outs.append(shaped((tokens, width), BF16))
             out_specs.append(whole(tokens, width))
         scratch += [
             pltpu.VMEM((part_rows, width), F32),
@@ -513,100 +599,170 @@
         before = tuple(before) + (value_part,)
     quant, slope, ct_back, ct_vg = prepare(lead, part_count - lead, before)
 
+    on_first = 1 - flag
+    anywhere = pl.BlockSpec(memory_space=pl.ANY)
+
+    def only(lines, *tail):
+        return pl.BlockSpec((lines,) + tail, lambda i, active: (i * active[0], 0))
+
+    def each(lines, *tail):
+        return pl.BlockSpec((lines,) + tail, lambda i, active: (i, 0))
+
+    def fixed(*shape):
+        return pl.BlockSpec(shape, lambda i, active: (0,) * len(shape))
+
     second = exchange(jnp.where(is_first, values0, ct_vg))
-    vg1 = exchange(spread(add_parts(second)))
+    second, to_gather = lax.optimization_barrier((second, spread(add_parts(second))))
+    vg1 = exchange(to_gather)
 
     mixed, x1 = call(
         functools.partial(forward_kernel, kv_count),
         (shaped((tokens, width), BF16), shaped((local, tokens), BF16)),
         (big, 2 * local * width),
+        prefetch=1,
         grid=(local // rows,),
         in_specs=[
-            whole(tokens, kv_width),
-            whole(*probs.shape),
-            split(rows, width),
-            split(rows, tokens),
+            fixed(tokens, kv_width),
+            fixed(*probs.shape),
+            only(rows, width),
+            only(rows, tokens),
         ],
-        out_specs=(whole(tokens, width), split(rows, tokens)),
-    )(second, probs, quant, x0)
+        out_specs=(fixed(tokens, width), only(rows, tokens)),
+    )(on_first, second, probs, quant, x0)
     arrived = lax.ppermute(x1, "section", [(0, 1)])
-    x1 = jnp.where(is_first, x1, arrived)
-
-    projected = call(
+
+    half_rows = max(local // 2, min(local, 128))
+    projected, grad1 = call(
         project_kernel,
-        shaped((tokens, kv_width + tokens), BF16),
-        (2 * local * kv_width * tokens, 2 * local * kv_width),
-    )(x1, gain, value_q)
+        (shaped((tokens, kv_width + tokens), BF16), shaped((local, tokens), BF16)),
+        (4 * local * kv_width * tokens, 2 * local * kv_width),
+        prefetch=1,
+        grid=(local // half_rows,),
+        in_specs=[
+            each(half_rows, tokens),
+            each(half_rows, tokens),
+            fixed(tokens, kv_width),
+            each(half_rows, tokens),
+            only(half_rows, kv_width),
+        ],
+        out_specs=(fixed(tokens, kv_width + tokens), only(half_rows, tokens)),
+        scratch_shapes=[pltpu.VMEM((tokens, kv_width), F32), pltpu.VMEM((1, tokens), F32)],
+    )(flag, x1, arrived, vg1, gain, value_q)
     received = add_parts(exchange(projected))
     mean1 = lax.rsqrt(received[:1, kv_width:] / model_width + norm_eps)
 
-    grad1 = call(
-        input_grad_kernel,
-        shaped((local, tokens), BF16),
-        (2 * local * kv_width * tokens, 2 * local * kv_width),
-    )(vg1, value_q, gain)
     grad1 = lax.ppermute(grad1, "section", [(1, 0)])
     grad_back = call(
         back_kernel,
         shaped((tokens, width), BF16),
         (big, 2 * local * width),
+        prefetch=1,
         grid=(local // rows,),
-        in_specs=[split(rows, width), split(rows, tokens)],
-        out_specs=whole(tokens, width),
+        in_specs=[only(rows, width), only(rows, tokens), anywhere],
+        out_specs=fixed(tokens, width),
         scratch_shapes=[pltpu.VMEM((tokens, width), F32)],
-    )(quant, grad1)
+    )(on_first, quant, grad1, projected)
 
     vg0 = call(
         functools.partial(value_grad_kernel, kv_count),
         shaped((tokens, kv_width), BF16),
         (2 * tokens * width * seq, 6 * tokens * width),
-    )(mean1, ct_back, grad_back, probs)
+        prefetch=1,
+        grid=(blocks,),
+        in_specs=[
+            fixed(1, tokens),
+            each(seq, width),
+            each(seq, width),
+            pl.BlockSpec((1, heads * seq, seq), lambda i, active: (i, 0, 0)),
+        ],
+        out_specs=each(seq, kv_width),
+        scratch_shapes=[pltpu.VMEM((tokens, tokens), F32)],
+    )(on_first, mean1, ct_back, grad_back, probs)
     mine = lax.axis_index("tensor") * (tokens // count)
     own_mean = lax.dynamic_slice(mean1[0], (mine,), (tokens // count,))[:, None]
-    values1 = exchange(jnp.where(is_first, vg0, spread(received[:, :kv_width] * own_mean)))
+    to_send = jnp.where(is_first, vg0, spread(received[:, :kv_width] * own_mean))
+    values1 = exchange(to_send)
+
+    def early(lines, *tail):
+        return pl.BlockSpec((lines,) + tail, lambda i, section: (i * (1 - section[0]), 0))
+
+    half = part_count // 2
+    pair_total = pltpu.VMEM((2 * LANES, 2 * LANES), F32)
+    out_part = jnp.zeros((LANES, LANES), F32)
+    if half:
+        out_part = call(
+            early_grad_kernel,
+            shaped((LANES, LANES), F32),
+            (big, 2 * local * width),
+            prefetch=1,
+            grid=(half,),
+            in_specs=[
+                fixed(1, tokens),
+                fixed(tokens, width),
+                early(part_rows, tokens),
+                early(part_rows, tokens),
+                early(part_rows, width),
+                early(part_rows, width),
+                anywhere,
+            ],
+            out_specs=fixed(LANES, LANES),
+            scratch_shapes=[pair_total],
+        )(flag, mean1, mixed, ct, grad1, out_w, slope, to_send)
+        values1, out_part = lax.optimization_barrier((values1, out_part))
     vg0 = exchange(spread(add_parts(values1)))
 
+    def late(lines, *tail):
+        return pl.BlockSpec(
+            (lines,) + tail, lambda i, section: (jnp.maximum(i, (1 - section[0]) * half), 0)
+        )
+
     out_part = call(
-        functools.partial(out_grad_kernel, kv_count),
+        functools.partial(out_grad_kernel, kv_count, half),
         shaped((LANES, LANES), F32),
         (2 * big, 4 * local * width),
-        grid=(local // rows,),
+        prefetch=1,
+        grid=(part_count,),
+        in_specs=[
+            fixed(tokens, kv_width),
+            fixed(1, tokens),
+            fixed(*probs.shape),
+            fixed(tokens, width),
+            late(part_rows, tokens),
+            late(part_rows, tokens),
+            late(part_rows, width),
+            late(part_rows, width),
+            fixed(LANES, LANES),
+        ],
+        out_specs=fixed(LANES, LANES),
+        scratch_shapes=[pltpu.VMEM((tokens, width), BF16), pair_total],
+    )(flag, values1, mean1, probs, mixed, ct, grad1, out_w, slope, out_part)
+
+    rot_part = call(
+        value_part_kernel,
+        shaped((count * LANES, LANES), BF16),
+        (4 * local * kv_width * tokens, 4 * local * kv_width),
+        grid=(1,),
         in_specs=[
             pl.BlockSpec(memory_space=pltpu.SMEM),
+            split(local, tokens),
+            split(local, tokens),
+            whole(1, tokens),
+            whole(1, tokens),
+            split(local, tokens),
             whole(tokens, kv_width),
-            whole(1, tokens),
-            whole(*probs.shape),
-            whole(tokens, width),
-            split(rows, tokens),
-            split(rows, tokens),
-            split(rows, width),
-            split(rows, width),
+            whole(tokens, kv_width),
+            split(local, kv_width),
+            split(local, kv_width),
+            whole(LANES, LANES),
         ],
-        out_specs=whole(LANES, LANES),
-        scratch_shapes=[
-            pltpu.VMEM((tokens, width), BF16),
-            pltpu.VMEM((2 * LANES, 2 * LANES), F32),
-        ],
-    )(flag, values1, mean1, probs, mixed, ct, grad1, out_w, slope)
-
-    rot_part = call(
-        value_part_kernel,
-        shaped((LANES, LANES), BF16),
-        (4 * local * kv_width * tokens, 4 * local * kv_width),
-    )(
-        jnp.where(is_first, x0, x1),
-        jnp.where(is_first, mean0, mean1),
-        gain,
-        jnp.where(is_first, vg0, vg1),
-        value_w,
-        value_slope,
-        out_part,
-    )
+        out_specs=whole(count * LANES, LANES),
+        scratch_shapes=[pltpu.VMEM((LANES, LANES), F32)],
+    )(flag, x0, arrived, mean0, mean1, gain, vg0, vg1, value_w, value_slope, out_part)
     rot_grad, rot_new = call(
         cayley_kernel,
         (shaped((LANES, LANES), F32), shaped((LANES, LANES), F32)),
         (12 * 5 * LANES**3, 8 * LANES**2),
-    )(exchange(jnp.tile(rot_part, (count, 1))), rot)
+    )(exchange(rot_part), rot)
     return rot_grad[None], rot_new[None]
 
 

time: 210 us -> 205 us (0.976)
  blocking collectives: 43.2 us -> 14.3 us
  starting transfers between devices: 26.5 us -> 43.4 us
  waiting for transfers between devices: 5.97 us -> 12.4 us
  other arithmetic: 5.16 us -> 2.65 us
    all_to_all x3 -> x1, blocking collectives: 43.2 us -> 14.3 us  [exchange(): lax.all_to_all(rows, 'tensor', split_axis=0, concat_axis=0, tiled=True)]
    all_to_all x5 -> x7, starting transfers between devices: 23.9 us -> 40.6 us  [exchange(): lax.all_to_all(rows, 'tensor', split_axis=0, concat_axis=0, tiled=True)]
    all_to_all x5 -> x7, waiting for transfers between devices: 3.64 us -> 8.74 us  [exchange(): lax.all_to_all(rows, 'tensor', split_axis=0, concat_axis=0, tiled=True)]
    select_n x2 -> x0, other arithmetic: 2.6 us -> none  [the longest x1 1.83 us: on_device(): jnp.where(is_first, x0, x1)]
    pallas_call x4, Pallas kernels: 27.7 us -> 30.1 us  [the longest x1 12.1 us: on_device(): call(functools.partial(out_grad_kernel, kv_count, half), shaped((LANES, L...]
  transfers between devices with their start and end apart: 7 -> 9, of which waited for: 2 -> 3; matrix products, arithmetic and copies ran while one was open for 3% -> 2% of each run, Pallas kernels for 40% -> 46%
where the time goes in v3:
time: 205 us; the launch traced here: 204 us
  Pallas kernels  121 us (59%)
  starting transfers between devices  43.4 us (21%)
  blocking collectives  14.3 us (7%)
  waiting for transfers between devices  12.4 us (6%)
  local copies, waits for them, and re-layouts  9.51 us (5%)
  other arithmetic  2.65 us (1%)
    pallas_call x2, Pallas kernels, prepare(): call(functools.partial(prep_kernel, kv_count, starts, ends, number), tupl...  50.1 us
    all_to_all x7, starting transfers between devices, exchange(): lax.all_to_all(rows, 'tensor', split_axis=0, concat_axis=0, tiled=True)  40.6 us
    all_to_all x1, blocking collectives, exchange(): lax.all_to_all(rows, 'tensor', split_axis=0, concat_axis=0, tiled=True)  14.3 us
    pallas_call x1, Pallas kernels, on_device(): call(functools.partial(out_grad_kernel, kv_count, half), shaped((LANES, L...  12.1 us
    pallas_call x1, Pallas kernels, on_device(): call(functools.partial(forward_kernel, kv_count), (shaped((tokens, width)...  11.5 us
    pallas_call x1, Pallas kernels, on_device(): call(early_grad_kernel, shaped((LANES, LANES), F32), (big, 2 * local * wi...  10.5 us
    pallas_call x1, Pallas kernels, on_device(): call(back_kernel, shaped((tokens, width), BF16), (big, 2 * local * width)...  9.18 us
    all_to_all x7, waiting for transfers between devices, exchange(): lax.all_to_all(rows, 'tensor', split_axis=0, concat_axis=0, tiled=True)  8.74 us
  transfers between devices with their start and end apart: 9, of which 3 were waited for; matrix products, arithmetic and copies ran while one was open for 2% of the time, Pallas kernels for 46%

profile of v3, /device:TPU:0, one launch (start us, length us, event | category | flops | bytes accessed | tf_op | source)
XLA Modules:
  0.0 203.9 jit_solution(13465791811676705816)
XLA Ops:
  0.6 5.5 %shard_map.86 = (bf16[1024,128]{1,0:T(8,128)(2,1)}, bf16[1024,128]{1,0:T(8,128)(2,1)}, f32[1024,128]{1,0:T(8,128)}, f32[1024,1024]{1,0:T(8,128)}, f32[8,1152]{1,0:T(8,128)}) custom-call(bf16[128,1024]{1,0:T(8,128)(2,1)} %hidden_ref.1, bf16[128,1024]{1,0:T(8,128)(2,1)} %ct_ref.1, f32[1,1024]{1,0:T(1,128)} %gain_row_ref.1, bf16[1024,1024]{1,0:T(8,128)(2,1)} %bitcast.35, ...), custom_call_target="tpu_custom_call" | custom-call | flops 536870912 | bytes 6291456 | tf_op jit(solution)/shard_map/pallas_call | solution.py:484
  6.2 1.4 copy.11
  7.6 7.3 %all-to-all-start = ((f32[8,1,1152]{2,1,0:T(1,128)}), f32[8,1,1152]{2,1,0:T(1,128)S(1)}, u32[]{:S(2)}, u32[]{:S(2)}) async-start(f32[8,1,1152]{2,1,0:T(1,128)} %copy.11), calls=%async_computation | async-start | bytes 73728 | tf_op jit(solution)/shard_map/all_to_all | solution.py:453
  14.8 14.4 %shard_map.88 = (bf16[1024,8192]{1,0:T(8,128)(2,1)}, bf16[1024,8192]{1,0:T(8,128)(2,1)}, bf16[128,8192]{1,0:T(8,128)(2,1)}) custom-call(bf16[1024,8192]{1,0:T(8,128)(2,1)} %bitcast.31, f32[128,128]{1,0:T(8,128)} %bitcast.48, bf16[1024,128]{1,0:T(8,128)(2,1)} %get-tuple-element.33.refs_2_.ct_ref), custom_call_target="tpu_custom_call" | custom-call | flops 21474836480 | bytes 12582912 | tf_op jit(solution)/shard_map/pallas_call | solution.py:552
  29.2 3.3 %reshape_squeeze.3.refs_3_.probs_ref = bf16[2,4096,64]{2,1,0:T(8,128)(2,1)} reshape(bf16[1,2,64,4096]{3,2,1,0:T(8,128)(2,1)S(1)} %copy-done.4) | data formatting | bytes 2097152 | tf_op jit(solution)/shard_map/reshape;squeeze | solution.py:470
  33.2 7.7 %shard_map.87 = (bf16[1024,1024]{1,0:T(8,128)(2,1)}, bf16[1024,1024]{1,0:T(8,128)(2,1)}, bf16[128,1024]{1,0:T(8,128)(2,1)}, f32[1,128]{1,0:T(1,128)}) custom-call(f32[1024,1024]{1,0:T(8,128)} %get-tuple-element.29.turned_ref, f32[8,1152]{1,0:T(8,128)} %bitcast.46, bf16[1024,128]{1,0:T(8,128)(2,1)} %get-tuple-element.28.x_ref.x0_ref, ...), custom_call_target="tpu_custom_call" | custom-call | flops 268435456 | bytes 8388608 | tf_op jit(solution)/shard_map/pallas_call | solution.py:566
  40.9 6.0 %all-to-all-start.1 = ((bf16[8,16,1024]{2,1,0:T(8,128)(2,1)}), bf16[8,16,1024]{2,1,0:T(8,128)(2,1)S(1)}, u32[]{:S(2)}, u32[]{:S(2)}) async-start(bf16[8,16,1024]{2,1,0:T(8,128)(2,1)} %bitcast.44), calls=%async_computation.1 | async-start | bytes 524288 | tf_op jit(solution)/shard_map/all_to_all | solution.py:453
  46.9 35.8 %shard_map.89 = (bf16[1024,8192]{1,0:T(8,128)(2,1)}, bf16[1024,8192]{1,0:T(8,128)(2,1)}, bf16[128,8192]{1,0:T(8,128)(2,1)}, bf16[128,1024]{1,0:T(8,128)(2,1)}) custom-call(bf16[1024,8192]{1,0:T(8,128)(2,1)} %bitcast.32, f32[128,128]{1,0:T(8,128)} %bitcast.49, ...), custom_call_target="tpu_custom_call", output_to_operand_aliasing={{0}: (6, {}), {1}: (7, {})} | custom-call | flops 64424509440 | bytes 37748736 | tf_op jit(solution)/shard_map/pallas_call | solution.py:552
  82.7 0.7 bitcast_select_fusion.1
  83.4 6.0 %all-to-all-start.2 = ((bf16[8,16,1024]{2,1,0:T(8,128)(2,1)}), bf16[8,16,1024]{2,1,0:T(8,128)(2,1)S(1)}, u32[]{:S(2)}, u32[]{:S(2)}) async-start(bf16[8,16,1024]{2,1,0:T(8,128)(2,1)} %bitcast.7), calls=%async_computation.2 | async-start | bytes 524288 | tf_op jit(solution)/shard_map/all_to_all | solution.py:453
  89.4 8.7 %all-to-all-done.2 = bf16[8,16,1024]{2,1,0:T(8,128)(2,1)S(1)} async-done(((bf16[8,16,1024]{2,1,0:T(8,128)(2,1)}), bf16[8,16,1024]{2,1,0:T(8,128)(2,1)S(1)}, u32[]{:S(2)}, u32[]{:S(2)}) %all-to-all-start.2) | async-done | bytes 262176 | tf_op jit(solution)/shard_map/all_to_all | solution.py:453
  98.2 0.8 tile.16
  99.0 3.6 %all-to-all-start.3 = ((bf16[8,16,1024]{2,1,0:T(8,128)(2,1)}), bf16[8,16,1024]{2,1,0:T(8,128)(2,1)S(1)}, u32[]{:S(2)}, u32[]{:S(2)}) async-start(bf16[8,16,1024]{2,1,0:T(8,128)(2,1)} %bitcast.10), calls=%async_computation.3 | async-start | bytes 524288 | tf_op jit(solution)/shard_map/all_to_all | solution.py:453
  102.6 11.5 %shard_map.90 = (bf16[128,8192]{1,0:T(8,128)(2,1)}, bf16[1024,128]{1,0:T(8,128)(2,1)}) custom-call(s32[1]{0:T(128)S(6)} %sub.3.active_ref, bf16[128,1024]{1,0:T(8,128)(2,1)} %bitcast.38, bf16[2,4096,64]{2,1,0:T(8,128)(2,1)} %reshape_squeeze.3.refs_3_.probs_ref, bf16[1024,8192]{1,0:T(8,128)(2,1)} %get-tuple-element.39.q_ref, ...), custom_call_target="tpu_custom_call" | custom-call | flops 2147483648 | bytes 16777216 | tf_op jit(solution)/shard_map/pallas_call | solution.py:618
  114.1 1.5 collective-permute-start
  115.6 1.2 collective-permute-done.arrived_ref.x1_ref
  117.5 2.6 %shard_map.91 = (bf16[128,1152]{1,0:T(8,128)(2,1)}, bf16[1024,128]{1,0:T(8,128)(2,1)}) custom-call(s32[1]{0:T(128)} %bitcast.active_ref.section_ref, bf16[1024,128]{1,0:T(8,128)(2,1)} %get-tuple-element.40.own_ref, bf16[1024,128]{1,0:T(8,128)(2,1)} %copy-done.5, bf16[128,1024]{1,0:T(8,128)(2,1)} %bitcast.39, f32[1024,128]{1,0:T(8,128)} %get-tuple-element.31.gain_ref, ...), custom_call_target="tpu_custom_call" | custom-call | flops 536870912 | bytes 2097152 | tf_op jit(solution)/shard_map/pallas_call | solution.py:635
  120.1 6.0 %all-to-all-start.4 = ((bf16[8,16,1152]{2,1,0:T(8,128)(2,1)}), bf16[8,16,1152]{2,1,0:T(8,128)(2,1)S(1)}, u32[]{:S(2)}, u32[]{:S(2)}) async-start(bf16[8,16,1152]{2,1,0:T(8,128)(2,1)} %bitcast.41), calls=%async_computation.4 | async-start | bytes 589824 | tf_op jit(solution)/shard_map/all_to_all | solution.py:453
  126.1 1.3 collective-permute-start.1
  127.4 2.5 %collective-permute-done.1.grad_ref = bf16[1024,128]{1,0:T(8,128)(2,1)S(1)} collective-permute-done((bf16[1024,128]{1,0:T(8,128)(2,1)}, bf16[1024,128]{1,0:T(8,128)(2,1)S(1)}, u32[]{:S(2)}, u32[]{:S(2)}) %collective-permute-start.1) | collective-permute-done | bytes 262176 | tf_op jit(solution)/shard_map/ppermute | solution.py:654
  130.7 9.2 %shard_map.92.back_ref = bf16[128,8192]{1,0:T(8,128)(2,1)} custom-call(s32[1]{0:T(128)S(6)} %sub.3.active_ref, bf16[1024,8192]{1,0:T(8,128)(2,1)} %get-tuple-element.39.q_ref, bf16[1024,128]{1,0:T(8,128)(2,1)} %copy-done, bf16[128,1152]{1,0:T(8,128)(2,1)} %get-tuple-element.44.after_ref), custom_call_target="tpu_custom_call" | custom-call | flops 2147483648 | bytes 16777216 | tf_op jit(solution)/shard_map/pallas_call | solution.py:655
  140.4 4.1 %shard_map.93 = bf16[128,1024]{1,0:T(8,128)(2,1)} custom-call(s32[1]{0:T(128)S(6)} %sub.3.active_ref, f32[1,128]{1,0:T(1,128)} %copy-done.7, bf16[128,8192]{1,0:T(8,128)(2,1)} %get-tuple-element.45.ct_back_ref, bf16[128,8192]{1,0:T(8,128)(2,1)} %shard_map.92.back_ref, bf16[2,4096,64]{2,1,0:T(8,128)(2,1)} %reshape_squeeze.3.refs_3_.probs_ref), custom_call_target="tpu_custom_call" | custom-call | flops 134217728 | bytes 6291456 | tf_op jit(solution)/shard_map/pallas_call | solution.py:666
  144.5 1.7 bitcast_select_fusion.after_ref
  146.2 5.8 %all-to-all-start.5 = ((bf16[8,16,1024]{2,1,0:T(8,128)(2,1)}), bf16[8,16,1024]{2,1,0:T(8,128)(2,1)S(1)}, u32[]{:S(2)}, u32[]{:S(2)}) async-start(bf16[8,16,1024]{2,1,0:T(8,128)(2,1)} %bitcast.15), calls=%async_computation.5 | async-start | bytes 524288 | tf_op jit(solution)/shard_map/all_to_all | solution.py:453
  152.0 10.5 %shard_map.94.other_ref = f32[128,128]{1,0:T(8,128)} custom-call(s32[1]{0:T(128)} %bitcast.active_ref.section_ref, f32[1,128]{1,0:T(1,128)} %copy-done.7, bf16[128,8192]{1,0:T(8,128)(2,1)} %get-tuple-element.47.mixed_ref.mixed_in_ref, bf16[1024,128]{1,0:T(8,128)(2,1)} %get-tuple-element.33.refs_2_.ct_ref, bf16[1024,128]{1,0:T(8,128)(2,1)} %copy-done, ...), custom_call_target="tpu_custom_call" | custom-call | flops 2147483648 | bytes 16777216 | tf_op jit(solution)/shard_map/pallas_call | solution.py:693
  162.5 0.8 tile.40
  163.3 6.0 %all-to-all-start.6 = ((bf16[8,16,1024]{2,1,0:T(8,128)(2,1)}), bf16[8,16,1024]{2,1,0:T(8,128)(2,1)S(1)}, u32[]{:S(2)}, u32[]{:S(2)}) async-start(bf16[8,16,1024]{2,1,0:T(8,128)(2,1)} %tile.40), calls=%async_computation.6 | async-start | bytes 524288 | tf_op jit(solution)/shard_map/all_to_all | solution.py:453
  169.3 12.1 %shard_map.95.other_ref = f32[128,128]{1,0:T(8,128)} custom-call(s32[1]{0:T(128)} %bitcast.active_ref.section_ref, bf16[128,1024]{1,0:T(8,128)(2,1)} %bitcast.37, f32[1,128]{1,0:T(1,128)} %copy-done.7, bf16[2,4096,64]{2,1,0:T(8,128)(2,1)} %reshape_squeeze.3.refs_3_.probs_ref, bf16[128,8192]{1,0:T(8,128)(2,1)} %get-tuple-element.47.mixed_ref.mixed_in_ref, ...), custom_call_target="tpu_custom_call" | custom-call | flops 4294967296 | bytes 33554432 | tf_op jit(solution)/shard_map/pallas_call | solution.py:719
  181.4 0.7 copy-done.6
  182.1 4.9 %shard_map.96 = bf16[1024,128]{1,0:T(8,128)(2,1)} custom-call(s32[1]{0:T(128)} %bitcast.active_ref.section_ref, bf16[1024,128]{1,0:T(8,128)(2,1)} %get-tuple-element.28.x_ref.x0_ref, bf16[1024,128]{1,0:T(8,128)(2,1)} %copy-done.5, f32[1,128]{1,0:T(1,128)} %get-tuple-element.41.mean0_ref, f32[1,128]{1,0:T(1,128)} %copy-done.7, ...), custom_call_target="tpu_custom_call" | custom-call | flops 536870912 | bytes 4194304 | tf_op jit(solution)/shard_map/pallas_call | solution.py:740
  187.0 14.3 %all_to_all.83 = bf16[8,128,128]{2,1,0:T(8,128)(2,1)} all-to-all(bf16[8,128,128]{2,1,0:T(8,128)(2,1)} %bitcast.43), channel_id=1, replica_groups=mesh['groups'=2,'tensor'=8,'section'=2] {'tensor'}, dimensions={0} | all-to-all | bytes 524288 | tf_op jit(solution)/shard_map/all_to_all | solution.py:453
  201.3 2.6 %shard_map.97 = (f32[128,128]{1,0:T(8,128)}, f32[128,128]{1,0:T(8,128)}) custom-call(bf16[1024,128]{1,0:T(8,128)(2,1)} %bitcast.45, f32[128,128]{1,0:T(8,128)} %bitcast.50), custom_call_target="tpu_custom_call" | custom-call | flops 125829120 | bytes 131072 | tf_op jit(solution)/shard_map/pallas_call | solution.py:761
  (29 shorter events, 2.8 us)
Async XLA Ops:
  7.6 25.0 %all-to-all-start = ((f32[8,1,1152]{2,1,0:T(1,128)}), f32[8,1,1152]{2,1,0:T(1,128)S(1)}, u32[]{:S(2)}, u32[]{:S(2)}) async-start(f32[8,1,1152]{2,1,0:T(1,128)} %copy.11), calls=%async_computation | async-start | bytes 73728 | tf_op jit(solution)/shard_map/all_to_all | solution.py:453
  14.8 14.4 %copy-start.4 = (bf16[1,2,64,4096]{3,2,1,0:T(8,128)(2,1)S(1)}, bf16[1,2,64,4096]{3,2,1,0:T(8,128)(2,1)}, u32[]{:S(2)}) copy-start(bf16[1,2,64,4096]{3,2,1,0:T(8,128)(2,1)} %param.13) | copy-start | bytes 3145732
  40.9 41.8 %all-to-all-start.1 = ((bf16[8,16,1024]{2,1,0:T(8,128)(2,1)}), bf16[8,16,1024]{2,1,0:T(8,128)(2,1)S(1)}, u32[]{:S(2)}, u32[]{:S(2)}) async-start(bf16[8,16,1024]{2,1,0:T(8,128)(2,1)} %bitcast.44), calls=%async_computation.1 | async-start | bytes 524288 | tf_op jit(solution)/shard_map/all_to_all | solution.py:453
  83.4 14.7 %all-to-all-start.2 = ((bf16[8,16,1024]{2,1,0:T(8,128)(2,1)}), bf16[8,16,1024]{2,1,0:T(8,128)(2,1)S(1)}, u32[]{:S(2)}, u32[]{:S(2)}) async-start(bf16[8,16,1024]{2,1,0:T(8,128)(2,1)} %bitcast.7), calls=%async_computation.2 | async-start | bytes 524288 | tf_op jit(solution)/shard_map/all_to_all | solution.py:453
  98.2 4.4 %copy-start.2 = (bf16[8,16,1024]{2,1,0:T(8,128)(2,1)}, bf16[8,16,1024]{2,1,0:T(8,128)(2,1)S(1)}, u32[]{:S(2)}) copy-start(bf16[8,16,1024]{2,1,0:T(8,128)(2,1)S(1)} %all-to-all-done.2) | copy-start | bytes 786436
  99.0 17.7 %all-to-all-start.3 = ((bf16[8,16,1024]{2,1,0:T(8,128)(2,1)}), bf16[8,16,1024]{2,1,0:T(8,128)(2,1)S(1)}, u32[]{:S(2)}, u32[]{:S(2)}) async-start(bf16[8,16,1024]{2,1,0:T(8,128)(2,1)} %bitcast.10), calls=%async_computation.3 | async-start | bytes 524288 | tf_op jit(solution)/shard_map/all_to_all | solution.py:453
  114.1 2.6 %collective-permute-start = (bf16[1024,128]{1,0:T(8,128)(2,1)}, bf16[1024,128]{1,0:T(8,128)(2,1)S(1)}, u32[]{:S(2)}, u32[]{:S(2)}) collective-permute-start(bf16[1024,128]{1,0:T(8,128)(2,1)} %get-tuple-element.40.own_ref), channel_id=1, source_target_pairs={{0,1},{2,3},{4,5},{6,7},{8,9},{10,11},{12,13},{14,15},{16,17},{18,... | collective-permute-start | bytes 786440 | tf_op jit(solution)/shard_map/ppermute | solution.py:632
  116.7 0.7 copy-start.5
  116.7 0.8 copy-start.3
  120.1 19.7 %all-to-all-start.4 = ((bf16[8,16,1152]{2,1,0:T(8,128)(2,1)}), bf16[8,16,1152]{2,1,0:T(8,128)(2,1)S(1)}, u32[]{:S(2)}, u32[]{:S(2)}) async-start(bf16[8,16,1152]{2,1,0:T(8,128)(2,1)} %bitcast.41), calls=%async_computation.4 | async-start | bytes 589824 | tf_op jit(solution)/shard_map/all_to_all | solution.py:453
  126.1 3.8 %collective-permute-start.1 = (bf16[1024,128]{1,0:T(8,128)(2,1)}, bf16[1024,128]{1,0:T(8,128)(2,1)S(1)}, u32[]{:S(2)}, u32[]{:S(2)}) collective-permute-start(bf16[1024,128]{1,0:T(8,128)(2,1)} %get-tuple-element.46), channel_id=1, source_target_pairs={{1,0},{3,2},{5,4},{7,6},{9,8},{11,10},{13,12},{15,14},{17,16},{19,... | collective-permute-start | bytes 786440 | tf_op jit(solution)/shard_map/ppermute | solution.py:654
  130.0 0.7 copy-start
  139.9 0.5 copy-start.7
  146.2 16.3 %all-to-all-start.5 = ((bf16[8,16,1024]{2,1,0:T(8,128)(2,1)}), bf16[8,16,1024]{2,1,0:T(8,128)(2,1)S(1)}, u32[]{:S(2)}, u32[]{:S(2)}) async-start(bf16[8,16,1024]{2,1,0:T(8,128)(2,1)} %bitcast.15), calls=%async_computation.5 | async-start | bytes 524288 | tf_op jit(solution)/shard_map/all_to_all | solution.py:453
  162.5 6.8 %copy-start.1 = (bf16[8,16,1024]{2,1,0:T(8,128)(2,1)}, bf16[8,16,1024]{2,1,0:T(8,128)(2,1)S(1)}, u32[]{:S(2)}) copy-start(bf16[8,16,1024]{2,1,0:T(8,128)(2,1)S(1)} %all-to-all-done.5) | copy-start | bytes 786436
  163.3 18.1 %all-to-all-start.6 = ((bf16[8,16,1024]{2,1,0:T(8,128)(2,1)}), bf16[8,16,1024]{2,1,0:T(8,128)(2,1)S(1)}, u32[]{:S(2)}, u32[]{:S(2)}) async-start(bf16[8,16,1024]{2,1,0:T(8,128)(2,1)} %tile.40), calls=%async_computation.6 | async-start | bytes 524288 | tf_op jit(solution)/shard_map/all_to_all | solution.py:453
  181.4 0.7 copy-start.6

commit v4 on v3

--- a/solution.py
+++ b/solution.py
@@ -333,7 +333,7 @@
 
 
 def out_grad_block(grad, mixed_ref, w_ref, slope_ref, total_ref):
-    width, together = w_ref.shape[1], 8
+    width, together = w_ref.shape[1], 4
     for first in range(0, width, 2 * LANES * together):
         pieces = []
         for at in range(first, min(first + 2 * LANES * together, width), 2 * LANES):
@@ -481,6 +481,7 @@
         return pl.BlockSpec(shape, lambda i: (0,) * len(shape))
 
     rows = min(local, 256)
+    half_rows = max(local // 2, min(local, 128))
     x0, ct, gain, value_rot, stat = call(
         value_rot_kernel,
         (
@@ -491,19 +492,19 @@
             shaped((count, kv_width + tokens), F32),
         ),
         (4 * local * kv_width * LANES, 6 * local * kv_width),
-        grid=(local // rows,),
+        grid=(local // half_rows,),
         in_specs=[
-            across(tokens, rows),
-            across(tokens, rows),
-            across(1, rows),
-            split(rows, kv_width),
+            across(tokens, half_rows),
+            across(tokens, half_rows),
+            across(1, half_rows),
+            split(half_rows, kv_width),
             whole(LANES, LANES),
         ],
         out_specs=(
-            split(rows, tokens),
-            split(rows, tokens),
-            split(rows, tokens),
-            split(rows, kv_width),
+            split(half_rows, tokens),
+            split(half_rows, tokens),
+            split(half_rows, tokens),
+            split(half_rows, kv_width),
             whole(count, kv_width + tokens),
         ),
         scratch_shapes=[pltpu.VMEM((1, kv_width + tokens), F32)],
@@ -572,16 +573,16 @@
             shaped((1, tokens), F32),
         ),
         (2 * local * kv_width * tokens, 8 * local * kv_width),
-        grid=(local // rows,),
+        grid=(local // half_rows,),
         in_specs=[
-            split(rows, kv_width),
+            split(half_rows, kv_width),
             whole(count, kv_width + tokens),
-            split(rows, tokens),
-            split(rows, tokens),
+            split(half_rows, tokens),
+            split(half_rows, tokens),
         ],
         out_specs=(
-            split(rows, kv_width),
-            split(rows, kv_width),
+            split(half_rows, kv_width),
+            split(half_rows, kv_width),
             whole(tokens, kv_width),
             whole(1, tokens),
         ),
@@ -631,7 +632,6 @@
     )(on_first, second, probs, quant, x0)
     arrived = lax.ppermute(x1, "section", [(0, 1)])
 
-    half_rows = max(local // 2, min(local, 128))
     projected, grad1 = call(
         project_kernel,
         (shaped((tokens, kv_width + tokens), BF16), shaped((local, tokens), BF16)),
@@ -686,7 +686,7 @@
     def early(lines, *tail):
         return pl.BlockSpec((lines,) + tail, lambda i, section: (i * (1 - section[0]), 0))
 
-    half = part_count // 2
+    half = local // rows // 2
     pair_total = pltpu.VMEM((2 * LANES, 2 * LANES), F32)
     out_part = jnp.zeros((LANES, LANES), F32)
     if half:
@@ -699,10 +699,10 @@
             in_specs=[
                 fixed(1, tokens),
                 fixed(tokens, width),
-                early(part_rows, tokens),
-                early(part_rows, tokens),
-                early(part_rows, width),
-                early(part_rows, width),
+                early(rows, tokens),
+                early(rows, tokens),
+                early(rows, width),
+                early(rows, width),
                 anywhere,
             ],
             out_specs=fixed(LANES, LANES),
@@ -721,16 +721,16 @@
         shaped((LANES, LANES), F32),
         (2 * big, 4 * local * width),
         prefetch=1,
-        grid=(part_count,),
+        grid=(local // rows,),
         in_specs=[
             fixed(tokens, kv_width),
             fixed(1, tokens),
             fixed(*probs.shape),
             fixed(tokens, width),
-            late(part_rows, tokens),
-            late(part_rows, tokens),
-            late(part_rows, width),
-            late(part_rows, width),
+            late(rows, tokens),
+            late(rows, tokens),
+            late(rows, width),
+            late(rows, width),
             fixed(LANES, LANES),
         ],
         out_specs=fixed(LANES, LANES),

time: 205 us -> 203 us (level)
  no operation moved by 1% of the time
where the time goes in v4:
time: 203 us; the launch traced here: 202 us
  Pallas kernels  119 us (59%)
  starting transfers between devices  43.4 us (21%)
  blocking collectives  14.3 us (7%)
  waiting for transfers between devices  12.4 us (6%)
  local copies, waits for them, and re-layouts  9.51 us (5%)
  other arithmetic  2.65 us (1%)
    pallas_call x2, Pallas kernels, prepare(): call(functools.partial(prep_kernel, kv_count, starts, ends, number), tupl...  50.1 us
    all_to_all x7, starting transfers between devices, exchange(): lax.all_to_all(rows, 'tensor', split_axis=0, concat_axis=0, tiled=True)  40.6 us
    all_to_all x1, blocking collectives, exchange(): lax.all_to_all(rows, 'tensor', split_axis=0, concat_axis=0, tiled=True)  14.3 us
    pallas_call x1, Pallas kernels, on_device(): call(functools.partial(out_grad_kernel, kv_count, half), shaped((LANES, L...  11.7 us
    pallas_call x1, Pallas kernels, on_device(): call(functools.partial(forward_kernel, kv_count), (shaped((tokens, width)...  11.5 us
    pallas_call x1, Pallas kernels, on_device(): call(early_grad_kernel, shaped((LANES, LANES), F32), (big, 2 * local * wi...  9.92 us
    pallas_call x1, Pallas kernels, on_device(): call(back_kernel, shaped((tokens, width), BF16), (big, 2 * local * width)...  9.18 us
    all_to_all x7, waiting for transfers between devices, exchange(): lax.all_to_all(rows, 'tensor', split_axis=0, concat_axis=0, tiled=True)  8.74 us
  transfers between devices with their start and end apart: 9, of which 3 were waited for; matrix products, arithmetic and copies ran while one was open for 2% of the time, Pallas kernels for 46%

profile of v4, /device:TPU:0, one launch (start us, length us, event | category | flops | bytes accessed | tf_op | source)
XLA Modules:
  0.0 201.7 jit_solution(7873507448856266549)
XLA Ops:
  0.6 4.5 %shard_map.86 = (bf16[1024,128]{1,0:T(8,128)(2,1)}, bf16[1024,128]{1,0:T(8,128)(2,1)}, f32[1024,128]{1,0:T(8,128)}, f32[1024,1024]{1,0:T(8,128)}, f32[8,1152]{1,0:T(8,128)}) custom-call(bf16[128,1024]{1,0:T(8,128)(2,1)} %hidden_ref.1, bf16[128,1024]{1,0:T(8,128)(2,1)} %ct_ref.1, f32[1,1024]{1,0:T(1,128)} %gain_row_ref.1, bf16[1024,1024]{1,0:T(8,128)(2,1)} %bitcast.35, ...), custom_call_target="tpu_custom_call" | custom-call | flops 536870912 | bytes 6291456 | tf_op jit(solution)/shard_map/pallas_call | solution.py:485
  5.1 1.4 copy.11
  6.6 7.3 %all-to-all-start = ((f32[8,1,1152]{2,1,0:T(1,128)}), f32[8,1,1152]{2,1,0:T(1,128)S(1)}, u32[]{:S(2)}, u32[]{:S(2)}) async-start(f32[8,1,1152]{2,1,0:T(1,128)} %copy.11), calls=%async_computation | async-start | bytes 73728 | tf_op jit(solution)/shard_map/all_to_all | solution.py:453
  13.8 14.4 %shard_map.88 = (bf16[1024,8192]{1,0:T(8,128)(2,1)}, bf16[1024,8192]{1,0:T(8,128)(2,1)}, bf16[128,8192]{1,0:T(8,128)(2,1)}) custom-call(bf16[1024,8192]{1,0:T(8,128)(2,1)} %bitcast.31, f32[128,128]{1,0:T(8,128)} %bitcast.48, bf16[1024,128]{1,0:T(8,128)(2,1)} %get-tuple-element.33.refs_2_.ct_ref), custom_call_target="tpu_custom_call" | custom-call | flops 21474836480 | bytes 12582912 | tf_op jit(solution)/shard_map/pallas_call | solution.py:553
  28.2 3.3 %reshape_squeeze.3.refs_3_.probs_ref = bf16[2,4096,64]{2,1,0:T(8,128)(2,1)} reshape(bf16[1,2,64,4096]{3,2,1,0:T(8,128)(2,1)S(1)} %copy-done.4) | data formatting | bytes 2097152 | tf_op jit(solution)/shard_map/reshape;squeeze | solution.py:470
  32.1 7.5 %shard_map.87 = (bf16[1024,1024]{1,0:T(8,128)(2,1)}, bf16[1024,1024]{1,0:T(8,128)(2,1)}, bf16[128,1024]{1,0:T(8,128)(2,1)}, f32[1,128]{1,0:T(1,128)}) custom-call(f32[1024,1024]{1,0:T(8,128)} %get-tuple-element.29.turned_ref, f32[8,1152]{1,0:T(8,128)} %bitcast.46, bf16[1024,128]{1,0:T(8,128)(2,1)} %get-tuple-element.28.x_ref.x0_ref, ...), custom_call_target="tpu_custom_call" | custom-call | flops 268435456 | bytes 8388608 | tf_op jit(solution)/shard_map/pallas_call | solution.py:567
  39.6 6.0 %all-to-all-start.1 = ((bf16[8,16,1024]{2,1,0:T(8,128)(2,1)}), bf16[8,16,1024]{2,1,0:T(8,128)(2,1)S(1)}, u32[]{:S(2)}, u32[]{:S(2)}) async-start(bf16[8,16,1024]{2,1,0:T(8,128)(2,1)} %bitcast.44), calls=%async_computation.1 | async-start | bytes 524288 | tf_op jit(solution)/shard_map/all_to_all | solution.py:453
  45.7 35.7 %shard_map.89 = (bf16[1024,8192]{1,0:T(8,128)(2,1)}, bf16[1024,8192]{1,0:T(8,128)(2,1)}, bf16[128,8192]{1,0:T(8,128)(2,1)}, bf16[128,1024]{1,0:T(8,128)(2,1)}) custom-call(bf16[1024,8192]{1,0:T(8,128)(2,1)} %bitcast.32, f32[128,128]{1,0:T(8,128)} %bitcast.49, ...), custom_call_target="tpu_custom_call", output_to_operand_aliasing={{0}: (6, {}), {1}: (7, {})} | custom-call | flops 64424509440 | bytes 37748736 | tf_op jit(solution)/shard_map/pallas_call | solution.py:553
  81.5 0.7 bitcast_select_fusion.1
  82.2 6.0 %all-to-all-start.2 = ((bf16[8,16,1024]{2,1,0:T(8,128)(2,1)}), bf16[8,16,1024]{2,1,0:T(8,128)(2,1)S(1)}, u32[]{:S(2)}, u32[]{:S(2)}) async-start(bf16[8,16,1024]{2,1,0:T(8,128)(2,1)} %bitcast.7), calls=%async_computation.2 | async-start | bytes 524288 | tf_op jit(solution)/shard_map/all_to_all | solution.py:453
  88.2 8.7 %all-to-all-done.2 = bf16[8,16,1024]{2,1,0:T(8,128)(2,1)S(1)} async-done(((bf16[8,16,1024]{2,1,0:T(8,128)(2,1)}), bf16[8,16,1024]{2,1,0:T(8,128)(2,1)S(1)}, u32[]{:S(2)}, u32[]{:S(2)}) %all-to-all-start.2) | async-done | bytes 262176 | tf_op jit(solution)/shard_map/all_to_all | solution.py:453
  97.0 0.8 tile.16
  97.7 3.6 %all-to-all-start.3 = ((bf16[8,16,1024]{2,1,0:T(8,128)(2,1)}), bf16[8,16,1024]{2,1,0:T(8,128)(2,1)S(1)}, u32[]{:S(2)}, u32[]{:S(2)}) async-start(bf16[8,16,1024]{2,1,0:T(8,128)(2,1)} %bitcast.10), calls=%async_computation.3 | async-start | bytes 524288 | tf_op jit(solution)/shard_map/all_to_all | solution.py:453
  101.3 11.5 %shard_map.90 = (bf16[128,8192]{1,0:T(8,128)(2,1)}, bf16[1024,128]{1,0:T(8,128)(2,1)}) custom-call(s32[1]{0:T(128)S(6)} %sub.3.active_ref, bf16[128,1024]{1,0:T(8,128)(2,1)} %bitcast.38, bf16[2,4096,64]{2,1,0:T(8,128)(2,1)} %reshape_squeeze.3.refs_3_.probs_ref, bf16[1024,8192]{1,0:T(8,128)(2,1)} %get-tuple-element.39.q_ref, ...), custom_call_target="tpu_custom_call" | custom-call | flops 2147483648 | bytes 16777216 | tf_op jit(solution)/shard_map/pallas_call | solution.py:619
  112.8 1.5 collective-permute-start
  114.3 1.2 collective-permute-done.arrived_ref.x1_ref
  116.3 2.6 %shard_map.91 = (bf16[128,1152]{1,0:T(8,128)(2,1)}, bf16[1024,128]{1,0:T(8,128)(2,1)}) custom-call(s32[1]{0:T(128)} %bitcast.active_ref.section_ref, bf16[1024,128]{1,0:T(8,128)(2,1)} %get-tuple-element.40.own_ref, bf16[1024,128]{1,0:T(8,128)(2,1)} %copy-done.5, bf16[128,1024]{1,0:T(8,128)(2,1)} %bitcast.39, f32[1024,128]{1,0:T(8,128)} %get-tuple-element.31.gain_ref, ...), custom_call_target="tpu_custom_call" | custom-call | flops 536870912 | bytes 2097152 | tf_op jit(solution)/shard_map/pallas_call | solution.py:635
  118.9 6.0 %all-to-all-start.4 = ((bf16[8,16,1152]{2,1,0:T(8,128)(2,1)}), bf16[8,16,1152]{2,1,0:T(8,128)(2,1)S(1)}, u32[]{:S(2)}, u32[]{:S(2)}) async-start(bf16[8,16,1152]{2,1,0:T(8,128)(2,1)} %bitcast.41), calls=%async_computation.4 | async-start | bytes 589824 | tf_op jit(solution)/shard_map/all_to_all | solution.py:453
  124.9 1.3 collective-permute-start.1
  126.2 2.5 %collective-permute-done.1.grad_ref = bf16[1024,128]{1,0:T(8,128)(2,1)S(1)} collective-permute-done((bf16[1024,128]{1,0:T(8,128)(2,1)}, bf16[1024,128]{1,0:T(8,128)(2,1)S(1)}, u32[]{:S(2)}, u32[]{:S(2)}) %collective-permute-start.1) | collective-permute-done | bytes 262176 | tf_op jit(solution)/shard_map/ppermute | solution.py:654
  129.4 9.2 %shard_map.92.back_ref = bf16[128,8192]{1,0:T(8,128)(2,1)} custom-call(s32[1]{0:T(128)S(6)} %sub.3.active_ref, bf16[1024,8192]{1,0:T(8,128)(2,1)} %get-tuple-element.39.q_ref, bf16[1024,128]{1,0:T(8,128)(2,1)} %copy-done, bf16[128,1152]{1,0:T(8,128)(2,1)} %get-tuple-element.44.after_ref), custom_call_target="tpu_custom_call" | custom-call | flops 2147483648 | bytes 16777216 | tf_op jit(solution)/shard_map/pallas_call | solution.py:655
  139.1 4.1 %shard_map.93 = bf16[128,1024]{1,0:T(8,128)(2,1)} custom-call(s32[1]{0:T(128)S(6)} %sub.3.active_ref, f32[1,128]{1,0:T(1,128)} %copy-done.7, bf16[128,8192]{1,0:T(8,128)(2,1)} %get-tuple-element.45.ct_back_ref, bf16[128,8192]{1,0:T(8,128)(2,1)} %shard_map.92.back_ref, bf16[2,4096,64]{2,1,0:T(8,128)(2,1)} %reshape_squeeze.3.refs_3_.probs_ref), custom_call_target="tpu_custom_call" | custom-call | flops 134217728 | bytes 6291456 | tf_op jit(solution)/shard_map/pallas_call | solution.py:666
  143.3 1.7 bitcast_select_fusion.after_ref
  144.9 5.8 %all-to-all-start.5 = ((bf16[8,16,1024]{2,1,0:T(8,128)(2,1)}), bf16[8,16,1024]{2,1,0:T(8,128)(2,1)S(1)}, u32[]{:S(2)}, u32[]{:S(2)}) async-start(bf16[8,16,1024]{2,1,0:T(8,128)(2,1)} %bitcast.15), calls=%async_computation.5 | async-start | bytes 524288 | tf_op jit(solution)/shard_map/all_to_all | solution.py:453
  150.7 9.9 %shard_map.94.other_ref = f32[128,128]{1,0:T(8,128)} custom-call(s32[1]{0:T(128)} %bitcast.active_ref.section_ref, f32[1,128]{1,0:T(1,128)} %copy-done.7, bf16[128,8192]{1,0:T(8,128)(2,1)} %get-tuple-element.47.mixed_ref.mixed_in_ref, bf16[1024,128]{1,0:T(8,128)(2,1)} %get-tuple-element.33.refs_2_.ct_ref, bf16[1024,128]{1,0:T(8,128)(2,1)} %copy-done, ...), custom_call_target="tpu_custom_call" | custom-call | flops 2147483648 | bytes 16777216 | tf_op jit(solution)/shard_map/pallas_call | solution.py:693
  160.7 0.8 tile.40
  161.5 6.0 %all-to-all-start.6 = ((bf16[8,16,1024]{2,1,0:T(8,128)(2,1)}), bf16[8,16,1024]{2,1,0:T(8,128)(2,1)S(1)}, u32[]{:S(2)}, u32[]{:S(2)}) async-start(bf16[8,16,1024]{2,1,0:T(8,128)(2,1)} %tile.40), calls=%async_computation.6 | async-start | bytes 524288 | tf_op jit(solution)/shard_map/all_to_all | solution.py:453
  167.5 11.7 %shard_map.95.other_ref = f32[128,128]{1,0:T(8,128)} custom-call(s32[1]{0:T(128)} %bitcast.active_ref.section_ref, bf16[128,1024]{1,0:T(8,128)(2,1)} %bitcast.37, f32[1,128]{1,0:T(1,128)} %copy-done.7, bf16[2,4096,64]{2,1,0:T(8,128)(2,1)} %reshape_squeeze.3.refs_3_.probs_ref, bf16[128,8192]{1,0:T(8,128)(2,1)} %get-tuple-element.47.mixed_ref.mixed_in_ref, ...), custom_call_target="tpu_custom_call" | custom-call | flops 4294967296 | bytes 33554432 | tf_op jit(solution)/shard_map/pallas_call | solution.py:719
  179.2 0.7 copy-done.6
  179.9 4.9 %shard_map.96 = bf16[1024,128]{1,0:T(8,128)(2,1)} custom-call(s32[1]{0:T(128)} %bitcast.active_ref.section_ref, bf16[1024,128]{1,0:T(8,128)(2,1)} %get-tuple-element.28.x_ref.x0_ref, bf16[1024,128]{1,0:T(8,128)(2,1)} %copy-done.5, f32[1,128]{1,0:T(1,128)} %get-tuple-element.41.mean0_ref, f32[1,128]{1,0:T(1,128)} %copy-done.7, ...), custom_call_target="tpu_custom_call" | custom-call | flops 536870912 | bytes 4194304 | tf_op jit(solution)/shard_map/pallas_call | solution.py:740
  184.8 14.3 %all_to_all.83 = bf16[8,128,128]{2,1,0:T(8,128)(2,1)} all-to-all(bf16[8,128,128]{2,1,0:T(8,128)(2,1)} %bitcast.43), channel_id=1, replica_groups=mesh['groups'=2,'tensor'=8,'section'=2] {'tensor'}, dimensions={0} | all-to-all | bytes 524288 | tf_op jit(solution)/shard_map/all_to_all | solution.py:453
  199.1 2.6 %shard_map.97 = (f32[128,128]{1,0:T(8,128)}, f32[128,128]{1,0:T(8,128)}) custom-call(bf16[1024,128]{1,0:T(8,128)(2,1)} %bitcast.45, f32[128,128]{1,0:T(8,128)} %bitcast.50), custom_call_target="tpu_custom_call" | custom-call | flops 125829120 | bytes 131072 | tf_op jit(solution)/shard_map/pallas_call | solution.py:761
  (29 shorter events, 2.8 us)
Async XLA Ops:
  6.6 25.0 %all-to-all-start = ((f32[8,1,1152]{2,1,0:T(1,128)}), f32[8,1,1152]{2,1,0:T(1,128)S(1)}, u32[]{:S(2)}, u32[]{:S(2)}) async-start(f32[8,1,1152]{2,1,0:T(1,128)} %copy.11), calls=%async_computation | async-start | bytes 73728 | tf_op jit(solution)/shard_map/all_to_all | solution.py:453
  13.8 14.4 %copy-start.4 = (bf16[1,2,64,4096]{3,2,1,0:T(8,128)(2,1)S(1)}, bf16[1,2,64,4096]{3,2,1,0:T(8,128)(2,1)}, u32[]{:S(2)}) copy-start(bf16[1,2,64,4096]{3,2,1,0:T(8,128)(2,1)} %param.13) | copy-start | bytes 3145732
  39.6 41.8 %all-to-all-start.1 = ((bf16[8,16,1024]{2,1,0:T(8,128)(2,1)}), bf16[8,16,1024]{2,1,0:T(8,128)(2,1)S(1)}, u32[]{:S(2)}, u32[]{:S(2)}) async-start(bf16[8,16,1024]{2,1,0:T(8,128)(2,1)} %bitcast.44), calls=%async_computation.1 | async-start | bytes 524288 | tf_op jit(solution)/shard_map/all_to_all | solution.py:453
  82.2 14.7 %all-to-all-start.2 = ((bf16[8,16,1024]{2,1,0:T(8,128)(2,1)}), bf16[8,16,1024]{2,1,0:T(8,128)(2,1)S(1)}, u32[]{:S(2)}, u32[]{:S(2)}) async-start(bf16[8,16,1024]{2,1,0:T(8,128)(2,1)} %bitcast.7), calls=%async_computation.2 | async-start | bytes 524288 | tf_op jit(solution)/shard_map/all_to_all | solution.py:453
  96.9 4.4 %copy-start.2 = (bf16[8,16,1024]{2,1,0:T(8,128)(2,1)}, bf16[8,16,1024]{2,1,0:T(8,128)(2,1)S(1)}, u32[]{:S(2)}) copy-start(bf16[8,16,1024]{2,1,0:T(8,128)(2,1)S(1)} %all-to-all-done.2) | copy-start | bytes 786436
  97.7 17.7 %all-to-all-start.3 = ((bf16[8,16,1024]{2,1,0:T(8,128)(2,1)}), bf16[8,16,1024]{2,1,0:T(8,128)(2,1)S(1)}, u32[]{:S(2)}, u32[]{:S(2)}) async-start(bf16[8,16,1024]{2,1,0:T(8,128)(2,1)} %bitcast.10), calls=%async_computation.3 | async-start | bytes 524288 | tf_op jit(solution)/shard_map/all_to_all | solution.py:453
  112.8 2.6 %collective-permute-start = (bf16[1024,128]{1,0:T(8,128)(2,1)}, bf16[1024,128]{1,0:T(8,128)(2,1)S(1)}, u32[]{:S(2)}, u32[]{:S(2)}) collective-permute-start(bf16[1024,128]{1,0:T(8,128)(2,1)} %get-tuple-element.40.own_ref), channel_id=1, source_target_pairs={{0,1},{2,3},{4,5},{6,7},{8,9},{10,11},{12,13},{14,15},{16,17},{18,... | collective-permute-start | bytes 786440 | tf_op jit(solution)/shard_map/ppermute | solution.py:633
  115.5 0.7 copy-start.5
  115.5 0.8 copy-start.3
  118.9 19.7 %all-to-all-start.4 = ((bf16[8,16,1152]{2,1,0:T(8,128)(2,1)}), bf16[8,16,1152]{2,1,0:T(8,128)(2,1)S(1)}, u32[]{:S(2)}, u32[]{:S(2)}) async-start(bf16[8,16,1152]{2,1,0:T(8,128)(2,1)} %bitcast.41), calls=%async_computation.4 | async-start | bytes 589824 | tf_op jit(solution)/shard_map/all_to_all | solution.py:453
  124.9 3.8 %collective-permute-start.1 = (bf16[1024,128]{1,0:T(8,128)(2,1)}, bf16[1024,128]{1,0:T(8,128)(2,1)S(1)}, u32[]{:S(2)}, u32[]{:S(2)}) collective-permute-start(bf16[1024,128]{1,0:T(8,128)(2,1)} %get-tuple-element.46), channel_id=1, source_target_pairs={{1,0},{3,2},{5,4},{7,6},{9,8},{11,10},{13,12},{15,14},{17,16},{19,... | collective-permute-start | bytes 786440 | tf_op jit(solution)/shard_map/ppermute | solution.py:654
  128.7 0.7 copy-start
  138.7 0.5 copy-start.7
  144.9 15.7 %all-to-all-start.5 = ((bf16[8,16,1024]{2,1,0:T(8,128)(2,1)}), bf16[8,16,1024]{2,1,0:T(8,128)(2,1)S(1)}, u32[]{:S(2)}, u32[]{:S(2)}) async-start(bf16[8,16,1024]{2,1,0:T(8,128)(2,1)} %bitcast.15), calls=%async_computation.5 | async-start | bytes 524288 | tf_op jit(solution)/shard_map/all_to_all | solution.py:453
  160.7 6.8 %copy-start.1 = (bf16[8,16,1024]{2,1,0:T(8,128)(2,1)}, bf16[8,16,1024]{2,1,0:T(8,128)(2,1)S(1)}, u32[]{:S(2)}) copy-start(bf16[8,16,1024]{2,1,0:T(8,128)(2,1)S(1)} %all-to-all-done.5) | copy-start | bytes 786436
  161.5 17.7 %all-to-all-start.6 = ((bf16[8,16,1024]{2,1,0:T(8,128)(2,1)}), bf16[8,16,1024]{2,1,0:T(8,128)(2,1)S(1)}, u32[]{:S(2)}, u32[]{:S(2)}) async-start(bf16[8,16,1024]{2,1,0:T(8,128)(2,1)} %tile.40), calls=%async_computation.6 | async-start | bytes 524288 | tf_op jit(solution)/shard_map/all_to_all | solution.py:453
  179.2 0.7 copy-start.6

commit v5 on v4

--- a/solution.py
+++ b/solution.py
@@ -511,7 +511,7 @@
     )(hidden, cotangent, norm_gain, value_w, rot)
     stats = exchange(stat)
 
-    part_rows = min(local, 128)
+    part_rows = min(local, 256)
     part_count = local // part_rows
 
     def prepare(first, number, before):

time: 203 us -> 202 us (level)
  no operation moved by 1% of the time
where the time goes in v5:
time: 202 us; the launch traced here: 201 us
  Pallas kernels  118 us (58%)
  starting transfers between devices  43.2 us (21%)
  blocking collectives  14.3 us (7%)
  waiting for transfers between devices  12.6 us (6%)
  local copies, waits for them, and re-layouts  9.5 us (5%)
  other arithmetic  2.65 us (1%)
    pallas_call x2, Pallas kernels, prepare(): call(functools.partial(prep_kernel, kv_count, starts, ends, number), tupl...  49.1 us
    all_to_all x7, starting transfers between devices, exchange(): lax.all_to_all(rows, 'tensor', split_axis=0, concat_axis=0, tiled=True)  40.6 us
    all_to_all x1, blocking collectives, exchange(): lax.all_to_all(rows, 'tensor', split_axis=0, concat_axis=0, tiled=True)  14.3 us
    pallas_call x1, Pallas kernels, on_device(): call(functools.partial(out_grad_kernel, kv_count, half), shaped((LANES, L...  11.7 us
    pallas_call x1, Pallas kernels, on_device(): call(functools.partial(forward_kernel, kv_count), (shaped((tokens, width)...  11.5 us
    pallas_call x1, Pallas kernels, on_device(): call(early_grad_kernel, shaped((LANES, LANES), F32), (big, 2 * local * wi...  9.92 us
    pallas_call x1, Pallas kernels, on_device(): call(back_kernel, shaped((tokens, width), BF16), (big, 2 * local * width)...  9.18 us
    all_to_all x7, waiting for transfers between devices, exchange(): lax.all_to_all(rows, 'tensor', split_axis=0, concat_axis=0, tiled=True)  8.75 us
  transfers between devices with their start and end apart: 9, of which 3 were waited for; matrix products, arithmetic and copies ran while one was open for 2% of the time, Pallas kernels for 46%

profile of v5, /device:TPU:0, one launch (start us, length us, event | category | flops | bytes accessed | tf_op | source)
XLA Modules:
  0.0 200.6 jit_solution(17266566509152411269)
XLA Ops:
  0.6 4.5 %shard_map.86 = (bf16[1024,128]{1,0:T(8,128)(2,1)}, bf16[1024,128]{1,0:T(8,128)(2,1)}, f32[1024,128]{1,0:T(8,128)}, f32[1024,1024]{1,0:T(8,128)}, f32[8,1152]{1,0:T(8,128)}) custom-call(bf16[128,1024]{1,0:T(8,128)(2,1)} %hidden_ref.1, bf16[128,1024]{1,0:T(8,128)(2,1)} %ct_ref.1, f32[1,1024]{1,0:T(1,128)} %gain_row_ref.1, bf16[1024,1024]{1,0:T(8,128)(2,1)} %bitcast.35, ...), custom_call_target="tpu_custom_call" | custom-call | flops 536870912 | bytes 6291456 | tf_op jit(solution)/shard_map/pallas_call | solution.py:485
  5.1 1.4 copy.11
  6.6 7.3 %all-to-all-start = ((f32[8,1,1152]{2,1,0:T(1,128)}), f32[8,1,1152]{2,1,0:T(1,128)S(1)}, u32[]{:S(2)}, u32[]{:S(2)}) async-start(f32[8,1,1152]{2,1,0:T(1,128)} %copy.11), calls=%async_computation | async-start | bytes 73728 | tf_op jit(solution)/shard_map/all_to_all | solution.py:453
  13.8 14.3 %shard_map.88 = (bf16[1024,8192]{1,0:T(8,128)(2,1)}, bf16[1024,8192]{1,0:T(8,128)(2,1)}, bf16[128,8192]{1,0:T(8,128)(2,1)}) custom-call(bf16[1024,8192]{1,0:T(8,128)(2,1)} %bitcast.31, f32[128,128]{1,0:T(8,128)} %bitcast.48, bf16[1024,128]{1,0:T(8,128)(2,1)} %get-tuple-element.33.refs_2_.ct_ref), custom_call_target="tpu_custom_call" | custom-call | flops 21474836480 | bytes 12582912 | tf_op jit(solution)/shard_map/pallas_call | solution.py:553
  28.1 3.3 %reshape_squeeze.3.refs_3_.probs_ref = bf16[2,4096,64]{2,1,0:T(8,128)(2,1)} reshape(bf16[1,2,64,4096]{3,2,1,0:T(8,128)(2,1)S(1)} %copy-done.4) | data formatting | bytes 2097152 | tf_op jit(solution)/shard_map/reshape;squeeze | solution.py:470
  32.0 7.5 %shard_map.87 = (bf16[1024,1024]{1,0:T(8,128)(2,1)}, bf16[1024,1024]{1,0:T(8,128)(2,1)}, bf16[128,1024]{1,0:T(8,128)(2,1)}, f32[1,128]{1,0:T(1,128)}) custom-call(f32[1024,1024]{1,0:T(8,128)} %get-tuple-element.29.turned_ref, f32[8,1152]{1,0:T(8,128)} %bitcast.46, bf16[1024,128]{1,0:T(8,128)(2,1)} %get-tuple-element.28.x_ref.x0_ref, ...), custom_call_target="tpu_custom_call" | custom-call | flops 268435456 | bytes 8388608 | tf_op jit(solution)/shard_map/pallas_call | solution.py:567
  39.5 6.0 %all-to-all-start.1 = ((bf16[8,16,1024]{2,1,0:T(8,128)(2,1)}), bf16[8,16,1024]{2,1,0:T(8,128)(2,1)S(1)}, u32[]{:S(2)}, u32[]{:S(2)}) async-start(bf16[8,16,1024]{2,1,0:T(8,128)(2,1)} %bitcast.44), calls=%async_computation.1 | async-start | bytes 524288 | tf_op jit(solution)/shard_map/all_to_all | solution.py:453
  45.5 34.8 %shard_map.89 = (bf16[1024,8192]{1,0:T(8,128)(2,1)}, bf16[1024,8192]{1,0:T(8,128)(2,1)}, bf16[128,8192]{1,0:T(8,128)(2,1)}, bf16[128,1024]{1,0:T(8,128)(2,1)}) custom-call(bf16[1024,8192]{1,0:T(8,128)(2,1)} %bitcast.32, f32[128,128]{1,0:T(8,128)} %bitcast.49, ...), custom_call_target="tpu_custom_call", output_to_operand_aliasing={{0}: (6, {}), {1}: (7, {})} | custom-call | flops 64424509440 | bytes 37748736 | tf_op jit(solution)/shard_map/pallas_call | solution.py:553
  80.4 0.7 bitcast_select_fusion.1
  81.1 6.0 %all-to-all-start.2 = ((bf16[8,16,1024]{2,1,0:T(8,128)(2,1)}), bf16[8,16,1024]{2,1,0:T(8,128)(2,1)S(1)}, u32[]{:S(2)}, u32[]{:S(2)}) async-start(bf16[8,16,1024]{2,1,0:T(8,128)(2,1)} %bitcast.7), calls=%async_computation.2 | async-start | bytes 524288 | tf_op jit(solution)/shard_map/all_to_all | solution.py:453
  87.1 8.7 %all-to-all-done.2 = bf16[8,16,1024]{2,1,0:T(8,128)(2,1)S(1)} async-done(((bf16[8,16,1024]{2,1,0:T(8,128)(2,1)}), bf16[8,16,1024]{2,1,0:T(8,128)(2,1)S(1)}, u32[]{:S(2)}, u32[]{:S(2)}) %all-to-all-start.2) | async-done | bytes 262176 | tf_op jit(solution)/shard_map/all_to_all | solution.py:453
  95.9 0.8 tile.16
  96.7 3.6 %all-to-all-start.3 = ((bf16[8,16,1024]{2,1,0:T(8,128)(2,1)}), bf16[8,16,1024]{2,1,0:T(8,128)(2,1)S(1)}, u32[]{:S(2)}, u32[]{:S(2)}) async-start(bf16[8,16,1024]{2,1,0:T(8,128)(2,1)} %bitcast.10), calls=%async_computation.3 | async-start | bytes 524288 | tf_op jit(solution)/shard_map/all_to_all | solution.py:453
  100.3 11.5 %shard_map.90 = (bf16[128,8192]{1,0:T(8,128)(2,1)}, bf16[1024,128]{1,0:T(8,128)(2,1)}) custom-call(s32[1]{0:T(128)S(6)} %sub.3.active_ref, bf16[128,1024]{1,0:T(8,128)(2,1)} %bitcast.38, bf16[2,4096,64]{2,1,0:T(8,128)(2,1)} %reshape_squeeze.3.refs_3_.probs_ref, bf16[1024,8192]{1,0:T(8,128)(2,1)} %get-tuple-element.39.q_ref, ...), custom_call_target="tpu_custom_call" | custom-call | flops 2147483648 | bytes 16777216 | tf_op jit(solution)/shard_map/pallas_call | solution.py:619
  111.8 1.3 collective-permute-start
  113.1 1.3 collective-permute-done.arrived_ref.x1_ref
  115.2 2.6 %shard_map.91 = (bf16[128,1152]{1,0:T(8,128)(2,1)}, bf16[1024,128]{1,0:T(8,128)(2,1)}) custom-call(s32[1]{0:T(128)} %bitcast.active_ref.section_ref, bf16[1024,128]{1,0:T(8,128)(2,1)} %get-tuple-element.40.own_ref, bf16[1024,128]{1,0:T(8,128)(2,1)} %copy-done.5, bf16[128,1024]{1,0:T(8,128)(2,1)} %bitcast.39, f32[1024,128]{1,0:T(8,128)} %get-tuple-element.31.gain_ref, ...), custom_call_target="tpu_custom_call" | custom-call | flops 536870912 | bytes 2097152 | tf_op jit(solution)/shard_map/pallas_call | solution.py:635
  117.8 6.0 %all-to-all-start.4 = ((bf16[8,16,1152]{2,1,0:T(8,128)(2,1)}), bf16[8,16,1152]{2,1,0:T(8,128)(2,1)S(1)}, u32[]{:S(2)}, u32[]{:S(2)}) async-start(bf16[8,16,1152]{2,1,0:T(8,128)(2,1)} %bitcast.41), calls=%async_computation.4 | async-start | bytes 589824 | tf_op jit(solution)/shard_map/all_to_all | solution.py:453
  123.8 1.3 collective-permute-start.1
  125.1 2.5 %collective-permute-done.1.grad_ref = bf16[1024,128]{1,0:T(8,128)(2,1)S(1)} collective-permute-done((bf16[1024,128]{1,0:T(8,128)(2,1)}, bf16[1024,128]{1,0:T(8,128)(2,1)S(1)}, u32[]{:S(2)}, u32[]{:S(2)}) %collective-permute-start.1) | collective-permute-done | bytes 262176 | tf_op jit(solution)/shard_map/ppermute | solution.py:654
  128.3 9.2 %shard_map.92.back_ref = bf16[128,8192]{1,0:T(8,128)(2,1)} custom-call(s32[1]{0:T(128)S(6)} %sub.3.active_ref, bf16[1024,8192]{1,0:T(8,128)(2,1)} %get-tuple-element.39.q_ref, bf16[1024,128]{1,0:T(8,128)(2,1)} %copy-done, bf16[128,1152]{1,0:T(8,128)(2,1)} %get-tuple-element.44.after_ref), custom_call_target="tpu_custom_call" | custom-call | flops 2147483648 | bytes 16777216 | tf_op jit(solution)/shard_map/pallas_call | solution.py:655
  138.1 4.1 %shard_map.93 = bf16[128,1024]{1,0:T(8,128)(2,1)} custom-call(s32[1]{0:T(128)S(6)} %sub.3.active_ref, f32[1,128]{1,0:T(1,128)} %copy-done.7, bf16[128,8192]{1,0:T(8,128)(2,1)} %get-tuple-element.45.ct_back_ref, bf16[128,8192]{1,0:T(8,128)(2,1)} %shard_map.92.back_ref, bf16[2,4096,64]{2,1,0:T(8,128)(2,1)} %reshape_squeeze.3.refs_3_.probs_ref), custom_call_target="tpu_custom_call" | custom-call | flops 134217728 | bytes 6291456 | tf_op jit(solution)/shard_map/pallas_call | solution.py:666
  142.2 1.7 bitcast_select_fusion.after_ref
  143.9 5.8 %all-to-all-start.5 = ((bf16[8,16,1024]{2,1,0:T(8,128)(2,1)}), bf16[8,16,1024]{2,1,0:T(8,128)(2,1)S(1)}, u32[]{:S(2)}, u32[]{:S(2)}) async-start(bf16[8,16,1024]{2,1,0:T(8,128)(2,1)} %bitcast.15), calls=%async_computation.5 | async-start | bytes 524288 | tf_op jit(solution)/shard_map/all_to_all | solution.py:453
  149.6 9.9 %shard_map.94.other_ref = f32[128,128]{1,0:T(8,128)} custom-call(s32[1]{0:T(128)} %bitcast.active_ref.section_ref, f32[1,128]{1,0:T(1,128)} %copy-done.7, bf16[128,8192]{1,0:T(8,128)(2,1)} %get-tuple-element.47.mixed_ref.mixed_in_ref, bf16[1024,128]{1,0:T(8,128)(2,1)} %get-tuple-element.33.refs_2_.ct_ref, bf16[1024,128]{1,0:T(8,128)(2,1)} %copy-done, ...), custom_call_target="tpu_custom_call" | custom-call | flops 2147483648 | bytes 16777216 | tf_op jit(solution)/shard_map/pallas_call | solution.py:693
  159.6 0.8 tile.40
  160.4 6.0 %all-to-all-start.6 = ((bf16[8,16,1024]{2,1,0:T(8,128)(2,1)}), bf16[8,16,1024]{2,1,0:T(8,128)(2,1)S(1)}, u32[]{:S(2)}, u32[]{:S(2)}) async-start(bf16[8,16,1024]{2,1,0:T(8,128)(2,1)} %tile.40), calls=%async_computation.6 | async-start | bytes 524288 | tf_op jit(solution)/shard_map/all_to_all | solution.py:453
  166.4 11.7 %shard_map.95.other_ref = f32[128,128]{1,0:T(8,128)} custom-call(s32[1]{0:T(128)} %bitcast.active_ref.section_ref, bf16[128,1024]{1,0:T(8,128)(2,1)} %bitcast.37, f32[1,128]{1,0:T(1,128)} %copy-done.7, bf16[2,4096,64]{2,1,0:T(8,128)(2,1)} %reshape_squeeze.3.refs_3_.probs_ref, bf16[128,8192]{1,0:T(8,128)(2,1)} %get-tuple-element.47.mixed_ref.mixed_in_ref, ...), custom_call_target="tpu_custom_call" | custom-call | flops 4294967296 | bytes 33554432 | tf_op jit(solution)/shard_map/pallas_call | solution.py:719
  178.1 0.7 copy-done.6
  178.8 4.9 %shard_map.96 = bf16[1024,128]{1,0:T(8,128)(2,1)} custom-call(s32[1]{0:T(128)} %bitcast.active_ref.section_ref, bf16[1024,128]{1,0:T(8,128)(2,1)} %get-tuple-element.28.x_ref.x0_ref, bf16[1024,128]{1,0:T(8,128)(2,1)} %copy-done.5, f32[1,128]{1,0:T(1,128)} %get-tuple-element.41.mean0_ref, f32[1,128]{1,0:T(1,128)} %copy-done.7, ...), custom_call_target="tpu_custom_call" | custom-call | flops 536870912 | bytes 4194304 | tf_op jit(solution)/shard_map/pallas_call | solution.py:740
  183.7 14.3 %all_to_all.83 = bf16[8,128,128]{2,1,0:T(8,128)(2,1)} all-to-all(bf16[8,128,128]{2,1,0:T(8,128)(2,1)} %bitcast.43), channel_id=1, replica_groups=mesh['groups'=2,'tensor'=8,'section'=2] {'tensor'}, dimensions={0} | all-to-all | bytes 524288 | tf_op jit(solution)/shard_map/all_to_all | solution.py:453
  198.0 2.6 %shard_map.97 = (f32[128,128]{1,0:T(8,128)}, f32[128,128]{1,0:T(8,128)}) custom-call(bf16[1024,128]{1,0:T(8,128)(2,1)} %bitcast.45, f32[128,128]{1,0:T(8,128)} %bitcast.50), custom_call_target="tpu_custom_call" | custom-call | flops 125829120 | bytes 131072 | tf_op jit(solution)/shard_map/pallas_call | solution.py:761
  (29 shorter events, 2.8 us)
Async XLA Ops:
  6.6 24.9 %all-to-all-start = ((f32[8,1,1152]{2,1,0:T(1,128)}), f32[8,1,1152]{2,1,0:T(1,128)S(1)}, u32[]{:S(2)}, u32[]{:S(2)}) async-start(f32[8,1,1152]{2,1,0:T(1,128)} %copy.11), calls=%async_computation | async-start | bytes 73728 | tf_op jit(solution)/shard_map/all_to_all | solution.py:453
  13.8 14.3 %copy-start.4 = (bf16[1,2,64,4096]{3,2,1,0:T(8,128)(2,1)S(1)}, bf16[1,2,64,4096]{3,2,1,0:T(8,128)(2,1)}, u32[]{:S(2)}) copy-start(bf16[1,2,64,4096]{3,2,1,0:T(8,128)(2,1)} %param.13) | copy-start | bytes 3145732
  39.5 40.8 %all-to-all-start.1 = ((bf16[8,16,1024]{2,1,0:T(8,128)(2,1)}), bf16[8,16,1024]{2,1,0:T(8,128)(2,1)S(1)}, u32[]{:S(2)}, u32[]{:S(2)}) async-start(bf16[8,16,1024]{2,1,0:T(8,128)(2,1)} %bitcast.44), calls=%async_computation.1 | async-start | bytes 524288 | tf_op jit(solution)/shard_map/all_to_all | solution.py:453
  81.1 14.7 %all-to-all-start.2 = ((bf16[8,16,1024]{2,1,0:T(8,128)(2,1)}), bf16[8,16,1024]{2,1,0:T(8,128)(2,1)S(1)}, u32[]{:S(2)}, u32[]{:S(2)}) async-start(bf16[8,16,1024]{2,1,0:T(8,128)(2,1)} %bitcast.7), calls=%async_computation.2 | async-start | bytes 524288 | tf_op jit(solution)/shard_map/all_to_all | solution.py:453
  95.8 4.4 %copy-start.2 = (bf16[8,16,1024]{2,1,0:T(8,128)(2,1)}, bf16[8,16,1024]{2,1,0:T(8,128)(2,1)S(1)}, u32[]{:S(2)}) copy-start(bf16[8,16,1024]{2,1,0:T(8,128)(2,1)S(1)} %all-to-all-done.2) | copy-start | bytes 786436
  96.7 17.8 %all-to-all-start.3 = ((bf16[8,16,1024]{2,1,0:T(8,128)(2,1)}), bf16[8,16,1024]{2,1,0:T(8,128)(2,1)S(1)}, u32[]{:S(2)}, u32[]{:S(2)}) async-start(bf16[8,16,1024]{2,1,0:T(8,128)(2,1)} %bitcast.10), calls=%async_computation.3 | async-start | bytes 524288 | tf_op jit(solution)/shard_map/all_to_all | solution.py:453
  111.8 2.6 %collective-permute-start = (bf16[1024,128]{1,0:T(8,128)(2,1)}, bf16[1024,128]{1,0:T(8,128)(2,1)S(1)}, u32[]{:S(2)}, u32[]{:S(2)}) collective-permute-start(bf16[1024,128]{1,0:T(8,128)(2,1)} %get-tuple-element.40.own_ref), channel_id=1, source_target_pairs={{0,1},{2,3},{4,5},{6,7},{8,9},{10,11},{12,13},{14,15},{16,17},{18,... | collective-permute-start | bytes 786440 | tf_op jit(solution)/shard_map/ppermute | solution.py:633
  114.4 0.7 copy-start.5
  114.4 0.8 copy-start.3
  117.8 19.7 %all-to-all-start.4 = ((bf16[8,16,1152]{2,1,0:T(8,128)(2,1)}), bf16[8,16,1152]{2,1,0:T(8,128)(2,1)S(1)}, u32[]{:S(2)}, u32[]{:S(2)}) async-start(bf16[8,16,1152]{2,1,0:T(8,128)(2,1)} %bitcast.41), calls=%async_computation.4 | async-start | bytes 589824 | tf_op jit(solution)/shard_map/all_to_all | solution.py:453
  123.8 3.8 %collective-permute-start.1 = (bf16[1024,128]{1,0:T(8,128)(2,1)}, bf16[1024,128]{1,0:T(8,128)(2,1)S(1)}, u32[]{:S(2)}, u32[]{:S(2)}) collective-permute-start(bf16[1024,128]{1,0:T(8,128)(2,1)} %get-tuple-element.46), channel_id=1, source_target_pairs={{1,0},{3,2},{5,4},{7,6},{9,8},{11,10},{13,12},{15,14},{17,16},{19,... | collective-permute-start | bytes 786440 | tf_op jit(solution)/shard_map/ppermute | solution.py:654
  127.6 0.7 copy-start
  137.6 0.5 copy-start.7
  143.9 15.7 %all-to-all-start.5 = ((bf16[8,16,1024]{2,1,0:T(8,128)(2,1)}), bf16[8,16,1024]{2,1,0:T(8,128)(2,1)S(1)}, u32[]{:S(2)}, u32[]{:S(2)}) async-start(bf16[8,16,1024]{2,1,0:T(8,128)(2,1)} %bitcast.15), calls=%async_computation.5 | async-start | bytes 524288 | tf_op jit(solution)/shard_map/all_to_all | solution.py:453
  159.6 6.8 %copy-start.1 = (bf16[8,16,1024]{2,1,0:T(8,128)(2,1)}, bf16[8,16,1024]{2,1,0:T(8,128)(2,1)S(1)}, u32[]{:S(2)}) copy-start(bf16[8,16,1024]{2,1,0:T(8,128)(2,1)S(1)} %all-to-all-done.5) | copy-start | bytes 786436
  160.4 17.7 %all-to-all-start.6 = ((bf16[8,16,1024]{2,1,0:T(8,128)(2,1)}), bf16[8,16,1024]{2,1,0:T(8,128)(2,1)S(1)}, u32[]{:S(2)}, u32[]{:S(2)}) async-start(bf16[8,16,1024]{2,1,0:T(8,128)(2,1)} %tile.40), calls=%async_computation.6 | async-start | bytes 524288 | tf_op jit(solution)/shard_map/all_to_all | solution.py:453
  178.1 0.7 copy-start.6

commit v6 on v5

--- a/solution.py
+++ b/solution.py
@@ -186,7 +186,7 @@
     inv_ref[...] = jnp.broadcast_to(1.0 / scale, inv_ref.shape)
     factor_ref[...] = jnp.broadcast_to(sine_scale(scale), inv_ref.shape)
 
-    @pl.loop(0, rows // lines, unroll=2)
+    @pl.loop(0, rows // lines, unroll=4)
     def _(i):
         here = pl.ds(pl.multiple_of(i * lines, lines), lines)
         inverse, factor = inv_ref[here, :], factor_ref[here, :]

time: 202 us -> 201 us (level)
  transfers between devices with their start and end apart: 9 -> 9, of which waited for: 3 -> 3; matrix products, arithmetic and copies ran while one was open for 2% -> 2% of each run, Pallas kernels for 46% -> 45%
where the time goes in v6:
time: 201 us; the launch traced here: 200 us
  Pallas kernels  117 us (58%)
  starting transfers between devices  43.2 us (21%)
  blocking collectives  14.3 us (7%)
  waiting for transfers between devices  12.6 us (6%)
  local copies, waits for them, and re-layouts  9.5 us (5%)
  other arithmetic  2.65 us (1%)
    pallas_call x2, Pallas kernels, prepare(): call(functools.partial(prep_kernel, kv_count, starts, ends, number), tupl...  48.8 us
    all_to_all x7, starting transfers between devices, exchange(): lax.all_to_all(rows, 'tensor', split_axis=0, concat_axis=0, tiled=True)  40.6 us
    all_to_all x1, blocking collectives, exchange(): lax.all_to_all(rows, 'tensor', split_axis=0, concat_axis=0, tiled=True)  14.3 us
    pallas_call x1, Pallas kernels, on_device(): call(functools.partial(out_grad_kernel, kv_count, half), shaped((LANES, L...  11.7 us
    pallas_call x1, Pallas kernels, on_device(): call(functools.partial(forward_kernel, kv_count), (shaped((tokens, width)...  11.5 us
    pallas_call x1, Pallas kernels, on_device(): call(early_grad_kernel, shaped((LANES, LANES), F32), (big, 2 * local * wi...  9.92 us
    pallas_call x1, Pallas kernels, on_device(): call(back_kernel, shaped((tokens, width), BF16), (big, 2 * local * width)...  9.17 us
    all_to_all x7, waiting for transfers between devices, exchange(): lax.all_to_all(rows, 'tensor', split_axis=0, concat_axis=0, tiled=True)  8.77 us
  transfers between devices with their start and end apart: 9, of which 3 were waited for; matrix products, arithmetic and copies ran while one was open for 2% of the time, Pallas kernels for 45%

profile of v6, /device:TPU:0, one launch (start us, length us, event | category | flops | bytes accessed | tf_op | source)
XLA Modules:
  0.0 200.3 jit_solution(11300294614174068489)
XLA Ops:
  0.6 4.5 %shard_map.86 = (bf16[1024,128]{1,0:T(8,128)(2,1)}, bf16[1024,128]{1,0:T(8,128)(2,1)}, f32[1024,128]{1,0:T(8,128)}, f32[1024,1024]{1,0:T(8,128)}, f32[8,1152]{1,0:T(8,128)}) custom-call(bf16[128,1024]{1,0:T(8,128)(2,1)} %hidden_ref.1, bf16[128,1024]{1,0:T(8,128)(2,1)} %ct_ref.1, f32[1,1024]{1,0:T(1,128)} %gain_row_ref.1, bf16[1024,1024]{1,0:T(8,128)(2,1)} %bitcast.35, ...), custom_call_target="tpu_custom_call" | custom-call | flops 536870912 | bytes 6291456 | tf_op jit(solution)/shard_map/pallas_call | solution.py:485
  5.1 1.4 copy.11
  6.6 7.3 %all-to-all-start = ((f32[8,1,1152]{2,1,0:T(1,128)}), f32[8,1,1152]{2,1,0:T(1,128)S(1)}, u32[]{:S(2)}, u32[]{:S(2)}) async-start(f32[8,1,1152]{2,1,0:T(1,128)} %copy.11), calls=%async_computation | async-start | bytes 73728 | tf_op jit(solution)/shard_map/all_to_all | solution.py:453
  13.8 14.2 %shard_map.88 = (bf16[1024,8192]{1,0:T(8,128)(2,1)}, bf16[1024,8192]{1,0:T(8,128)(2,1)}, bf16[128,8192]{1,0:T(8,128)(2,1)}) custom-call(bf16[1024,8192]{1,0:T(8,128)(2,1)} %bitcast.31, f32[128,128]{1,0:T(8,128)} %bitcast.48, bf16[1024,128]{1,0:T(8,128)(2,1)} %get-tuple-element.33.refs_2_.ct_ref), custom_call_target="tpu_custom_call" | custom-call | flops 21474836480 | bytes 12582912 | tf_op jit(solution)/shard_map/pallas_call | solution.py:553
  28.0 3.3 %reshape_squeeze.3.refs_3_.probs_ref = bf16[2,4096,64]{2,1,0:T(8,128)(2,1)} reshape(bf16[1,2,64,4096]{3,2,1,0:T(8,128)(2,1)S(1)} %copy-done.4) | data formatting | bytes 2097152 | tf_op jit(solution)/shard_map/reshape;squeeze | solution.py:470
  32.0 7.5 %shard_map.87 = (bf16[1024,1024]{1,0:T(8,128)(2,1)}, bf16[1024,1024]{1,0:T(8,128)(2,1)}, bf16[128,1024]{1,0:T(8,128)(2,1)}, f32[1,128]{1,0:T(1,128)}) custom-call(f32[1024,1024]{1,0:T(8,128)} %get-tuple-element.29.turned_ref, f32[8,1152]{1,0:T(8,128)} %bitcast.46, bf16[1024,128]{1,0:T(8,128)(2,1)} %get-tuple-element.28.x_ref.x0_ref, ...), custom_call_target="tpu_custom_call" | custom-call | flops 268435456 | bytes 8388608 | tf_op jit(solution)/shard_map/pallas_call | solution.py:567
  39.5 6.0 %all-to-all-start.1 = ((bf16[8,16,1024]{2,1,0:T(8,128)(2,1)}), bf16[8,16,1024]{2,1,0:T(8,128)(2,1)S(1)}, u32[]{:S(2)}, u32[]{:S(2)}) async-start(bf16[8,16,1024]{2,1,0:T(8,128)(2,1)} %bitcast.44), calls=%async_computation.1 | async-start | bytes 524288 | tf_op jit(solution)/shard_map/all_to_all | solution.py:453
  45.5 34.6 %shard_map.89 = (bf16[1024,8192]{1,0:T(8,128)(2,1)}, bf16[1024,8192]{1,0:T(8,128)(2,1)}, bf16[128,8192]{1,0:T(8,128)(2,1)}, bf16[128,1024]{1,0:T(8,128)(2,1)}) custom-call(bf16[1024,8192]{1,0:T(8,128)(2,1)} %bitcast.32, f32[128,128]{1,0:T(8,128)} %bitcast.49, ...), custom_call_target="tpu_custom_call", output_to_operand_aliasing={{0}: (6, {}), {1}: (7, {})} | custom-call | flops 64424509440 | bytes 37748736 | tf_op jit(solution)/shard_map/pallas_call | solution.py:553
  80.1 0.7 bitcast_select_fusion.1
  80.8 6.0 %all-to-all-start.2 = ((bf16[8,16,1024]{2,1,0:T(8,128)(2,1)}), bf16[8,16,1024]{2,1,0:T(8,128)(2,1)S(1)}, u32[]{:S(2)}, u32[]{:S(2)}) async-start(bf16[8,16,1024]{2,1,0:T(8,128)(2,1)} %bitcast.7), calls=%async_computation.2 | async-start | bytes 524288 | tf_op jit(solution)/shard_map/all_to_all | solution.py:453
  86.8 8.8 %all-to-all-done.2 = bf16[8,16,1024]{2,1,0:T(8,128)(2,1)S(1)} async-done(((bf16[8,16,1024]{2,1,0:T(8,128)(2,1)}), bf16[8,16,1024]{2,1,0:T(8,128)(2,1)S(1)}, u32[]{:S(2)}, u32[]{:S(2)}) %all-to-all-start.2) | async-done | bytes 262176 | tf_op jit(solution)/shard_map/all_to_all | solution.py:453
  95.6 0.8 tile.16
  96.4 3.6 %all-to-all-start.3 = ((bf16[8,16,1024]{2,1,0:T(8,128)(2,1)}), bf16[8,16,1024]{2,1,0:T(8,128)(2,1)S(1)}, u32[]{:S(2)}, u32[]{:S(2)}) async-start(bf16[8,16,1024]{2,1,0:T(8,128)(2,1)} %bitcast.10), calls=%async_computation.3 | async-start | bytes 524288 | tf_op jit(solution)/shard_map/all_to_all | solution.py:453
  100.0 11.5 %shard_map.90 = (bf16[128,8192]{1,0:T(8,128)(2,1)}, bf16[1024,128]{1,0:T(8,128)(2,1)}) custom-call(s32[1]{0:T(128)S(6)} %sub.3.active_ref, bf16[128,1024]{1,0:T(8,128)(2,1)} %bitcast.38, bf16[2,4096,64]{2,1,0:T(8,128)(2,1)} %reshape_squeeze.3.refs_3_.probs_ref, bf16[1024,8192]{1,0:T(8,128)(2,1)} %get-tuple-element.39.q_ref, ...), custom_call_target="tpu_custom_call" | custom-call | flops 2147483648 | bytes 16777216 | tf_op jit(solution)/shard_map/pallas_call | solution.py:619
  111.5 1.3 collective-permute-start
  112.8 1.3 collective-permute-done.arrived_ref.x1_ref
  114.9 2.6 %shard_map.91 = (bf16[128,1152]{1,0:T(8,128)(2,1)}, bf16[1024,128]{1,0:T(8,128)(2,1)}) custom-call(s32[1]{0:T(128)} %bitcast.active_ref.section_ref, bf16[1024,128]{1,0:T(8,128)(2,1)} %get-tuple-element.40.own_ref, bf16[1024,128]{1,0:T(8,128)(2,1)} %copy-done.5, bf16[128,1024]{1,0:T(8,128)(2,1)} %bitcast.39, f32[1024,128]{1,0:T(8,128)} %get-tuple-element.31.gain_ref, ...), custom_call_target="tpu_custom_call" | custom-call | flops 536870912 | bytes 2097152 | tf_op jit(solution)/shard_map/pallas_call | solution.py:635
  117.5 6.0 %all-to-all-start.4 = ((bf16[8,16,1152]{2,1,0:T(8,128)(2,1)}), bf16[8,16,1152]{2,1,0:T(8,128)(2,1)S(1)}, u32[]{:S(2)}, u32[]{:S(2)}) async-start(bf16[8,16,1152]{2,1,0:T(8,128)(2,1)} %bitcast.41), calls=%async_computation.4 | async-start | bytes 589824 | tf_op jit(solution)/shard_map/all_to_all | solution.py:453
  123.5 1.3 collective-permute-start.1
  124.8 2.5 %collective-permute-done.1.grad_ref = bf16[1024,128]{1,0:T(8,128)(2,1)S(1)} collective-permute-done((bf16[1024,128]{1,0:T(8,128)(2,1)}, bf16[1024,128]{1,0:T(8,128)(2,1)S(1)}, u32[]{:S(2)}, u32[]{:S(2)}) %collective-permute-start.1) | collective-permute-done | bytes 262176 | tf_op jit(solution)/shard_map/ppermute | solution.py:654
  128.1 9.2 %shard_map.92.back_ref = bf16[128,8192]{1,0:T(8,128)(2,1)} custom-call(s32[1]{0:T(128)S(6)} %sub.3.active_ref, bf16[1024,8192]{1,0:T(8,128)(2,1)} %get-tuple-element.39.q_ref, bf16[1024,128]{1,0:T(8,128)(2,1)} %copy-done, bf16[128,1152]{1,0:T(8,128)(2,1)} %get-tuple-element.44.after_ref), custom_call_target="tpu_custom_call" | custom-call | flops 2147483648 | bytes 16777216 | tf_op jit(solution)/shard_map/pallas_call | solution.py:655
  137.8 4.1 %shard_map.93 = bf16[128,1024]{1,0:T(8,128)(2,1)} custom-call(s32[1]{0:T(128)S(6)} %sub.3.active_ref, f32[1,128]{1,0:T(1,128)} %copy-done.7, bf16[128,8192]{1,0:T(8,128)(2,1)} %get-tuple-element.45.ct_back_ref, bf16[128,8192]{1,0:T(8,128)(2,1)} %shard_map.92.back_ref, bf16[2,4096,64]{2,1,0:T(8,128)(2,1)} %reshape_squeeze.3.refs_3_.probs_ref), custom_call_target="tpu_custom_call" | custom-call | flops 134217728 | bytes 6291456 | tf_op jit(solution)/shard_map/pallas_call | solution.py:666
  141.9 1.7 bitcast_select_fusion.after_ref
  143.6 5.8 %all-to-all-start.5 = ((bf16[8,16,1024]{2,1,0:T(8,128)(2,1)}), bf16[8,16,1024]{2,1,0:T(8,128)(2,1)S(1)}, u32[]{:S(2)}, u32[]{:S(2)}) async-start(bf16[8,16,1024]{2,1,0:T(8,128)(2,1)} %bitcast.15), calls=%async_computation.5 | async-start | bytes 524288 | tf_op jit(solution)/shard_map/all_to_all | solution.py:453
  149.4 9.9 %shard_map.94.other_ref = f32[128,128]{1,0:T(8,128)} custom-call(s32[1]{0:T(128)} %bitcast.active_ref.section_ref, f32[1,128]{1,0:T(1,128)} %copy-done.7, bf16[128,8192]{1,0:T(8,128)(2,1)} %get-tuple-element.47.mixed_ref.mixed_in_ref, bf16[1024,128]{1,0:T(8,128)(2,1)} %get-tuple-element.33.refs_2_.ct_ref, bf16[1024,128]{1,0:T(8,128)(2,1)} %copy-done, ...), custom_call_target="tpu_custom_call" | custom-call | flops 2147483648 | bytes 16777216 | tf_op jit(solution)/shard_map/pallas_call | solution.py:693
  159.4 0.8 tile.40
  160.1 6.0 %all-to-all-start.6 = ((bf16[8,16,1024]{2,1,0:T(8,128)(2,1)}), bf16[8,16,1024]{2,1,0:T(8,128)(2,1)S(1)}, u32[]{:S(2)}, u32[]{:S(2)}) async-start(bf16[8,16,1024]{2,1,0:T(8,128)(2,1)} %tile.40), calls=%async_computation.6 | async-start | bytes 524288 | tf_op jit(solution)/shard_map/all_to_all | solution.py:453
  166.1 11.7 %shard_map.95.other_ref = f32[128,128]{1,0:T(8,128)} custom-call(s32[1]{0:T(128)} %bitcast.active_ref.section_ref, bf16[128,1024]{1,0:T(8,128)(2,1)} %bitcast.37, f32[1,128]{1,0:T(1,128)} %copy-done.7, bf16[2,4096,64]{2,1,0:T(8,128)(2,1)} %reshape_squeeze.3.refs_3_.probs_ref, bf16[128,8192]{1,0:T(8,128)(2,1)} %get-tuple-element.47.mixed_ref.mixed_in_ref, ...), custom_call_target="tpu_custom_call" | custom-call | flops 4294967296 | bytes 33554432 | tf_op jit(solution)/shard_map/pallas_call | solution.py:719
  177.8 0.7 copy-done.6
  178.5 4.9 %shard_map.96 = bf16[1024,128]{1,0:T(8,128)(2,1)} custom-call(s32[1]{0:T(128)} %bitcast.active_ref.section_ref, bf16[1024,128]{1,0:T(8,128)(2,1)} %get-tuple-element.28.x_ref.x0_ref, bf16[1024,128]{1,0:T(8,128)(2,1)} %copy-done.5, f32[1,128]{1,0:T(1,128)} %get-tuple-element.41.mean0_ref, f32[1,128]{1,0:T(1,128)} %copy-done.7, ...), custom_call_target="tpu_custom_call" | custom-call | flops 536870912 | bytes 4194304 | tf_op jit(solution)/shard_map/pallas_call | solution.py:740
  183.4 14.3 %all_to_all.83 = bf16[8,128,128]{2,1,0:T(8,128)(2,1)} all-to-all(bf16[8,128,128]{2,1,0:T(8,128)(2,1)} %bitcast.43), channel_id=1, replica_groups=mesh['groups'=2,'tensor'=8,'section'=2] {'tensor'}, dimensions={0} | all-to-all | bytes 524288 | tf_op jit(solution)/shard_map/all_to_all | solution.py:453
  197.7 2.6 %shard_map.97 = (f32[128,128]{1,0:T(8,128)}, f32[128,128]{1,0:T(8,128)}) custom-call(bf16[1024,128]{1,0:T(8,128)(2,1)} %bitcast.45, f32[128,128]{1,0:T(8,128)} %bitcast.50), custom_call_target="tpu_custom_call" | custom-call | flops 125829120 | bytes 131072 | tf_op jit(solution)/shard_map/pallas_call | solution.py:761
  (29 shorter events, 2.8 us)
Async XLA Ops:
  6.6 24.8 %all-to-all-start = ((f32[8,1,1152]{2,1,0:T(1,128)}), f32[8,1,1152]{2,1,0:T(1,128)S(1)}, u32[]{:S(2)}, u32[]{:S(2)}) async-start(f32[8,1,1152]{2,1,0:T(1,128)} %copy.11), calls=%async_computation | async-start | bytes 73728 | tf_op jit(solution)/shard_map/all_to_all | solution.py:453
  13.8 14.2 %copy-start.4 = (bf16[1,2,64,4096]{3,2,1,0:T(8,128)(2,1)S(1)}, bf16[1,2,64,4096]{3,2,1,0:T(8,128)(2,1)}, u32[]{:S(2)}) copy-start(bf16[1,2,64,4096]{3,2,1,0:T(8,128)(2,1)} %param.13) | copy-start | bytes 3145732
  39.5 40.6 %all-to-all-start.1 = ((bf16[8,16,1024]{2,1,0:T(8,128)(2,1)}), bf16[8,16,1024]{2,1,0:T(8,128)(2,1)S(1)}, u32[]{:S(2)}, u32[]{:S(2)}) async-start(bf16[8,16,1024]{2,1,0:T(8,128)(2,1)} %bitcast.44), calls=%async_computation.1 | async-start | bytes 524288 | tf_op jit(solution)/shard_map/all_to_all | solution.py:453
  80.8 14.8 %all-to-all-start.2 = ((bf16[8,16,1024]{2,1,0:T(8,128)(2,1)}), bf16[8,16,1024]{2,1,0:T(8,128)(2,1)S(1)}, u32[]{:S(2)}, u32[]{:S(2)}) async-start(bf16[8,16,1024]{2,1,0:T(8,128)(2,1)} %bitcast.7), calls=%async_computation.2 | async-start | bytes 524288 | tf_op jit(solution)/shard_map/all_to_all | solution.py:453
  95.6 4.4 %copy-start.2 = (bf16[8,16,1024]{2,1,0:T(8,128)(2,1)}, bf16[8,16,1024]{2,1,0:T(8,128)(2,1)S(1)}, u32[]{:S(2)}) copy-start(bf16[8,16,1024]{2,1,0:T(8,128)(2,1)S(1)} %all-to-all-done.2) | copy-start | bytes 786436
  96.4 17.7 %all-to-all-start.3 = ((bf16[8,16,1024]{2,1,0:T(8,128)(2,1)}), bf16[8,16,1024]{2,1,0:T(8,128)(2,1)S(1)}, u32[]{:S(2)}, u32[]{:S(2)}) async-start(bf16[8,16,1024]{2,1,0:T(8,128)(2,1)} %bitcast.10), calls=%async_computation.3 | async-start | bytes 524288 | tf_op jit(solution)/shard_map/all_to_all | solution.py:453
  111.5 2.6 %collective-permute-start = (bf16[1024,128]{1,0:T(8,128)(2,1)}, bf16[1024,128]{1,0:T(8,128)(2,1)S(1)}, u32[]{:S(2)}, u32[]{:S(2)}) collective-permute-start(bf16[1024,128]{1,0:T(8,128)(2,1)} %get-tuple-element.40.own_ref), channel_id=1, source_target_pairs={{0,1},{2,3},{4,5},{6,7},{8,9},{10,11},{12,13},{14,15},{16,17},{18,... | collective-permute-start | bytes 786440 | tf_op jit(solution)/shard_map/ppermute | solution.py:633
  114.1 0.7 copy-start.5
  114.1 0.8 copy-start.3
  117.5 19.7 %all-to-all-start.4 = ((bf16[8,16,1152]{2,1,0:T(8,128)(2,1)}), bf16[8,16,1152]{2,1,0:T(8,128)(2,1)S(1)}, u32[]{:S(2)}, u32[]{:S(2)}) async-start(bf16[8,16,1152]{2,1,0:T(8,128)(2,1)} %bitcast.41), calls=%async_computation.4 | async-start | bytes 589824 | tf_op jit(solution)/shard_map/all_to_all | solution.py:453
  123.5 3.8 %collective-permute-start.1 = (bf16[1024,128]{1,0:T(8,128)(2,1)}, bf16[1024,128]{1,0:T(8,128)(2,1)S(1)}, u32[]{:S(2)}, u32[]{:S(2)}) collective-permute-start(bf16[1024,128]{1,0:T(8,128)(2,1)} %get-tuple-element.46), channel_id=1, source_target_pairs={{1,0},{3,2},{5,4},{7,6},{9,8},{11,10},{13,12},{15,14},{17,16},{19,... | collective-permute-start | bytes 786440 | tf_op jit(solution)/shard_map/ppermute | solution.py:654
  127.4 0.7 copy-start
  137.3 0.5 copy-start.7
  143.6 15.7 %all-to-all-start.5 = ((bf16[8,16,1024]{2,1,0:T(8,128)(2,1)}), bf16[8,16,1024]{2,1,0:T(8,128)(2,1)S(1)}, u32[]{:S(2)}, u32[]{:S(2)}) async-start(bf16[8,16,1024]{2,1,0:T(8,128)(2,1)} %bitcast.15), calls=%async_computation.5 | async-start | bytes 524288 | tf_op jit(solution)/shard_map/all_to_all | solution.py:453
  159.3 6.8 %copy-start.1 = (bf16[8,16,1024]{2,1,0:T(8,128)(2,1)}, bf16[8,16,1024]{2,1,0:T(8,128)(2,1)S(1)}, u32[]{:S(2)}) copy-start(bf16[8,16,1024]{2,1,0:T(8,128)(2,1)S(1)} %all-to-all-done.5) | copy-start | bytes 786436
  160.1 17.7 %all-to-all-start.6 = ((bf16[8,16,1024]{2,1,0:T(8,128)(2,1)}), bf16[8,16,1024]{2,1,0:T(8,128)(2,1)S(1)}, u32[]{:S(2)}, u32[]{:S(2)}) async-start(bf16[8,16,1024]{2,1,0:T(8,128)(2,1)} %tile.40), calls=%async_computation.6 | async-start | bytes 524288 | tf_op jit(solution)/shard_map/all_to_all | solution.py:453
  177.8 0.7 copy-start.6
